TPU v7x, 32 devices: a whole 2x2x4 slice. The times are simulated.
32 devices in a mesh: dp: 8 (over z, core), tensor: 4 (over y, x).
Axes of the slice: x: 2, y: 2, z: 4, core: 2. Of those that a mesh axis runs over, the one named last changes fastest.
Arguments:
- tokens: bfloat16 [8, 1024, 2048], P('dp', 'tensor'), may hold values from -6 to 6
- cotangent: bfloat16 [8, 1024, 2048], P('dp', 'tensor'), may hold values from -6 to 6
- w_query: bfloat16 [2048, 2048], P(None, 'tensor'), may hold values from -0.1875 to 0.1875
- w_key: bfloat16 [2048, 1024], P(None, 'tensor'), may hold values from -0.1875 to 0.1875
- w_value: bfloat16 [2048, 1024], P(None, 'tensor'), may hold values from -0.125 to 0.125
- w_output: bfloat16 [2048, 2048], P('tensor'), may hold values from -0.375 to 0.375
- w_gate: bfloat16 [2048, 5632], P(None, 'tensor'), may hold values from -0.125 to 0.125
- w_up: bfloat16 [2048, 5632], P(None, 'tensor'), may hold values from -0.125 to 0.125
- w_down: bfloat16 [5632, 2048], P('tensor'), may hold values from -0.078125 to 0.078125
- gain_attn: float32 [2048], replicated, may hold values from 0.5 to 1.5
- gain_mlp: float32 [2048], replicated, may hold values from 0.5 to 1.5
- dropped: int32 [8], P('dp'), may hold values 0 or 1
- exit_scale: float32 [8], P('dp'), may hold values from 0.5 to 2
- positions: int32 [8, 1024], P('dp'), may hold values from 0 to 1023, as said below
Outputs:
- mixed: bfloat16 [8, 1024, 2048], P('dp', 'tensor')
- input_grad: float32 [8, 1024, 2048], P('dp', 'tensor')
- grad_query: float32 [2048, 2048], P(None, 'tensor')
- grad_key: float32 [2048, 1024], P(None, 'tensor')
- grad_value: float32 [2048, 1024], P(None, 'tensor')
- grad_output: float32 [2048, 2048], P('tensor')
- grad_gate: float32 [2048, 5632], P(None, 'tensor')
- grad_up: float32 [2048, 5632], P(None, 'tensor')
- grad_down: float32 [5632, 2048], P('tensor')
- grad_gain_attn: float32 [2048], replicated
- grad_gain_mlp: float32 [2048], replicated
Inputs may be any that keep to these rules, and one draw needn't show every extreme that they name: Each sequence is cut into up to four documents, and positions count from 0 at each document's start; one sequence, drawn from the seed, is a single document.
All inputs are finite; a program needn't handle non-finite values. No bound on the sum of `dropped` on one device may be relied on, other than what follows from the above.
Results may differ from a plain program's by a relative error of at most 0.015.
Values may be sent and summed in bfloat16 or wider, within the bound.
No kernel may reach another device: no remote copies, remote signals or barrier semaphores. Data moves between devices by JAX's collectives and lax.ppermute only.
A program may use at most 320 MiB of HBM per device.

v0:
```python
import math

import jax
import jax.numpy as jnp
from jax import lax
from jax.sharding import PartitionSpec as P

HD = 128


def rms_scale(hidden_in, gain_vec):
    return (
        hidden_in
        * lax.rsqrt(jnp.mean(hidden_in * hidden_in, axis=-1, keepdims=True) + 1e-05)
        * gain_vec
    )


def gain_part(hidden_in, grad_rows):
    normed = hidden_in * lax.rsqrt(jnp.mean(hidden_in * hidden_in, axis=-1, keepdims=True) + 1e-05)
    return jnp.sum(grad_rows * normed, axis=0)


def angle_tables(pos_ids, head_width):
    freqs = jnp.exp(
        jnp.arange(head_width // 2, dtype=jnp.float32) * (-2.0 * math.log(10000.0) / head_width)
    )
    turned = pos_ids.astype(jnp.float32)[:, None] * freqs[None, :]
    return (jnp.cos(turned), jnp.sin(turned))


def rotate(vectors, cos_table, sin_table):
    half_width = vectors.shape[-1] // 2
    first = vectors[..., :half_width]
    second = vectors[..., half_width:]
    cos_part = cos_table[:, None, :]
    sin_part = sin_table[:, None, :]
    return jnp.concatenate(
        [first * cos_part - second * sin_part, second * cos_part + first * sin_part], axis=-1
    )


def unrotate(grads_in, cos_table, sin_table):
    half_width = grads_in.shape[-1] // 2
    first = grads_in[..., :half_width]
    second = grads_in[..., half_width:]
    cos_part = cos_table[:, None, :]
    sin_part = sin_table[:, None, :]
    return jnp.concatenate(
        [first * cos_part + second * sin_part, second * cos_part - first * sin_part], axis=-1
    )


def local(
    tokens,
    cotangent,
    w_query,
    w_key,
    w_value,
    w_output,
    w_gate,
    w_up,
    w_down,
    gain_attn,
    gain_mlp,
    dropped,
    exit_scale,
    positions,
):
    fp32 = jnp.float32
    bf16 = jnp.bfloat16
    whole_x, whole_ct = (
        lax.all_gather(tokens, "tensor", axis=1, tiled=True),
        lax.all_gather(cotangent, "tensor", axis=1, tiled=True),
    )
    x_bf = whole_x[0]
    seq_len = x_bf.shape[0]
    cot_full = whole_ct[0].astype(fp32) * exit_scale[0]
    survive = 1.0 - dropped[0].astype(fp32)
    cos_table, sin_table = angle_tables(positions[0], HD)
    local_heads = w_query.shape[1] // HD
    local_kv = w_key.shape[1] // HD
    share = local_heads // local_kv
    factor = 1.0 / math.sqrt(HD)
    x_rows = tokens[0].astype(fp32)
    x_full = x_bf.astype(fp32)
    n_one = rms_scale(x_full, gain_attn).astype(bf16)
    query_heads = (
        rotate(
            jnp.dot(n_one, w_query, preferred_element_type=fp32).reshape(seq_len, local_heads, HD),
            cos_table,
            sin_table,
        )
        .astype(bf16)
        .reshape(seq_len, local_kv, share, HD)
    )
    key_heads = rotate(
        jnp.dot(n_one, w_key, preferred_element_type=fp32).reshape(seq_len, local_kv, HD),
        cos_table,
        sin_table,
    ).astype(bf16)
    value_heads = (
        jnp.dot(n_one, w_value, preferred_element_type=fp32)
        .astype(bf16)
        .reshape(seq_len, local_kv, HD)
    )
    block_rows = min(512, seq_len)
    block_count = seq_len // block_rows

    def block_scores(query_block, first_row):
        raw_scores = (
            jnp.einsum("qkgd,skd->kgqs", query_block, key_heads, preferred_element_type=fp32)
            * factor
        )
        row_ids = first_row + lax.broadcasted_iota(jnp.int32, (block_rows, seq_len), 0)
        col_ids = lax.broadcasted_iota(jnp.int32, (block_rows, seq_len), 1)
        return jnp.where(col_ids <= row_ids, raw_scores, -1e30)

    attended = []
    log_sums = []
    for block_index in range(block_count):
        first_row = block_index * block_rows
        masked = block_scores(query_heads[first_row : first_row + block_rows], first_row)
        row_max = jnp.max(masked, axis=-1, keepdims=True)
        powers = jnp.exp(masked - row_max)
        row_total = jnp.sum(powers, axis=-1, keepdims=True)
        prob_bf = (powers / row_total).astype(bf16)
        attended.append(
            jnp.einsum("kgqs,skd->qkgd", prob_bf, value_heads, preferred_element_type=fp32)
        )
        log_sums.append(row_max + jnp.log(row_total))
    attn_bf = jnp.concatenate(attended, axis=0).reshape(seq_len, local_heads * HD).astype(bf16)
    attn_part = lax.psum_scatter(
        jnp.dot(attn_bf, w_output, preferred_element_type=fp32),
        "tensor",
        scatter_dimension=0,
        tiled=True,
    )
    h_one_rows = x_rows + survive * attn_part
    n_two = lax.all_gather(
        rms_scale(h_one_rows, gain_mlp).astype(bf16), "tensor", axis=0, tiled=True
    )
    gate_proj = jnp.dot(n_two, w_gate, preferred_element_type=fp32)
    up_proj = jnp.dot(n_two, w_up, preferred_element_type=fp32)
    sig_gate = jax.nn.sigmoid(gate_proj)
    silu_gate = gate_proj * sig_gate
    hidden = (silu_gate * up_proj).astype(bf16)
    mlp_rows = lax.psum_scatter(
        jnp.dot(hidden, w_down, preferred_element_type=fp32).astype(jnp.bfloat16),
        "tensor",
        scatter_dimension=0,
        tiled=True,
    ).astype(jnp.float32)
    mixed = (h_one_rows + survive * mlp_rows).astype(bf16)[None]
    grad_m = (survive * cot_full).astype(bf16)
    grad_hidden = jnp.einsum("sd,fd->sf", grad_m, w_down, preferred_element_type=fp32)
    grad_wd = jnp.einsum("sf,sd->fd", hidden, grad_m, preferred_element_type=fp32)
    grad_gate_bf = (grad_hidden * up_proj * sig_gate * (1.0 + gate_proj * (1.0 - sig_gate))).astype(
        bf16
    )
    grad_up_bf = (grad_hidden * silu_gate).astype(bf16)
    grad_wg = jnp.einsum("sd,sf->df", n_two, grad_gate_bf, preferred_element_type=fp32)
    grad_wu = jnp.einsum("sd,sf->df", n_two, grad_up_bf, preferred_element_type=fp32)
    mlp_sums = (grad_wg, grad_wu, grad_wd)
    total_part = jnp.einsum("sf,df->sd", grad_gate_bf, w_gate, preferred_element_type=fp32)
    grad_n_two_rows = lax.psum_scatter(
        total_part + jnp.einsum("sf,df->sd", grad_up_bf, w_up, preferred_element_type=fp32),
        "tensor",
        scatter_dimension=0,
        tiled=True,
    )
    norm_two_out, pull_two = jax.vjp(lambda hidden_in: rms_scale(hidden_in, gain_mlp), h_one_rows)
    cot_rows = cotangent[0].astype(fp32) * exit_scale[0]
    grad_h_rows = cot_rows + pull_two(grad_n_two_rows)[0]
    gain_two_part = gain_part(h_one_rows, grad_n_two_rows)
    grad_a = lax.all_gather((survive * grad_h_rows).astype(bf16), "tensor", axis=0, tiled=True)
    grad_wo = jnp.einsum("sf,sd->fd", attn_bf, grad_a, preferred_element_type=fp32)
    grad_attn = (
        jnp.einsum("sd,fd->sf", grad_a, w_output, preferred_element_type=fp32)
        .astype(bf16)
        .reshape(seq_len, local_kv, share, HD)
    )
    query_grads = []
    key_grad = jnp.zeros((seq_len, local_kv, HD), fp32)
    value_grad = jnp.zeros((seq_len, local_kv, HD), fp32)
    for block_index in range(block_count):
        first_row = block_index * block_rows
        query_block = query_heads[first_row : first_row + block_rows]
        masked = block_scores(query_block, first_row)
        prob_f32 = jnp.exp(masked - log_sums[block_index])
        prob_bf = prob_f32.astype(bf16)
        grad_block = grad_attn[first_row : first_row + block_rows]
        grad_prob = jnp.einsum(
            "qkgd,skd->kgqs", grad_block, value_heads, preferred_element_type=fp32
        )
        row_delta = jnp.sum(prob_f32 * grad_prob, axis=-1, keepdims=True)
        grad_score = (prob_f32 * (grad_prob - row_delta)).astype(bf16)
        query_grads.append(
            jnp.einsum("kgqs,skd->qkgd", grad_score, key_heads, preferred_element_type=fp32)
            * factor
        )
        key_grad = (
            key_grad
            + jnp.einsum("kgqs,qkgd->skd", grad_score, query_block, preferred_element_type=fp32)
            * factor
        )
        value_grad = value_grad + jnp.einsum(
            "kgqs,qkgd->skd", prob_bf, grad_block, preferred_element_type=fp32
        )
    query_grad = jnp.concatenate(query_grads, axis=0).reshape(seq_len, local_heads, HD)
    grad_q_bf = (
        unrotate(query_grad, cos_table, sin_table).reshape(seq_len, local_heads * HD).astype(bf16)
    )
    grad_k_bf = (
        unrotate(key_grad, cos_table, sin_table).reshape(seq_len, local_kv * HD).astype(bf16)
    )
    grad_v_bf = value_grad.reshape(seq_len, local_kv * HD).astype(bf16)
    grad_wq = jnp.einsum("sd,sf->df", n_one, grad_q_bf, preferred_element_type=fp32)
    grad_wk = jnp.einsum("sd,sf->df", n_one, grad_k_bf, preferred_element_type=fp32)
    grad_wv = jnp.einsum("sd,sf->df", n_one, grad_v_bf, preferred_element_type=fp32)
    total_part = jnp.einsum("sf,df->sd", grad_q_bf, w_query, preferred_element_type=fp32)
    total_part = total_part + jnp.einsum("sf,df->sd", grad_k_bf, w_key, preferred_element_type=fp32)
    grad_n_one = lax.psum_scatter(
        total_part + jnp.einsum("sf,df->sd", grad_v_bf, w_value, preferred_element_type=fp32),
        "tensor",
        scatter_dimension=0,
        tiled=True,
    )
    norm_one_out, pull_one = jax.vjp(lambda hidden_in: rms_scale(hidden_in, gain_attn), x_rows)
    input_grad = (grad_h_rows + pull_one(grad_n_one)[0])[None]
    gain_one_part = gain_part(x_rows, grad_n_one)
    gain_sums = lax.psum((gain_one_part, gain_two_part), ("dp", "tensor"))
    weight_sums = lax.psum(
        (grad_wq, grad_wk, grad_wv, grad_wo, mlp_sums[0], mlp_sums[1], mlp_sums[2]), "dp"
    )
    return (
        mixed,
        input_grad,
        weight_sums[0],
        weight_sums[1],
        weight_sums[2],
        weight_sums[3],
        weight_sums[4],
        weight_sums[5],
        weight_sums[6],
        gain_sums[0],
        gain_sums[1],
    )


def solution(mesh):
    placed = (
        P("dp", "tensor", None),
        P("dp", "tensor", None),
        P(None, "tensor"),
        P(None, "tensor"),
        P(None, "tensor"),
        P("tensor", None),
        P(None, "tensor"),
        P(None, "tensor"),
        P("tensor", None),
        P(),
        P(),
        P("dp"),
        P("dp"),
        P("dp", None),
    )
    return jax.shard_map(
        local,
        mesh=mesh,
        in_specs=placed,
        out_specs=(
            P("dp", "tensor", None),
            P("dp", "tensor", None),
            P(None, "tensor"),
            P(None, "tensor"),
            P(None, "tensor"),
            P("tensor", None),
            P(None, "tensor"),
            P(None, "tensor"),
            P("tensor", None),
            P(),
            P(),
        ),
        check_vma=False,
    )
```

profile of v0, /device:TPU:1, one launch (start us, length us, event | category | flops | bytes accessed | tf_op | source)
XLA Modules:
  0.0 1620.1 jit_solution(2634733938342639909)
XLA Ops:
  8.7 2.3 copy.65
  10.9 3.9 copy.68
  18.0 46.7 %all-gather.5.cloned.1.call-done = bf16[1,1024,2048]{2,1,0:T(8,128)(2,1)} async-done(((bf16[1,256,2048]{2,1,0:T(8,128)(2,1)}), bf16[1,1024,2048]{2,1,0:T(8,128)(2,1)}) %all-gather.5.cloned.1.call-update) | async-done | bytes 4194320 | tf_op jit(solution)/shard_map/all_gather | solution.py:73
  64.7 3.2 fusion.2
  68.2 2.8 fusion.27
  71.2 2.5 fusion.25
  80.3 1.8 fusion.75
  85.1 2.2 copy-done.3
  90.1 5.8 fusion.88
  96.7 85.7 %reduce-scatter.5.cloned.1.call-done = f32[256,2048]{1,0:T(8,128)} async-done(((f32[1024,2048]{1,0:T(8,128)}), f32[256,2048]{1,0:T(8,128)}) %reduce-scatter.5.cloned.1.call-update) | async-done | bytes 2097168 | tf_op jit(solution)/shard_map/reduce_scatter | solution.py:133
  182.4 2.7 multiply_reduce_fusion.2
  188.9 51.6 %all-gather.7.cloned.1.call-done = bf16[1024,2048]{1,0:T(8,128)(2,1)} async-done(((bf16[256,2048]{1,0:T(8,128)(2,1)}), bf16[1024,2048]{1,0:T(8,128)(2,1)}) %all-gather.7.cloned.1.call-update) | async-done | bytes 4194320 | tf_op jit(solution)/shard_map/all_gather | solution.py:140
  240.6 12.3 fusion.90
  252.8 10.2 fusion.89
  263.1 32.1 %all-gather.9.cloned.1.call-done = bf16[1,1024,2048]{2,1,0:T(8,128)(2,1)} async-done(((bf16[1,256,2048]{2,1,0:T(8,128)(2,1)}), bf16[1,1024,2048]{2,1,0:T(8,128)(2,1)}) %all-gather.9.cloned.1.call-update) | async-done | bytes 4194320 | tf_op jit(solution)/shard_map/all_gather | solution.py:74
  295.2 15.6 multiply_convert_fusion.1
  310.8 10.8 fusion.91
  321.6 10.9 convolution_add_fusion
  332.6 86.5 %reduce-scatter.9.cloned.1.call-done = f32[256,2048]{1,0:T(8,128)} async-done(((f32[1024,2048]{1,0:T(8,128)}), f32[256,2048]{1,0:T(8,128)}) %reduce-scatter.9.cloned.1.call-update) | async-done | bytes 2097168 | tf_op jit(solution)/shard_map/reduce_scatter | solution.py:166
  419.1 2.9 multiply_reduce_fusion
  424.5 52.8 %all-gather.11.cloned.1.call-done = bf16[1024,2048]{1,0:T(8,128)(2,1)} async-done(((bf16[256,2048]{1,0:T(8,128)(2,1)}), bf16[1024,2048]{1,0:T(8,128)(2,1)}) %all-gather.11.cloned.1.call-update) | async-done | bytes 4194320 | tf_op jit(solution)/shard_map/all_gather | solution.py:176
  477.3 4.5 convolution_convert_fusion.1
  482.0 5.4 fusion.7
  487.8 2.7 fusion.9
  490.5 2.5 convolution_bitcast_fusion
  496.3 1.9 fusion.10
  499.8 2.7 fusion.12
  506.8 2.4 fusion.92
  510.6 4.6 add_add_fusion
  515.3 10.9 convolution_convert_fusion
  526.3 12.4 fusion.41
  538.7 9.6 fusion.96
  548.3 9.8 fusion.95
  558.2 3.2 fusion.31
  561.4 3.2 fusion.33
  564.6 4.3 fusion.94
  568.9 4.9 fusion.29
  574.4 27.4 %reduce-scatter.11.cloned.1.call-done = f32[256,2048]{1,0:T(8,128)} async-done(((f32[1024,2048]{1,0:T(8,128)}), f32[256,2048]{1,0:T(8,128)}) %reduce-scatter.11.cloned.1.call-update) | async-done | bytes 2097168 | tf_op jit(solution)/shard_map/reduce_scatter | solution.py:223
  601.8 2.3 fusion.51
  604.1 39.7 %all-reduce = (f32[2048]{0:T(1024)}, f32[2048]{0:T(1024)}) all-reduce(f32[2048]{0:T(1024)S(1)} %get-tuple-element.13, f32[2048]{0:T(1024)S(1)} %get-tuple-element.11), channel_id=1, replica_groups=mesh['dp'=8,'tensor'=4] {'dp','tensor'}, use_global_device_ids=true, to_apply=%region_23.24 | all-reduce | flops 4096 | bytes 32768 | tf_op jit(solution)/shard_map/psum | solution.py:232
  643.8 14.8 reduce-scatter.7.cloned.1.call-done
  658.7 5.7 fusion.47
  664.3 908.8 %all-reduce.4.cloned.1.call-done = (f32[2048,512]{1,0:T(8,128)}, f32[2048,256]{1,0:T(8,128)}, f32[2048,256]{1,0:T(8,128)}, f32[512,2048]{1,0:T(8,128)}, f32[2048...) async-done(((f32[2048,512]{1,0:T(8,128)}, f32[2048,256]{1,0:T(8,128)}, f32[2048,256]{1,0:T(8,128)}, f32[512,2048]{1,0:T(8,128)}, f32[2048,1408]{1,0:T(8,128)}, ...) | async-done | bytes 47185936 | tf_op jit(solution)/shard_map/psum | solution.py:233
  1573.1 4.8 copy.84
  1581.7 2.0 copy.87
  1583.7 9.4 copy.88
  1593.1 9.4 copy.89
  1602.6 10.8 copy.90
  (174 shorter events, 38.4 us)
Async XLA Ops:
  7.2 82.9 %copy-start = (bf16[512,2048]{1,0:T(8,128)(2,1)S(1)}, bf16[512,2048]{1,0:T(8,128)(2,1)}, u32[]{:S(2)}) copy-start(bf16[512,2048]{1,0:T(8,128)(2,1)} %param.19) | copy-start | bytes 6291460
  7.2 57.5 %all-gather.5.cloned.1.call-start = ((), (), s32[]{:S(2)}) async-start(), calls=%async_computation.4 | async-start | bytes 5242880 | tf_op jit(solution)/shard_map/all_gather | solution.py:73
  7.9 174.5 %reduce-scatter.5.cloned.1.call-start = ((), (), s32[]{:S(2)}) async-start(), calls=%async_computation.5 | async-start | bytes 10485760 | tf_op jit(solution)/shard_map/reduce_scatter | solution.py:133
  10.9 57.0 %copy-start.42 = (f32[2048]{0:T(1024)S(1)}, f32[2048]{0:T(1024)}, u32[]{:S(2)}) copy-start(f32[2048]{0:T(1024)} %param.23) | copy-start | bytes 24580
  18.0 55.7 %copy-start.11 = (f32[1024,64]{0,1:T(8,128)}, f32[1024,64]{0,1:T(8,128)S(1)}, u32[]{:S(2)}) copy-start(f32[1024,64]{0,1:T(8,128)S(1)} %get-tuple-element.44) | copy-start | bytes 786436
  18.0 55.7 %copy-start.13 = (f32[1024,64]{0,1:T(8,128)}, f32[1024,64]{0,1:T(8,128)S(1)}, u32[]{:S(2)}) copy-start(f32[1024,64]{0,1:T(8,128)S(1)} %get-tuple-element.45) | copy-start | bytes 786436
  64.7 3.4 copy-start.16
  67.9 9.8 copy-start.45
  71.2 11.0 copy-start.20
  74.2 7.9 copy-start.30
  76.5 3.8 copy-start.2
  80.2 4.8 copy-start.23
  83.9 3.4 copy-start.3
  95.8 86.5 %copy-start.8 = (bf16[1,256,2048]{2,1,0:T(8,128)(2,1)S(1)}, bf16[1,256,2048]{2,1,0:T(8,128)(2,1)}, u32[]{:S(2)}) copy-start(bf16[1,256,2048]{2,1,0:T(8,128)(2,1)} %param.14) | copy-start | bytes 3145732
  95.9 90.6 %copy-start.41 = (f32[2048]{0:T(1024)S(1)}, f32[2048]{0:T(1024)}, u32[]{:S(2)}) copy-start(f32[2048]{0:T(1024)} %param.24) | copy-start | bytes 24580
  95.9 144.7 %all-gather.7.cloned.1.call-start = ((), (), s32[]{:S(2)}) async-start(), calls=%async_computation.6 | async-start | bytes 5242880 | tf_op jit(solution)/shard_map/all_gather | solution.py:140
  187.7 107.5 %all-gather.9.cloned.1.call-start = ((), (), s32[]{:S(2)}) async-start(), calls=%async_computation.8 | async-start | bytes 5242880 | tf_op jit(solution)/shard_map/all_gather | solution.py:74
  188.3 230.8 %reduce-scatter.9.cloned.1.call-start = ((), (), s32[]{:S(2)}) async-start(), calls=%async_computation.9 | async-start | bytes 10485760 | tf_op jit(solution)/shard_map/reduce_scatter | solution.py:166
  240.6 12.3 copy-start.47
  310.8 10.8 copy-start.50
  310.8 10.8 copy-start.52
  332.5 89.4 %copy-start.10 = (bf16[1,256,2048]{2,1,0:T(8,128)(2,1)S(1)}, bf16[1,256,2048]{2,1,0:T(8,128)(2,1)}, u32[]{:S(2)}) copy-start(bf16[1,256,2048]{2,1,0:T(8,128)(2,1)} %param.15) | copy-start | bytes 3145732
  332.6 144.7 %all-gather.11.cloned.1.call-start = ((), (), s32[]{:S(2)}) async-start(), calls=%async_computation.10 | async-start | bytes 5242880 | tf_op jit(solution)/shard_map/all_gather | solution.py:176
  419.1 3.5 copy-start.7
  424.4 177.4 %reduce-scatter.11.cloned.1.call-start = ((), (), s32[]{:S(2)}) async-start(), calls=%async_computation.11 | async-start | bytes 10485760 | tf_op jit(solution)/shard_map/reduce_scatter | solution.py:223
  424.5 57.5 %copy-start.24 = (bf16[1024,256]{0,1:T(8,128)(2,1)S(1)}, bf16[1024,256]{0,1:T(8,128)(2,1)}, u32[]{:S(2)}) copy-start(bf16[1024,256]{0,1:T(8,128)(2,1)} %copy-done.23) | copy-start | bytes 1572868
  481.9 5.4 slice-start
  481.9 5.8 slice-start.1
  482.0 12.8 slice-start.2
  487.8 7.0 slice-start.3
  505.8 3.4 copy-start.37
  515.3 143.4 %reduce-scatter.7.cloned.1.call-start = ((), (), s32[]{:S(2)}) async-start(), calls=%async_computation.7 | async-start | bytes 5242880 | tf_op jit(solution)/shard_map/reduce_scatter | solution.py:148
  526.2 1046.9 %all-reduce.4.cloned.1.call-start = ((), (), s32[]{:S(2)}) async-start(), calls=%async_computation.12 | async-start | bytes 94371840 | tf_op jit(solution)/shard_map/psum | solution.py:233
  526.3 12.4 copy-start.48
  526.3 12.4 copy-start.53
  538.7 9.6 copy-start.51
  548.3 9.8 copy-start.17
  548.3 9.8 copy-start.43
  548.3 9.8 copy-start.46
  561.4 3.2 copy-start.36
  561.4 3.2 copy-start.49
  564.6 4.3 copy-start.38
  573.8 28.1 %copy-start.9 = (bf16[1,256,2048]{2,1,0:T(8,128)(2,1)S(1)}, bf16[1,256,2048]{2,1,0:T(8,128)(2,1)}, u32[]{:S(2)}) copy-start(bf16[1,256,2048]{2,1,0:T(8,128)(2,1)} %param.14) | copy-start | bytes 3145732
  573.8 84.9 %copy-start.6 = (f32[256,2048]{1,0:T(8,128)S(1)}, f32[256,2048]{1,0:T(8,128)}, u32[]{:S(2)}) copy-start(f32[256,2048]{1,0:T(8,128)} %copy-done.4) | copy-start | bytes 6291460
  1573.1 4.8 copy-start.28
  1573.1 6.1 copy-start.27
  1578.0 3.7 copy-start.18
  1602.6 10.8 copy-start.1
  (19 other events, 34.1 us)
Sparse Core Ops, SparseCore 0:
  9.9 54.7 all-gather.4
  96.0 86.3 reduce-scatter.4
  187.8 52.7 all-gather.6
  242.4 52.6 all-gather.8
  332.7 86.3 reduce-scatter.8
  424.5 52.7 all-gather.10
  515.4 86.3 reduce-scatter.10
  605.6 52.9 reduce-scatter.6
  663.3 909.8 all-reduce.3
where the time goes:
time: 1630 us; the launch traced here: 1620 us
  waiting for transfers between devices  1310 us (80%)
  matrix products  168 us (10%)
  local copies, waits for them, and re-layouts  55.6 us (3%)
  blocking collectives  39.7 us (2%)
  other arithmetic  32.9 us (2%)
    psum x1, waiting for transfers between devices, local(): lax.psum((grad_wq, grad_wk, grad_wv, grad_wo, mlp_sums[0], mlp_sums[1], m...  909 us
    reduce_scatter x1, waiting for transfers between devices, local(): lax.psum_scatter(total_part + jnp.einsum('sf,df->sd', grad_up_bf, w_up, p...  86.5 us
    reduce_scatter x1, waiting for transfers between devices, local(): lax.psum_scatter(jnp.dot(attn_bf, w_output, preferred_element_type=fp32),...  85.7 us
    all_gather x1, waiting for transfers between devices, local(): lax.all_gather((survive * grad_h_rows).astype(bf16), 'tensor', axis=0, ti...  52.8 us
    all_gather x1, waiting for transfers between devices, local(): lax.all_gather(rms_scale(h_one_rows, gain_mlp).astype(bf16), 'tensor', ax...  51.6 us
    unnamed x123, local copies, waits for them, and re-layouts  49.3 us
    all_gather x1, waiting for transfers between devices, local(): lax.all_gather(tokens, 'tensor', axis=1, tiled=True)  46.7 us
    psum x1, blocking collectives, local(): gain_sums = lax.psum((gain_one_part, gain_two_part), ('dp', 'tensor'))  39.7 us
  transfers between devices with their start and end apart: 9, of which 9 were waited for; matrix products, arithmetic and copies ran while one was open for 6% of the time, Pallas kernels for 0%

commit v1 on v0

v1 whole, which is shorter than its diff:
```python
import math

import jax
import jax.numpy as jnp
from jax import lax
from jax.sharding import PartitionSpec as P

HD = 128
F32 = jnp.float32
BF16 = jnp.bfloat16


def dot(a, b, dims):
    return lax.dot_general(a, b, (dims, ((), ())), preferred_element_type=F32)


def dot_nn(a, b):
    return dot(a, b, ((1,), (0,)))


def dot_nt(a, b):
    return dot(a, b, ((1,), (1,)))


def dot_tn(a, b):
    return dot(a, b, ((0,), (0,)))


def rms_scale(hidden_in, gain_vec):
    return (
        hidden_in
        * lax.rsqrt(jnp.mean(hidden_in * hidden_in, axis=-1, keepdims=True) + 1e-05)
        * gain_vec
    )


def gain_part(hidden_in, grad_rows):
    normed = hidden_in * lax.rsqrt(jnp.mean(hidden_in * hidden_in, axis=-1, keepdims=True) + 1e-05)
    return jnp.sum(grad_rows * normed, axis=0)


def angle_tables(pos_ids, head_width):
    freqs = jnp.exp(
        jnp.arange(head_width // 2, dtype=F32) * (-2.0 * math.log(10000.0) / head_width)
    )
    turned = pos_ids.astype(F32)[:, None] * freqs[None, :]
    return (jnp.cos(turned), jnp.sin(turned))


def rotate(vectors, cos_table, sin_table):
    half_width = vectors.shape[-1] // 2
    first = vectors[..., :half_width]
    second = vectors[..., half_width:]
    cos_part = cos_table[:, None, :]
    sin_part = sin_table[:, None, :]
    return jnp.concatenate(
        [first * cos_part - second * sin_part, second * cos_part + first * sin_part], axis=-1
    )


def swap(value, axis, size, bit):
    return lax.ppermute(value, axis, [(i, i ^ bit) for i in range(size)])


class Rows:
    def __init__(self, size):
        self.size = size
        self.square = size == 4
        me = lax.axis_index("tensor")
        self.ids = [me ^ r for r in range(4)] if self.square else list(range(size))

    def swap(self, value, bit):
        return swap(value, "tensor", self.size, bit)

    def gather(self, block):
        if not self.square:
            whole = lax.all_gather(block, "tensor", axis=0, tiled=True)
            return jnp.split(whole, self.size, axis=0)
        half = block.shape[0] // 2
        top, low = block[:half], block[half:]
        x_top, y_low = self.swap(top, 1), self.swap(low, 2)
        x_low, y_top = self.swap(low, 1), self.swap(top, 2)
        d_top, d_low = self.swap(x_top, 2), self.swap(y_low, 1)
        return [
            block,
            jnp.concatenate([x_top, x_low]),
            jnp.concatenate([y_top, y_low]),
            jnp.concatenate([d_top, d_low]),
        ]

    def scatter(self, parts):
        if not self.square:
            whole = jnp.concatenate(parts, axis=0)
            return lax.psum_scatter(whole, "tensor", scatter_dimension=0, tiled=True).astype(F32)
        own, x_part, y_part, d_part = parts
        half = own.shape[0] // 2
        y_top = self.swap(d_part[:half], 1)
        x_low = self.swap(d_part[half:], 2)
        x_got_top = self.swap(x_part[:half], 1)
        y_got_low = self.swap(y_part[half:], 2)
        x_got_low = self.swap(add(x_part[half:], x_low), 1)
        y_got_top = self.swap(add(y_part[:half], y_top), 2)
        x_got = jnp.concatenate([x_got_top, x_got_low]).astype(F32)
        y_got = jnp.concatenate([y_got_top, y_got_low]).astype(F32)
        return own.astype(F32) + x_got + y_got


def add(a, b):
    return (a.astype(F32) + b.astype(F32)).astype(BF16)


class Sums:
    def __init__(self, size):
        self.size = size
        self.line = size == 8
        where = lax.axis_index("dp")
        self.core = where % 2
        z = where // 2
        self.middle = (z == 1) | (z == 2)

    def hop(self, value, steps):
        pairs = [(2 * a + c, 2 * b + c) for a, b in steps for c in range(2)]
        return lax.ppermute(value, "dp", pairs)

    def halves(self, left, right, axis, start, count):
        half = count // 2
        outs = []
        for pick in (1 - self.core, self.core):
            at = start + pick * half
            if axis == 0:
                outs.append((lax.dynamic_slice_in_dim(left, at, half, 1), right))
            else:
                outs.append((left, lax.dynamic_slice_in_dim(right, at, half, 1)))
        other = dot_tn(*outs[0]).astype(BF16)
        got = swap(other, "dp", self.size, 1)
        return (dot_tn(*outs[1]) + got.astype(F32)).astype(BF16)

    def run(self, jobs):
        if not self.line:
            return [
                lax.psum(dot_tn(left, right).astype(BF16), "dp").astype(F32)
                for left, right, _, _ in jobs
            ]
        todo = []
        for job, (left, right, axis, chunks) in enumerate(jobs):
            total = (left, right)[axis].shape[1]
            step = total // chunks
            for k in range(chunks):
                todo.append((job, axis, k * step, step))
        held, fold, mids, ends, done = {}, {}, {}, {}, {}
        count = len(todo)
        token = None

        def after(*values):
            if token is None:
                return values
            return lax.optimization_barrier((token, *values))[1:]

        for s in range(-1, count + 3):
            if s + 1 < count:
                job, axis, start, step = todo[s + 1]
                left, right = jobs[job][:2]
                held[s + 1] = self.halves(left, right, axis, start, step)
                fold[s + 1] = self.hop(held[s + 1], [(0, 1), (3, 2)])
            if 0 <= s < count:
                mine, got = after(held[s], fold[s])
                held[s] = token = add(mine, got)
                mids[s] = self.hop(held[s], [(1, 2), (2, 1)])
            if 0 <= s - 1 < count:
                mine, got = after(held[s - 1], mids[s - 1])
                held[s - 1] = token = add(mine, got)
                ends[s - 1] = self.hop(held[s - 1], [(1, 0), (2, 3)])
            if 0 <= s - 2 < count:
                mine, got = after(held[s - 2], ends[s - 2])
                held[s - 2] = token = jnp.where(self.middle, mine, got)
                done[s - 2] = swap(held[s - 2], "dp", self.size, 1)
        outs = []
        for job, (left, right, axis, chunks) in enumerate(jobs):
            pieces = []
            for s, what in enumerate(todo):
                if what[0] == job:
                    first = jnp.where(self.core == 0, held[s], done[s])
                    second = jnp.where(self.core == 0, done[s], held[s])
                    pieces += [first, second]
            outs.append(jnp.concatenate(pieces, axis=axis).astype(F32))
        return outs


def psum_small(value, mesh_shape):
    for axis in ("dp", "tensor"):
        size = mesh_shape[axis]
        if size & (size - 1):
            value = lax.psum(value, axis)
            continue
        bit = 1
        while bit < size:
            value = value + swap(value, axis, size, bit)
            bit *= 2
    return value


def local(
    mesh_shape,
    tokens,
    cotangent,
    w_query,
    w_key,
    w_value,
    w_output,
    w_gate,
    w_up,
    w_down,
    gain_attn,
    gain_mlp,
    dropped,
    exit_scale,
    positions,
):
    rows = Rows(mesh_shape["tensor"])
    sums = Sums(mesh_shape["dp"])
    ids = rows.ids
    survive = 1.0 - dropped[0].astype(F32)
    x_rows = tokens[0].astype(F32)
    cot_rows = cotangent[0].astype(F32) * exit_scale[0]
    own_rows = x_rows.shape[0]
    seq_len = own_rows * len(ids)
    n_one_own = rms_scale(x_rows, gain_attn).astype(BF16)
    n_one_parts = rows.gather(n_one_own)
    grad_m_parts = rows.gather((survive * cot_rows).astype(BF16))
    pos_parts = [lax.dynamic_slice_in_dim(positions[0], i * own_rows, own_rows) for i in ids]
    place = jnp.concatenate([i * own_rows + jnp.arange(own_rows, dtype=jnp.int32) for i in ids])
    cos_table, sin_table = angle_tables(jnp.concatenate(pos_parts), HD)
    local_heads = w_query.shape[1] // HD
    local_kv = w_key.shape[1] // HD
    share = local_heads // local_kv
    factor = 1.0 / math.sqrt(HD)

    def part(table, j):
        return table[j * own_rows : (j + 1) * own_rows]

    q_parts, k_parts, v_parts = [], [], []
    for j, block in enumerate(n_one_parts):
        cos_part, sin_part = part(cos_table, j), part(sin_table, j)
        q_parts.append(
            rotate(dot_nn(block, w_query).reshape(own_rows, local_heads, HD), cos_part, sin_part)
            .astype(BF16)
            .reshape(own_rows, local_kv, share, HD)
        )
        k_parts.append(
            rotate(
                dot_nn(block, w_key).reshape(own_rows, local_kv, HD), cos_part, sin_part
            ).astype(BF16)
        )
        v_parts.append(dot_nn(block, w_value).astype(BF16).reshape(own_rows, local_kv, HD))
    key_heads = jnp.concatenate(k_parts)
    value_heads = jnp.concatenate(v_parts)

    def block_scores(query_block, row_place):
        raw = jnp.einsum("qkgd,skd->kgqs", query_block, key_heads, preferred_element_type=F32)
        return jnp.where(place[None, :] <= row_place[:, None], raw * factor, -1e30)

    attn_parts, log_sums, out_parts = {}, {}, {}
    for j in reversed(range(len(ids))):
        masked = block_scores(q_parts[j], part(place, j))
        row_max = jnp.max(masked, axis=-1, keepdims=True)
        powers = jnp.exp(masked - row_max)
        row_total = jnp.sum(powers, axis=-1, keepdims=True)
        prob_bf = (powers / row_total).astype(BF16)
        log_sums[j] = row_max + jnp.log(row_total)
        attn_parts[j] = (
            jnp.einsum("kgqs,skd->qkgd", prob_bf, value_heads, preferred_element_type=F32)
            .reshape(own_rows, local_heads * HD)
            .astype(BF16)
        )
        out_parts[j] = dot_nn(attn_parts[j], w_output).astype(BF16)
    order = range(len(ids))
    attn_bf = jnp.concatenate([attn_parts[j] for j in order])
    h_one_rows = x_rows + survive * rows.scatter([out_parts[j] for j in order])
    n_two_parts = rows.gather(rms_scale(h_one_rows, gain_mlp).astype(BF16))

    hidden_parts, dgate_parts, dup_parts = [], [], []
    for block, grad_block in zip(n_two_parts, grad_m_parts):
        gate_proj = dot_nn(block, w_gate)
        up_proj = dot_nn(block, w_up)
        sig_gate = jax.nn.sigmoid(gate_proj)
        silu_gate = gate_proj * sig_gate
        hidden_parts.append((silu_gate * up_proj).astype(BF16))
        grad_hidden = dot_nt(grad_block, w_down)
        dgate_parts.append(
            (grad_hidden * up_proj * sig_gate * (1.0 + gate_proj * (1.0 - sig_gate))).astype(BF16)
        )
        dup_parts.append((grad_hidden * silu_gate).astype(BF16))
    hidden = jnp.concatenate(hidden_parts)
    dgate = jnp.concatenate(dgate_parts)
    dup = jnp.concatenate(dup_parts)
    n_two = jnp.concatenate(n_two_parts)
    grad_m = jnp.concatenate(grad_m_parts)
    n_one = jnp.concatenate(n_one_parts)

    grad_n_two_rows = rows.scatter(
        [(dot_nt(a, w_gate) + dot_nt(b, w_up)).astype(BF16) for a, b in zip(dgate_parts, dup_parts)]
    )
    mlp_rows = rows.scatter([dot_nn(a, w_down).astype(BF16) for a in hidden_parts])
    mixed = (h_one_rows + survive * mlp_rows).astype(BF16)[None]

    _, pull_two = jax.vjp(lambda hidden_in: rms_scale(hidden_in, gain_mlp), h_one_rows)
    grad_h_rows = cot_rows + pull_two(grad_n_two_rows)[0]
    gain_two_part = gain_part(h_one_rows, grad_n_two_rows)
    grad_a_parts = rows.gather((survive * grad_h_rows).astype(BF16))
    grad_a = jnp.concatenate(grad_a_parts)
    grad_attn = (
        jnp.concatenate([dot_nt(a, w_output).astype(BF16) for a in grad_a_parts])
    ).reshape(seq_len, local_kv, share, HD)

    query_grads = []
    key_grad = jnp.zeros((seq_len, local_kv, HD), F32)
    value_grad = jnp.zeros((seq_len, local_kv, HD), F32)
    for j in order:
        query_block = q_parts[j]
        masked = block_scores(query_block, part(place, j))
        prob_f32 = jnp.exp(masked - log_sums[j])
        prob_bf = prob_f32.astype(BF16)
        grad_block = part(grad_attn, j)
        grad_prob = jnp.einsum(
            "qkgd,skd->kgqs", grad_block, value_heads, preferred_element_type=F32
        )
        row_delta = jnp.sum(prob_f32 * grad_prob, axis=-1, keepdims=True)
        grad_score = (prob_f32 * (grad_prob - row_delta)).astype(BF16)
        query_grads.append(
            jnp.einsum("kgqs,skd->qkgd", grad_score, key_heads, preferred_element_type=F32)
            * factor
        )
        key_grad = (
            key_grad
            + jnp.einsum("kgqs,qkgd->skd", grad_score, query_block, preferred_element_type=F32)
            * factor
        )
        value_grad = value_grad + jnp.einsum(
            "kgqs,qkgd->skd", prob_bf, grad_block, preferred_element_type=F32
        )
    query_grad = jnp.concatenate(query_grads, axis=0).reshape(seq_len, local_heads, HD)
    grad_q_bf = (
        rotate(query_grad, cos_table, -sin_table).reshape(seq_len, local_heads * HD).astype(BF16)
    )
    grad_k_bf = (
        rotate(key_grad, cos_table, -sin_table).reshape(seq_len, local_kv * HD).astype(BF16)
    )
    grad_v_bf = value_grad.reshape(seq_len, local_kv * HD).astype(BF16)
    grad_n_one = rows.scatter(
        [
            (
                dot_nt(part(grad_q_bf, j), w_query)
                + dot_nt(part(grad_k_bf, j), w_key)
                + dot_nt(part(grad_v_bf, j), w_value)
            ).astype(BF16)
            for j in order
        ]
    )
    _, pull_one = jax.vjp(lambda hidden_in: rms_scale(hidden_in, gain_attn), x_rows)
    input_grad = (grad_h_rows + pull_one(grad_n_one)[0])[None]
    gain_one_part = gain_part(x_rows, grad_n_one)
    gain_sums = psum_small(jnp.stack([gain_one_part, gain_two_part]), mesh_shape)

    down, gate, up, out, query, key, value = sums.run(
        [
            (hidden, grad_m, 1, 4),
            (n_two, dgate, 0, 4),
            (n_two, dup, 0, 4),
            (attn_bf, grad_a, 1, 2),
            (n_one, grad_q_bf, 0, 2),
            (n_one, grad_k_bf, 0, 1),
            (n_one, grad_v_bf, 0, 1),
        ]
    )
    return (
        mixed,
        input_grad,
        query,
        key,
        value,
        out,
        gate,
        up,
        down,
        gain_sums[0],
        gain_sums[1],
    )


def solution(mesh):
    shape = dict(mesh.shape)
    placed = (
        P("dp", "tensor", None),
        P("dp", "tensor", None),
        P(None, "tensor"),
        P(None, "tensor"),
        P(None, "tensor"),
        P("tensor", None),
        P(None, "tensor"),
        P(None, "tensor"),
        P("tensor", None),
        P(),
        P(),
        P("dp"),
        P("dp"),
        P("dp", None),
    )

    def step(*args):
        return local(shape, *args)

    return jax.shard_map(
        step,
        mesh=mesh,
        in_specs=placed,
        out_specs=(
            P("dp", "tensor", None),
            P("dp", "tensor", None),
            P(None, "tensor"),
            P(None, "tensor"),
            P(None, "tensor"),
            P("tensor", None),
            P(None, "tensor"),
            P(None, "tensor"),
            P("tensor", None),
            P(),
            P(),
        ),
        check_vma=False,
    )
```

time: 1630 us -> 1000 us (0.61)
  waiting for transfers between devices: 1310 us -> 314 us
  starting transfers between devices: 0.37 us -> 293 us
  other arithmetic: 32.9 us -> 85.2 us
  matrix products: 168 us -> 216 us
  blocking collectives: 39.7 us -> 0 us
  local copies, waits for them, and re-layouts: 55.6 us -> 79.3 us
    psum x1 -> x0, waiting for transfers between devices: 909 us -> none  [local(): lax.psum((grad_wq, grad_wk, grad_wv, grad_wo, mlp_sums[0], mlp_sums[1], m...]
    ppermute x0 -> x143, waiting for transfers between devices: none -> 314 us  [the longest x54 198 us: hop(): return lax.ppermute(value, 'dp', pairs)]
    ppermute x0 -> x143, starting transfers between devices: none -> 293 us  [the longest x54 181 us: hop(): return lax.ppermute(value, 'dp', pairs)]
    reduce_scatter x4 -> x0, waiting for transfers between devices: 214 us -> none  [the longest x1 86.5 us: local(): lax.psum_scatter(total_part + jnp.einsum('sf,df->sd', grad_up_bf, w_up, p...]
    all_gather x4 -> x0, waiting for transfers between devices: 183 us -> none  [the longest x1 52.8 us: local(): lax.all_gather((survive * grad_h_rows).astype(bf16), 'tensor', axis=0, ti...]
    psum x1 -> x0, blocking collectives: 39.7 us -> none  [local(): gain_sums = lax.psum((gain_one_part, gain_two_part), ('dp', 'tensor'))]
    convert_element_type x7 -> x55, other arithmetic: 9.13 us -> 46.1 us  [the longest x7 24.5 us: run(): outs.append(jnp.concatenate(pieces, axis=axis).astype(F32))]
    dot_general x21 -> x92, matrix products: 144 us -> 179 us  [dot(): return lax.dot_general(a, b, (dims, ((), ())), preferred_element_type=F32)]
  transfers between devices with their start and end apart: 9 -> 143, of which waited for: 9 -> 41; matrix products, arithmetic and copies ran while one was open for 6% -> 33% of each run, Pallas kernels for 0% -> 0%
where the time goes in v1:
time: 1000 us; the launch traced here: 994 us
  waiting for transfers between devices  314 us (31%)
  starting transfers between devices  293 us (29%)
  matrix products  216 us (22%)
  other arithmetic  85.2 us (9%)
  local copies, waits for them, and re-layouts  79.3 us (8%)
    ppermute x54, waiting for transfers between devices, hop(): return lax.ppermute(value, 'dp', pairs)  198 us
    ppermute x54, starting transfers between devices, hop(): return lax.ppermute(value, 'dp', pairs)  181 us
    dot_general x92, matrix products, dot(): return lax.dot_general(a, b, (dims, ((), ())), preferred_element_type=F32)  179 us
    ppermute x89, waiting for transfers between devices, swap(): return lax.ppermute(value, axis, [(i, i ^ bit) for i in range(size)])  116 us
    ppermute x89, starting transfers between devices, swap(): return lax.ppermute(value, axis, [(i, i ^ bit) for i in range(size)])  112 us
    unnamed x488, local copies, waits for them, and re-layouts  40.3 us
    convert_element_type x7, other arithmetic, run(): outs.append(jnp.concatenate(pieces, axis=axis).astype(F32))  24.5 us
  transfers between devices with their start and end apart: 143, of which 41 were waited for; matrix products, arithmetic and copies ran while one was open for 33% of the time, Pallas kernels for 0%

profile of v1, /device:TPU:1, one launch (start us, length us, event | category | flops | bytes accessed | tf_op | source)
XLA Modules:
  0.0 994.2 jit_solution(7819407520222115515)
XLA Ops:
  32.4 5.6 fusion.309
  130.2 10.5 %collective-permute-done.8 = bf16[128,2048]{1,0:T(8,128)(2,1)S(1)} collective-permute-done((bf16[128,2048]{1,0:T(8,128)(2,1)S(1)}, bf16[128,2048]{1,0:T(8,128)(2,1)S(1)}, u32[]{:S(2)}, u32[]{:S(2)}) %collective-permute-start.8) | collective-permute-done | bytes 524320 | tf_op jit(solution)/shard_map/ppermute | solution.py:62
  159.9 6.2 collective-permute-done.12
  185.3 5.3 multiply_convert_fusion.2
  199.8 5.4 fusion.31
  206.8 4.5 fusion.33
  214.9 5.6 fusion.306
  223.4 5.9 multiply_convert_fusion.4
  253.0 6.4 collective-permute-start.57
  262.1 4.5 fusion.32
  276.0 9.9 %collective-permute-done.30 = bf16[128,2048]{1,0:T(8,128)(2,1)S(1)} collective-permute-done((bf16[128,2048]{1,0:T(8,128)(2,1)S(1)}, bf16[128,2048]{1,0:T(8,128)(2,1)S(1)}, u32[]{:S(2)}, u32[]{:S(2)}) %collective-permute-start.30) | collective-permute-done | bytes 524320 | tf_op jit(solution)/shard_map/ppermute | solution.py:62
  329.8 7.2 collective-permute-done.22
  348.2 5.7 multiply_reduce_fusion
  368.6 20.2 %collective-permute-done.49 = bf16[1408,256]{1,0:T(8,128)(2,1)} collective-permute-done((bf16[1408,256]{1,0:T(8,128)(2,1)}, bf16[1408,256]{1,0:T(8,128)(2,1)}, u32[]{:S(2)}, u32[]{:S(2)}) %collective-permute-start.49) | collective-permute-done | bytes 720928 | tf_op jit(solution)/shard_map/ppermute | solution.py:123
  395.7 6.3 collective-permute-done.39
  455.0 4.8 collective-permute-start.93
  482.2 10.6 %collective-permute-done.43 = bf16[128,2048]{1,0:T(8,128)(2,1)S(1)} collective-permute-done((bf16[128,2048]{1,0:T(8,128)(2,1)S(1)}, bf16[128,2048]{1,0:T(8,128)(2,1)S(1)}, u32[]{:S(2)}, u32[]{:S(2)}) %collective-permute-start.43) | collective-permute-done | bytes 524320 | tf_op jit(solution)/shard_map/ppermute | solution.py:62
  505.0 17.7 %collective-permute-done.45 = bf16[128,2048]{1,0:T(8,128)(2,1)S(1)} collective-permute-done((bf16[128,2048]{1,0:T(8,128)(2,1)S(1)}, bf16[128,2048]{1,0:T(8,128)(2,1)S(1)}, u32[]{:S(2)}, u32[]{:S(2)}) %collective-permute-start.45) | collective-permute-done | bytes 524320 | tf_op jit(solution)/shard_map/ppermute | solution.py:62
  526.4 18.2 %collective-permute-done.56 = bf16[1408,256]{1,0:T(8,128)(2,1)S(1)} collective-permute-done((bf16[1408,256]{1,0:T(8,128)(2,1)S(1)}, bf16[1408,256]{1,0:T(8,128)(2,1)S(1)}, u32[]{:S(2)}, u32[]{:S(2)}) %collective-permute-start.56) | collective-permute-done | bytes 720928 | tf_op jit(solution)/shard_map/ppermute | solution.py:123
  562.6 11.2 %collective-permute-done.60 = bf16[1408,256]{1,0:T(8,128)(2,1)S(1)} collective-permute-done((bf16[1408,256]{1,0:T(8,128)(2,1)S(1)}, bf16[1408,256]{1,0:T(8,128)(2,1)S(1)}, u32[]{:S(2)}, u32[]{:S(2)}) %collective-permute-start.60) | collective-permute-done | bytes 720928 | tf_op jit(solution)/shard_map/ppermute | solution.py:123
  575.4 34.4 %collective-permute-done.62 = bf16[256,1408]{1,0:T(8,128)(2,1)S(1)} collective-permute-done((bf16[256,1408]{1,0:T(8,128)(2,1)S(1)}, bf16[256,1408]{1,0:T(8,128)(2,1)S(1)}, u32[]{:S(2)}, u32[]{:S(2)}) %collective-permute-start.62) | collective-permute-done | bytes 720928 | tf_op jit(solution)/shard_map/ppermute | solution.py:123
  610.5 4.6 collective-permute-start.140
  615.4 13.7 %collective-permute-done.140 = f32[2,2048]{1,0:T(2,128)S(1)} collective-permute-done((f32[2,2048]{1,0:T(2,128)S(1)}, f32[2,2048]{1,0:T(2,128)S(1)}, u32[]{:S(2)}, u32[]{:S(2)}) %collective-permute-start.140) | collective-permute-done | bytes 16416 | tf_op jit(solution)/shard_map/ppermute | solution.py:62
  642.6 7.9 collective-permute-done.64
  651.3 6.2 collective-permute-start.134
  657.8 7.3 collective-permute-start.86
  665.3 7.4 collective-permute-start.135
  676.2 17.5 %collective-permute-done.68 = bf16[1408,256]{1,0:T(8,128)(2,1)S(1)} collective-permute-done((bf16[1408,256]{1,0:T(8,128)(2,1)S(1)}, bf16[1408,256]{1,0:T(8,128)(2,1)S(1)}, u32[]{:S(2)}, u32[]{:S(2)}) %collective-permute-start.68) | collective-permute-done | bytes 720928 | tf_op jit(solution)/shard_map/ppermute | solution.py:123
  696.1 17.2 %collective-permute-start.82 = (bf16[256,1408]{1,0:T(8,128)(2,1)S(1)}, bf16[256,1408]{1,0:T(8,128)(2,1)S(1)}, u32[]{:S(2)}, u32[]{:S(2)}) collective-permute-start(bf16[256,1408]{1,0:T(8,128)(2,1)S(1)} %copy-done.74), channel_id=1, source_target_pairs={{0,8},{4,12},{24,16},{28,20},{1,9},{5,13},{25,17},{29,21},{2,10},{... | collective-permute-start | bytes 2162696 | tf_op jit(solution)/shard_map/ppermute | solution.py:123
  718.9 22.2 %collective-permute-start.78 = (bf16[256,1408]{1,0:T(8,128)(2,1)S(1)}, bf16[256,1408]{1,0:T(8,128)(2,1)S(1)}, u32[]{:S(2)}, u32[]{:S(2)}) collective-permute-start(bf16[256,1408]{1,0:T(8,128)(2,1)S(1)} %copy-done.77), channel_id=1, source_target_pairs={{0,8},{4,12},{24,16},{28,20},{1,9},{5,13},{25,17},{29,21},{2,10},{... | collective-permute-start | bytes 2162696 | tf_op jit(solution)/shard_map/ppermute | solution.py:123
  742.1 13.2 %collective-permute-done.78 = bf16[256,1408]{1,0:T(8,128)(2,1)S(1)} collective-permute-done((bf16[256,1408]{1,0:T(8,128)(2,1)S(1)}, bf16[256,1408]{1,0:T(8,128)(2,1)S(1)}, u32[]{:S(2)}, u32[]{:S(2)}) %collective-permute-start.78) | collective-permute-done | bytes 720928 | tf_op jit(solution)/shard_map/ppermute | solution.py:123
  757.6 4.9 collective-permute-start.94
  767.9 6.0 convert_element_type.1152
  773.9 11.5 %collective-permute-done.80 = bf16[256,1408]{1,0:T(8,128)(2,1)S(1)} collective-permute-done((bf16[256,1408]{1,0:T(8,128)(2,1)S(1)}, bf16[256,1408]{1,0:T(8,128)(2,1)S(1)}, u32[]{:S(2)}, u32[]{:S(2)}) %collective-permute-start.80) | collective-permute-done | bytes 720928 | tf_op jit(solution)/shard_map/ppermute | solution.py:123
  787.9 17.0 %collective-permute-start.98 = (bf16[512,512]{1,0:T(8,128)(2,1)S(1)}, bf16[512,512]{1,0:T(8,128)(2,1)S(1)}, u32[]{:S(2)}, u32[]{:S(2)}) collective-permute-start(bf16[512,512]{1,0:T(8,128)(2,1)S(1)} %copy-done.92), channel_id=1, source_target_pairs={{0,8},{4,12},{24,16},{28,20},{1,9},{5,13},{25,17},{29,21},{2,10},{... | collective-permute-start | bytes 1572872 | tf_op jit(solution)/shard_map/ppermute | solution.py:123
  811.2 17.3 %collective-permute-start.115 = (bf16[1024,256]{1,0:T(8,128)(2,1)S(1)}, bf16[1024,256]{1,0:T(8,128)(2,1)S(1)}, u32[]{:S(2)}, u32[]{:S(2)}) collective-permute-start(bf16[1024,256]{1,0:T(8,128)(2,1)S(1)} %copy-done.88), channel_id=1, source_target_pairs={{0,8},{4,12},{24,16},{28,20},{1,9},{5,13},{25,17},{29,21},{2,10},{... | collective-permute-start | bytes 1572872 | tf_op jit(solution)/shard_map/ppermute | solution.py:123
  835.6 15.2 %collective-permute-start.110 = (bf16[1024,256]{1,0:T(8,128)(2,1)S(1)}, bf16[1024,256]{1,0:T(8,128)(2,1)S(1)}, u32[]{:S(2)}, u32[]{:S(2)}) collective-permute-start(bf16[1024,256]{1,0:T(8,128)(2,1)S(1)} %copy-done.90), channel_id=1, source_target_pairs={{0,8},{4,12},{24,16},{28,20},{1,9},{5,13},{25,17},{29,21},{2,10},{... | collective-permute-start | bytes 1572872 | tf_op jit(solution)/shard_map/ppermute | solution.py:123
  850.8 5.2 convert_element_type.1150
  859.6 16.6 %collective-permute-start.102 = (bf16[512,512]{1,0:T(8,128)(2,1)S(1)}, bf16[512,512]{1,0:T(8,128)(2,1)S(1)}, u32[]{:S(2)}, u32[]{:S(2)}) collective-permute-start(bf16[512,512]{1,0:T(8,128)(2,1)S(1)} %copy-done.91), channel_id=1, source_target_pairs={{0,8},{4,12},{24,16},{28,20},{1,9},{5,13},{25,17},{29,21},{2,10},{... | collective-permute-start | bytes 1572872 | tf_op jit(solution)/shard_map/ppermute | solution.py:123
  882.5 16.9 %collective-permute-done.100 = bf16[256,1408]{1,0:T(8,128)(2,1)S(1)} collective-permute-done((bf16[256,1408]{1,0:T(8,128)(2,1)S(1)}, bf16[256,1408]{1,0:T(8,128)(2,1)S(1)}, u32[]{:S(2)}, u32[]{:S(2)}) %collective-permute-start.100) | collective-permute-done | bytes 720928 | tf_op jit(solution)/shard_map/ppermute | solution.py:123
  907.4 13.0 %collective-permute-done.104 = bf16[512,512]{1,0:T(8,128)(2,1)S(1)} collective-permute-done((bf16[512,512]{1,0:T(8,128)(2,1)S(1)}, bf16[512,512]{1,0:T(8,128)(2,1)S(1)}, u32[]{:S(2)}, u32[]{:S(2)}) %collective-permute-start.104) | collective-permute-done | bytes 524320 | tf_op jit(solution)/shard_map/ppermute | solution.py:123
  924.0 11.2 %collective-permute-done.108 = bf16[512,512]{1,0:T(8,128)(2,1)S(1)} collective-permute-done((bf16[512,512]{1,0:T(8,128)(2,1)S(1)}, bf16[512,512]{1,0:T(8,128)(2,1)S(1)}, u32[]{:S(2)}, u32[]{:S(2)}) %collective-permute-start.108) | collective-permute-done | bytes 524320 | tf_op jit(solution)/shard_map/ppermute | solution.py:123
  940.1 5.2 convert_element_type.1151
  947.5 6.3 collective-permute-done.112
  959.7 6.2 collective-permute-done.117
  970.5 4.7 collective-permute-done.120
  975.2 5.0 collective-permute-start.121
  983.0 5.4 collective-permute-done.122
  (1044 shorter events, 496.8 us)
Async XLA Ops:
  6.6 59.9 %collective-permute-start.3 = (bf16[128,2048]{1,0:T(8,128)(2,1)}, bf16[128,2048]{1,0:T(8,128)(2,1)}, u32[]{:S(2)}, u32[]{:S(2)}) collective-permute-start(bf16[128,2048]{1,0:T(8,128)(2,1)} %get-tuple-element.285), channel_id=1, source_target_pairs={{0,2},{1,3},{2,0},{3,1},{4,6},{5,7},{6,4},{7,5},{8,10},{9,11},{10,... | collective-permute-start | bytes 1572872 | tf_op jit(solution)/shard_map/ppermute | solution.py:62
  8.7 46.5 %collective-permute-start.1 = (bf16[128,2048]{1,0:T(8,128)(2,1)}, bf16[128,2048]{1,0:T(8,128)(2,1)}, u32[]{:S(2)}, u32[]{:S(2)}) collective-permute-start(bf16[128,2048]{1,0:T(8,128)(2,1)} %get-tuple-element.285), channel_id=1, source_target_pairs={{0,1},{1,0},{2,3},{3,2},{4,5},{5,4},{6,7},{7,6},{8,9},{9,8},{10,11... | collective-permute-start | bytes 1572872 | tf_op jit(solution)/shard_map/ppermute | solution.py:62
  9.9 54.6 %collective-permute-start.2 = (bf16[128,2048]{1,0:T(8,128)(2,1)}, bf16[128,2048]{1,0:T(8,128)(2,1)}, u32[]{:S(2)}, u32[]{:S(2)}) collective-permute-start(bf16[128,2048]{1,0:T(8,128)(2,1)} %get-tuple-element.286), channel_id=1, source_target_pairs={{0,2},{1,3},{2,0},{3,1},{4,6},{5,7},{6,4},{7,5},{8,10},{9,11},{10,... | collective-permute-start | bytes 1572872 | tf_op jit(solution)/shard_map/ppermute | solution.py:62
  10.2 41.9 %collective-permute-start = (bf16[128,2048]{1,0:T(8,128)(2,1)}, bf16[128,2048]{1,0:T(8,128)(2,1)}, u32[]{:S(2)}, u32[]{:S(2)}) collective-permute-start(bf16[128,2048]{1,0:T(8,128)(2,1)} %get-tuple-element.286), channel_id=1, source_target_pairs={{0,1},{1,0},{2,3},{3,2},{4,5},{5,4},{6,7},{7,6},{8,9},{9,8},{10,11... | collective-permute-start | bytes 1572872 | tf_op jit(solution)/shard_map/ppermute | solution.py:62
  14.0 73.0 %collective-permute-start.32 = (bf16[128,2048]{1,0:T(8,128)(2,1)}, bf16[128,2048]{1,0:T(8,128)(2,1)}, u32[]{:S(2)}, u32[]{:S(2)}) collective-permute-start(bf16[128,2048]{1,0:T(8,128)(2,1)} %get-tuple-element.277), channel_id=1, source_target_pairs={{0,2},{1,3},{2,0},{3,1},{4,6},{5,7},{6,4},{7,5},{8,10},{9,11},{10,... | collective-permute-start | bytes 1572872 | tf_op jit(solution)/shard_map/ppermute | solution.py:62
  52.0 26.4 %collective-permute-start.24 = (bf16[128,2048]{1,0:T(8,128)(2,1)}, bf16[128,2048]{1,0:T(8,128)(2,1)}, u32[]{:S(2)}, u32[]{:S(2)}) collective-permute-start(bf16[128,2048]{1,0:T(8,128)(2,1)} %get-tuple-element.277), channel_id=1, source_target_pairs={{0,1},{1,0},{2,3},{3,2},{4,5},{5,4},{6,7},{7,6},{8,9},{9,8},{10,11... | collective-permute-start | bytes 1572872 | tf_op jit(solution)/shard_map/ppermute | solution.py:62
  55.3 29.0 %collective-permute-start.28 = (bf16[128,2048]{1,0:T(8,128)(2,1)}, bf16[128,2048]{1,0:T(8,128)(2,1)}, u32[]{:S(2)}, u32[]{:S(2)}) collective-permute-start(bf16[128,2048]{1,0:T(8,128)(2,1)} %get-tuple-element.278), channel_id=1, source_target_pairs={{0,2},{1,3},{2,0},{3,1},{4,6},{5,7},{6,4},{7,5},{8,10},{9,11},{10,... | collective-permute-start | bytes 1572872 | tf_op jit(solution)/shard_map/ppermute | solution.py:62
  84.3 33.6 %collective-permute-start.27 = (bf16[128,2048]{1,0:T(8,128)(2,1)}, bf16[128,2048]{1,0:T(8,128)(2,1)}, u32[]{:S(2)}, u32[]{:S(2)}) collective-permute-start(bf16[128,2048]{1,0:T(8,128)(2,1)} %collective-permute-done.24), channel_id=1, source_target_pairs={{0,2},{1,3},{2,0},{3,1},{4,6},{5,7},{6,4},{7,5},{8,10},{9,11},{10,... | collective-permute-start | bytes 1572872 | tf_op jit(solution)/shard_map/ppermute | solution.py:62
  84.5 34.6 %collective-permute-start.29 = (bf16[128,2048]{1,0:T(8,128)(2,1)}, bf16[128,2048]{1,0:T(8,128)(2,1)}, u32[]{:S(2)}, u32[]{:S(2)}) collective-permute-start(bf16[128,2048]{1,0:T(8,128)(2,1)} %collective-permute-done.28), channel_id=1, source_target_pairs={{0,1},{1,0},{2,3},{3,2},{4,5},{5,4},{6,7},{7,6},{8,9},{9,8},{10,11... | collective-permute-start | bytes 1572872 | tf_op jit(solution)/shard_map/ppermute | solution.py:62
  193.3 119.3 %collective-permute-start.14 = (bf16[128,2048]{1,0:T(8,128)(2,1)S(1)}, bf16[128,2048]{1,0:T(8,128)(2,1)}, u32[]{:S(2)}, u32[]{:S(2)}) collective-permute-start(bf16[128,2048]{1,0:T(8,128)(2,1)S(1)} %slice.398), channel_id=1, source_target_pairs={{0,1},{1,0},{2,3},{3,2},{4,5},{5,4},{6,7},{7,6},{8,9},{9,8},{10,11... | collective-permute-start | bytes 1572872 | tf_op jit(solution)/shard_map/ppermute | solution.py:62
  194.8 118.4 %collective-permute-start.23 = (bf16[128,2048]{1,0:T(8,128)(2,1)S(1)}, bf16[128,2048]{1,0:T(8,128)(2,1)}, u32[]{:S(2)}, u32[]{:S(2)}) collective-permute-start(bf16[128,2048]{1,0:T(8,128)(2,1)S(1)} %slice.403), channel_id=1, source_target_pairs={{0,2},{1,3},{2,0},{3,1},{4,6},{5,7},{6,4},{7,5},{8,10},{9,11},{10,... | collective-permute-start | bytes 1572872 | tf_op jit(solution)/shard_map/ppermute | solution.py:62
  253.0 36.0 %collective-permute-start.57 = (bf16[1408,256]{1,0:T(8,128)(2,1)}, bf16[1408,256]{1,0:T(8,128)(2,1)S(1)}, u32[]{:S(2)}, u32[]{:S(2)}) collective-permute-start(bf16[1408,256]{1,0:T(8,128)(2,1)} %convolution_convert_fusion.12), channel_id=1, source_target_pairs={{0,4},{4,0},{8,12},{12,8},{16,20},{20,16},{24,28},{28,24},{1,5},{5... | collective-permute-start | bytes 2162696 | tf_op jit(solution)/shard_map/ppermute | solution.py:62
  313.2 23.8 %collective-permute-start.22 = (bf16[128,2048]{1,0:T(8,128)(2,1)S(1)}, bf16[128,2048]{1,0:T(8,128)(2,1)S(1)}, u32[]{:S(2)}, u32[]{:S(2)}) collective-permute-start(bf16[128,2048]{1,0:T(8,128)(2,1)S(1)} %add_convert_fusion.42), channel_id=1, source_target_pairs={{0,2},{1,3},{2,0},{3,1},{4,6},{5,7},{6,4},{7,5},{8,10},{9,11},{10,... | collective-permute-start | bytes 1572872 | tf_op jit(solution)/shard_map/ppermute | solution.py:62
  319.2 24.1 %collective-permute-start.31 = (bf16[128,2048]{1,0:T(8,128)(2,1)S(1)}, bf16[128,2048]{1,0:T(8,128)(2,1)S(1)}, u32[]{:S(2)}, u32[]{:S(2)}) collective-permute-start(bf16[128,2048]{1,0:T(8,128)(2,1)S(1)} %add_convert_fusion.41), channel_id=1, source_target_pairs={{0,1},{1,0},{2,3},{3,2},{4,5},{5,4},{6,7},{7,6},{8,9},{9,8},{10,11... | collective-permute-start | bytes 1572872 | tf_op jit(solution)/shard_map/ppermute | solution.py:62
  319.3 28.9 %collective-permute-start.34 = (bf16[128,2048]{1,0:T(8,128)(2,1)S(1)}, bf16[128,2048]{1,0:T(8,128)(2,1)S(1)}, u32[]{:S(2)}, u32[]{:S(2)}) collective-permute-start(bf16[128,2048]{1,0:T(8,128)(2,1)S(1)} %add_convert_fusion.40), channel_id=1, source_target_pairs={{0,2},{1,3},{2,0},{3,1},{4,6},{5,7},{6,4},{7,5},{8,10},{9,11},{10,... | collective-permute-start | bytes 1572872 | tf_op jit(solution)/shard_map/ppermute | solution.py:62
  325.7 219.3 %collective-permute-start.58 = (bf16[1408,256]{1,0:T(8,128)(2,1)}, bf16[1408,256]{1,0:T(8,128)(2,1)}, u32[]{:S(2)}, u32[]{:S(2)}) collective-permute-start(bf16[1408,256]{1,0:T(8,128)(2,1)} %fusion.42), channel_id=1, source_target_pairs={{0,8},{4,12},{24,16},{28,20},{1,9},{5,13},{25,17},{29,21},{2,10},{... | collective-permute-start | bytes 2162696 | tf_op jit(solution)/shard_map/ppermute | solution.py:123
  337.0 141.1 %collective-permute-start.54 = (bf16[1408,256]{1,0:T(8,128)(2,1)}, bf16[1408,256]{1,0:T(8,128)(2,1)}, u32[]{:S(2)}, u32[]{:S(2)}) collective-permute-start(bf16[1408,256]{1,0:T(8,128)(2,1)} %fusion.41), channel_id=1, source_target_pairs={{0,8},{4,12},{24,16},{28,20},{1,9},{5,13},{25,17},{29,21},{2,10},{... | collective-permute-start | bytes 2162696 | tf_op jit(solution)/shard_map/ppermute | solution.py:123
  341.1 50.5 %collective-permute-start.51 = (bf16[1408,256]{1,0:T(8,128)(2,1)}, bf16[1408,256]{1,0:T(8,128)(2,1)}, u32[]{:S(2)}, u32[]{:S(2)}) collective-permute-start(bf16[1408,256]{1,0:T(8,128)(2,1)} %fusion.40), channel_id=1, source_target_pairs={{0,8},{4,12},{24,16},{28,20},{1,9},{5,13},{25,17},{29,21},{2,10},{... | collective-permute-start | bytes 2162696 | tf_op jit(solution)/shard_map/ppermute | solution.py:123
  343.3 45.6 %collective-permute-start.49 = (bf16[1408,256]{1,0:T(8,128)(2,1)}, bf16[1408,256]{1,0:T(8,128)(2,1)}, u32[]{:S(2)}, u32[]{:S(2)}) collective-permute-start(bf16[1408,256]{1,0:T(8,128)(2,1)} %fusion.39), channel_id=1, source_target_pairs={{0,8},{4,12},{24,16},{28,20},{1,9},{5,13},{25,17},{29,21},{2,10},{... | collective-permute-start | bytes 2162696 | tf_op jit(solution)/shard_map/ppermute | solution.py:123
  360.1 34.6 %collective-permute-start.38 = (bf16[128,2048]{1,0:T(8,128)(2,1)}, bf16[128,2048]{1,0:T(8,128)(2,1)S(1)}, u32[]{:S(2)}, u32[]{:S(2)}) collective-permute-start(bf16[128,2048]{1,0:T(8,128)(2,1)} %get-tuple-element.273), channel_id=1, source_target_pairs={{0,2},{1,3},{2,0},{3,1},{4,6},{5,7},{6,4},{7,5},{8,10},{9,11},{10,... | collective-permute-start | bytes 1572872 | tf_op jit(solution)/shard_map/ppermute | solution.py:62
  388.9 26.1 %collective-permute-start.36 = (bf16[128,2048]{1,0:T(8,128)(2,1)}, bf16[128,2048]{1,0:T(8,128)(2,1)}, u32[]{:S(2)}, u32[]{:S(2)}) collective-permute-start(bf16[128,2048]{1,0:T(8,128)(2,1)} %get-tuple-element.273), channel_id=1, source_target_pairs={{0,1},{1,0},{2,3},{3,2},{4,5},{5,4},{6,7},{7,6},{8,9},{9,8},{10,11... | collective-permute-start | bytes 1572872 | tf_op jit(solution)/shard_map/ppermute | solution.py:62
  402.0 74.0 %collective-permute-start.52 = (bf16[1408,256]{1,0:T(8,128)(2,1)}, bf16[1408,256]{1,0:T(8,128)(2,1)}, u32[]{:S(2)}, u32[]{:S(2)}) collective-permute-start(bf16[1408,256]{1,0:T(8,128)(2,1)} %add_convert_fusion.24), channel_id=1, source_target_pairs={{8,16},{12,20},{16,8},{20,12},{9,17},{13,21},{17,9},{21,13},{10,18... | collective-permute-start | bytes 2162696 | tf_op jit(solution)/shard_map/ppermute | solution.py:123
  437.4 42.3 %collective-permute-start.55 = (bf16[1408,256]{1,0:T(8,128)(2,1)}, bf16[1408,256]{1,0:T(8,128)(2,1)}, u32[]{:S(2)}, u32[]{:S(2)}) collective-permute-start(bf16[1408,256]{1,0:T(8,128)(2,1)} %add_convert_fusion.23), channel_id=1, source_target_pairs={{8,16},{12,20},{16,8},{20,12},{9,17},{13,21},{17,9},{21,13},{10,18... | collective-permute-start | bytes 2162696 | tf_op jit(solution)/shard_map/ppermute | solution.py:123
  455.0 39.2 %collective-permute-start.93 = (bf16[512,512]{1,0:T(8,128)(2,1)S(1)}, bf16[512,512]{1,0:T(8,128)(2,1)S(1)}, u32[]{:S(2)}, u32[]{:S(2)}) collective-permute-start(bf16[512,512]{1,0:T(8,128)(2,1)S(1)} %convolution_convert_fusion.23), channel_id=1, source_target_pairs={{0,4},{4,0},{8,12},{12,8},{16,20},{20,16},{24,28},{28,24},{1,5},{5... | collective-permute-start | bytes 1572872 | tf_op jit(solution)/shard_map/ppermute | solution.py:62
  478.1 24.4 %collective-permute-start.114 = (bf16[1024,256]{1,0:T(8,128)(2,1)S(1)}, bf16[1024,256]{1,0:T(8,128)(2,1)S(1)}, u32[]{:S(2)}, u32[]{:S(2)}) collective-permute-start(bf16[1024,256]{1,0:T(8,128)(2,1)S(1)} %fusion.141), channel_id=1, source_target_pairs={{0,4},{4,0},{8,12},{12,8},{16,20},{20,16},{24,28},{28,24},{1,5},{5... | collective-permute-start | bytes 1572872 | tf_op jit(solution)/shard_map/ppermute | solution.py:62
  492.8 31.3 %collective-permute-start.109 = (bf16[1024,256]{1,0:T(8,128)(2,1)S(1)}, bf16[1024,256]{1,0:T(8,128)(2,1)S(1)}, u32[]{:S(2)}, u32[]{:S(2)}) collective-permute-start(bf16[1024,256]{1,0:T(8,128)(2,1)S(1)} %fusion.138), channel_id=1, source_target_pairs={{0,4},{4,0},{8,12},{12,8},{16,20},{20,16},{24,28},{28,24},{1,5},{5... | collective-permute-start | bytes 1572872 | tf_op jit(solution)/shard_map/ppermute | solution.py:62
  497.9 51.9 %collective-permute-start.42 = (bf16[128,2048]{1,0:T(8,128)(2,1)S(1)}, bf16[128,2048]{1,0:T(8,128)(2,1)S(1)}, u32[]{:S(2)}, u32[]{:S(2)}) collective-permute-start(bf16[128,2048]{1,0:T(8,128)(2,1)S(1)} %slice.428), channel_id=1, source_target_pairs={{0,1},{1,0},{2,3},{3,2},{4,5},{5,4},{6,7},{7,6},{8,9},{9,8},{10,11... | collective-permute-start | bytes 1572872 | tf_op jit(solution)/shard_map/ppermute | solution.py:62
  502.5 48.7 %collective-permute-start.47 = (bf16[128,2048]{1,0:T(8,128)(2,1)S(1)}, bf16[128,2048]{1,0:T(8,128)(2,1)S(1)}, u32[]{:S(2)}, u32[]{:S(2)}) collective-permute-start(bf16[128,2048]{1,0:T(8,128)(2,1)S(1)} %slice.443), channel_id=1, source_target_pairs={{0,2},{1,3},{2,0},{3,1},{4,6},{5,7},{6,4},{7,5},{8,10},{9,11},{10,... | collective-permute-start | bytes 1572872 | tf_op jit(solution)/shard_map/ppermute | solution.py:62
  524.1 23.4 %collective-permute-start.59 = (bf16[1408,256]{1,0:T(8,128)(2,1)S(1)}, bf16[1408,256]{1,0:T(8,128)(2,1)S(1)}, u32[]{:S(2)}, u32[]{:S(2)}) collective-permute-start(bf16[1408,256]{1,0:T(8,128)(2,1)S(1)} %add_convert_fusion.21), channel_id=1, source_target_pairs={{8,16},{12,20},{16,8},{20,12},{9,17},{13,21},{17,9},{21,13},{10,18... | collective-permute-start | bytes 2162696 | tf_op jit(solution)/shard_map/ppermute | solution.py:123
  547.5 168.6 %collective-permute-start.74 = (bf16[256,1408]{1,0:T(8,128)(2,1)S(1)}, bf16[256,1408]{1,0:T(8,128)(2,1)S(1)}, u32[]{:S(2)}, u32[]{:S(2)}) collective-permute-start(bf16[256,1408]{1,0:T(8,128)(2,1)S(1)} %copy-done.75), channel_id=1, source_target_pairs={{0,8},{4,12},{24,16},{28,20},{1,9},{5,13},{25,17},{29,21},{2,10},{... | collective-permute-start | bytes 2162696 | tf_op jit(solution)/shard_map/ppermute | solution.py:123
  549.8 144.8 %collective-permute-start.70 = (bf16[256,1408]{1,0:T(8,128)(2,1)S(1)}, bf16[256,1408]{1,0:T(8,128)(2,1)S(1)}, u32[]{:S(2)}, u32[]{:S(2)}) collective-permute-start(bf16[256,1408]{1,0:T(8,128)(2,1)S(1)} %copy-done.76), channel_id=1, source_target_pairs={{0,8},{4,12},{24,16},{28,20},{1,9},{5,13},{25,17},{29,21},{2,10},{... | collective-permute-start | bytes 2162696 | tf_op jit(solution)/shard_map/ppermute | solution.py:123
  551.2 100.1 %collective-permute-start.66 = (bf16[256,1408]{1,0:T(8,128)(2,1)S(1)}, bf16[256,1408]{1,0:T(8,128)(2,1)S(1)}, u32[]{:S(2)}, u32[]{:S(2)}) collective-permute-start(bf16[256,1408]{1,0:T(8,128)(2,1)S(1)} %copy-done.78), channel_id=1, source_target_pairs={{0,8},{4,12},{24,16},{28,20},{1,9},{5,13},{25,17},{29,21},{2,10},{... | collective-permute-start | bytes 2162696 | tf_op jit(solution)/shard_map/ppermute | solution.py:123
  573.8 36.0 %collective-permute-start.62 = (bf16[256,1408]{1,0:T(8,128)(2,1)S(1)}, bf16[256,1408]{1,0:T(8,128)(2,1)S(1)}, u32[]{:S(2)}, u32[]{:S(2)}) collective-permute-start(bf16[256,1408]{1,0:T(8,128)(2,1)S(1)} %copy-done.79), channel_id=1, source_target_pairs={{0,8},{4,12},{24,16},{28,20},{1,9},{5,13},{25,17},{29,21},{2,10},{... | collective-permute-start | bytes 2162696 | tf_op jit(solution)/shard_map/ppermute | solution.py:123
  575.2 35.3 %collective-permute-start.139 = (f32[2,2048]{1,0:T(2,128)S(1)}, f32[2,2048]{1,0:T(2,128)S(1)}, u32[]{:S(2)}, u32[]{:S(2)}) collective-permute-start(f32[2,2048]{1,0:T(2,128)S(1)} %fusion.272), channel_id=1, source_target_pairs={{0,8},{4,12},{8,0},{12,4},{16,24},{20,28},{24,16},{28,20},{1,9},{5... | collective-permute-start | bytes 49160 | tf_op jit(solution)/shard_map/ppermute | solution.py:62
  609.8 28.4 %collective-permute-start.63 = (bf16[1408,256]{1,0:T(8,128)(2,1)S(1)}, bf16[1408,256]{1,0:T(8,128)(2,1)S(1)}, u32[]{:S(2)}, u32[]{:S(2)}) collective-permute-start(bf16[1408,256]{1,0:T(8,128)(2,1)S(1)} %add_convert_fusion.19), channel_id=1, source_target_pairs={{8,16},{12,20},{16,8},{20,12},{9,17},{13,21},{17,9},{21,13},{10,18... | collective-permute-start | bytes 2162696 | tf_op jit(solution)/shard_map/ppermute | solution.py:123
  638.2 191.7 %collective-permute-start.90 = (bf16[256,1408]{1,0:T(8,128)(2,1)S(1)}, bf16[256,1408]{1,0:T(8,128)(2,1)S(1)}, u32[]{:S(2)}, u32[]{:S(2)}) collective-permute-start(bf16[256,1408]{1,0:T(8,128)(2,1)S(1)} %copy-done.72), channel_id=1, source_target_pairs={{0,8},{4,12},{24,16},{28,20},{1,9},{5,13},{25,17},{29,21},{2,10},{... | collective-permute-start | bytes 2162696 | tf_op jit(solution)/shard_map/ppermute | solution.py:123
  657.8 149.9 %collective-permute-start.86 = (bf16[256,1408]{1,0:T(8,128)(2,1)S(1)}, bf16[256,1408]{1,0:T(8,128)(2,1)S(1)}, u32[]{:S(2)}, u32[]{:S(2)}) collective-permute-start(bf16[256,1408]{1,0:T(8,128)(2,1)S(1)} %copy-done.73), channel_id=1, source_target_pairs={{0,8},{4,12},{24,16},{28,20},{1,9},{5,13},{25,17},{29,21},{2,10},{... | collective-permute-start | bytes 2162696 | tf_op jit(solution)/shard_map/ppermute | solution.py:123
  696.1 90.1 %collective-permute-start.82 = (bf16[256,1408]{1,0:T(8,128)(2,1)S(1)}, bf16[256,1408]{1,0:T(8,128)(2,1)S(1)}, u32[]{:S(2)}, u32[]{:S(2)}) collective-permute-start(bf16[256,1408]{1,0:T(8,128)(2,1)S(1)} %copy-done.74), channel_id=1, source_target_pairs={{0,8},{4,12},{24,16},{28,20},{1,9},{5,13},{25,17},{29,21},{2,10},{... | collective-permute-start | bytes 2162696 | tf_op jit(solution)/shard_map/ppermute | solution.py:123
  716.1 25.2 %collective-permute-start.76 = (bf16[256,1408]{1,0:T(8,128)(2,1)S(1)}, bf16[256,1408]{1,0:T(8,128)(2,1)S(1)}, u32[]{:S(2)}, u32[]{:S(2)}) collective-permute-start(bf16[256,1408]{1,0:T(8,128)(2,1)S(1)} %add_convert_fusion.12), channel_id=1, source_target_pairs={{8,0},{12,4},{16,24},{20,28},{9,1},{13,5},{17,25},{21,29},{10,2},{... | collective-permute-start | bytes 2162696 | tf_op jit(solution)/shard_map/ppermute | solution.py:123
  718.9 36.4 %collective-permute-start.78 = (bf16[256,1408]{1,0:T(8,128)(2,1)S(1)}, bf16[256,1408]{1,0:T(8,128)(2,1)S(1)}, u32[]{:S(2)}, u32[]{:S(2)}) collective-permute-start(bf16[256,1408]{1,0:T(8,128)(2,1)S(1)} %copy-done.77), channel_id=1, source_target_pairs={{0,8},{4,12},{24,16},{28,20},{1,9},{5,13},{25,17},{29,21},{2,10},{... | collective-permute-start | bytes 2162696 | tf_op jit(solution)/shard_map/ppermute | solution.py:123
  757.6 99.4 %collective-permute-start.94 = (bf16[512,512]{1,0:T(8,128)(2,1)}, bf16[512,512]{1,0:T(8,128)(2,1)}, u32[]{:S(2)}, u32[]{:S(2)}) collective-permute-start(bf16[512,512]{1,0:T(8,128)(2,1)} %fusion.125), channel_id=1, source_target_pairs={{0,8},{4,12},{24,16},{28,20},{1,9},{5,13},{25,17},{29,21},{2,10},{... | collective-permute-start | bytes 1572872 | tf_op jit(solution)/shard_map/ppermute | solution.py:123
  787.9 90.6 %collective-permute-start.98 = (bf16[512,512]{1,0:T(8,128)(2,1)S(1)}, bf16[512,512]{1,0:T(8,128)(2,1)S(1)}, u32[]{:S(2)}, u32[]{:S(2)}) collective-permute-start(bf16[512,512]{1,0:T(8,128)(2,1)S(1)} %copy-done.92), channel_id=1, source_target_pairs={{0,8},{4,12},{24,16},{28,20},{1,9},{5,13},{25,17},{29,21},{2,10},{... | collective-permute-start | bytes 1572872 | tf_op jit(solution)/shard_map/ppermute | solution.py:123
  811.2 143.6 %collective-permute-start.115 = (bf16[1024,256]{1,0:T(8,128)(2,1)S(1)}, bf16[1024,256]{1,0:T(8,128)(2,1)S(1)}, u32[]{:S(2)}, u32[]{:S(2)}) collective-permute-start(bf16[1024,256]{1,0:T(8,128)(2,1)S(1)} %copy-done.88), channel_id=1, source_target_pairs={{0,8},{4,12},{24,16},{28,20},{1,9},{5,13},{25,17},{29,21},{2,10},{... | collective-permute-start | bytes 1572872 | tf_op jit(solution)/shard_map/ppermute | solution.py:123
  835.6 100.5 %collective-permute-start.110 = (bf16[1024,256]{1,0:T(8,128)(2,1)S(1)}, bf16[1024,256]{1,0:T(8,128)(2,1)S(1)}, u32[]{:S(2)}, u32[]{:S(2)}) collective-permute-start(bf16[1024,256]{1,0:T(8,128)(2,1)S(1)} %copy-done.90), channel_id=1, source_target_pairs={{0,8},{4,12},{24,16},{28,20},{1,9},{5,13},{25,17},{29,21},{2,10},{... | collective-permute-start | bytes 1572872 | tf_op jit(solution)/shard_map/ppermute | solution.py:123
  859.6 45.7 %collective-permute-start.102 = (bf16[512,512]{1,0:T(8,128)(2,1)S(1)}, bf16[512,512]{1,0:T(8,128)(2,1)S(1)}, u32[]{:S(2)}, u32[]{:S(2)}) collective-permute-start(bf16[512,512]{1,0:T(8,128)(2,1)S(1)} %copy-done.91), channel_id=1, source_target_pairs={{0,8},{4,12},{24,16},{28,20},{1,9},{5,13},{25,17},{29,21},{2,10},{... | collective-permute-start | bytes 1572872 | tf_op jit(solution)/shard_map/ppermute | solution.py:123
  906.8 31.5 %collective-permute-start.133 = (bf16[256,1408]{1,0:T(8,128)(2,1)S(1)}, bf16[256,1408]{1,0:T(8,128)(2,1)S(1)}, u32[]{:S(2)}, u32[]{:S(2)}) collective-permute-start(bf16[256,1408]{1,0:T(8,128)(2,1)S(1)} %broadcast_select_fusion.4), channel_id=1, source_target_pairs={{0,4},{4,0},{8,12},{12,8},{16,20},{20,16},{24,28},{28,24},{1,5},{5... | collective-permute-start | bytes 2162696 | tf_op jit(solution)/shard_map/ppermute | solution.py:62
  922.6 23.5 %collective-permute-start.124 = (bf16[512,512]{1,0:T(8,128)(2,1)S(1)}, bf16[512,512]{1,0:T(8,128)(2,1)S(1)}, u32[]{:S(2)}, u32[]{:S(2)}) collective-permute-start(bf16[512,512]{1,0:T(8,128)(2,1)S(1)} %broadcast_select_fusion.21), channel_id=1, source_target_pairs={{0,4},{4,0},{8,12},{12,8},{16,20},{20,16},{24,28},{28,24},{1,5},{5... | collective-permute-start | bytes 1572872 | tf_op jit(solution)/shard_map/ppermute | solution.py:62
  953.9 26.4 %collective-permute-start.113 = (bf16[512,512]{1,0:T(8,128)(2,1)S(1)}, bf16[512,512]{1,0:T(8,128)(2,1)S(1)}, u32[]{:S(2)}, u32[]{:S(2)}) collective-permute-start(bf16[512,512]{1,0:T(8,128)(2,1)S(1)} %broadcast_select_fusion.19), channel_id=1, source_target_pairs={{0,4},{4,0},{8,12},{12,8},{16,20},{20,16},{24,28},{28,24},{1,5},{5... | collective-permute-start | bytes 1572872 | tf_op jit(solution)/shard_map/ppermute | solution.py:62
  (329 other events, 3163.2 us)

commit v2 on v0

v2 whole, which is shorter than its diff:
```python
import functools
import math

import jax
import jax.numpy as jnp
from jax import lax
from jax.experimental import pallas as pl
from jax.experimental.pallas import tpu as pltpu
from jax.sharding import PartitionSpec as P

HD = 128
EPS = 1e-05
F32 = jnp.float32
BF16 = jnp.bfloat16
VMEM = pl.BlockSpec(memory_space=pltpu.VMEM)
SMEM = pl.BlockSpec(memory_space=pltpu.SMEM)
HBM = pl.BlockSpec(memory_space=pltpu.HBM)
PER_US = 1150000000.0
MIB = 1024 * 1024
LIMIT = 28


def spec(shape, dtype=BF16):
    return jax.ShapeDtypeStruct(tuple(shape), dtype)


def mm(a, b, dims):
    return lax.dot_general(a, b, (dims, ((), ())), preferred_element_type=F32)


def nn(a, b):
    return mm(a, b, ((1,), (0,)))


def nt(a, b):
    return mm(a, b, ((1,), (1,)))


def tn(a, b):
    return mm(a, b, ((0,), (0,)))


def stack(refs):
    return jnp.concatenate([r[...] for r in refs], axis=0)


def tiles(total, step):
    return [(at, min(step, total - at)) for at in range(0, total, step)]


def put_rows(refs, value, cols=slice(None)):
    rows = refs[0].shape[0]
    for i, ref in enumerate(refs):
        ref[:, cols] = value[i * rows : (i + 1) * rows].astype(ref.dtype)


def in_hbm(value):
    return pltpu.with_memory_space_constraint(value, pltpu.HBM)


class Order:
    def __init__(self):
        self.last = ()

    def tie(self, *values):
        if not self.last:
            return values if len(values) > 1 else values[0]
        out = lax.optimization_barrier((self.last[0], *values))[1:]
        return out if len(values) > 1 else out[0]

    def call(
        self,
        body,
        operands,
        outs,
        smem=(),
        prefetch=(),
        scratch=(),
        grid=(),
        ins=None,
        outspecs=None,
        reuse=(),
        us=1.5,
    ):
        ahead, total = len(prefetch) + len(smem), len(prefetch) + len(smem) + len(operands)
        skip = len(self.last) + len(reuse)

        def kernel(*refs):
            results = refs[total + skip :]
            body(*refs[:total], *results[: len(outs)], *results[len(outs) + 1 :])

        got = pl.pallas_call(
            kernel,
            out_shape=(*outs, pltpu.HBM((8, 128), F32)),
            grid_spec=pltpu.PrefetchScalarGridSpec(
                num_scalar_prefetch=len(prefetch),
                grid=grid,
                in_specs=[SMEM] * len(smem)
                + list(ins or [VMEM] * len(operands))
                + [HBM] * skip,
                out_specs=(*(outspecs or [VMEM] * len(outs)), HBM),
                scratch_shapes=scratch,
            ),
            input_output_aliases={total + len(self.last) + n: n for n in range(len(reuse))},
            cost_estimate=pl.CostEstimate(
                flops=int(2e10), bytes_accessed=int(1.2e8), transcendentals=0
            ),
            compiler_params=pltpu.CompilerParams(vmem_limit_bytes=LIMIT * MIB),
        )(*prefetch, *smem, *operands, *map(in_hbm, (*self.last, *reuse)))
        self.last = (got[-1],)
        return got[:-1]


def swap(value, axis, size, bit):
    return lax.ppermute(value, axis, [(i, i ^ bit) for i in range(size)])


def row_blocks(arrays, steps):
    return [pl.BlockSpec((a.shape[0] // steps, a.shape[1]), lambda i: (i, 0)) for a in arrays]


def pointwise(order, body, operands, outs, smem=(), steps=1, us=1.5):
    return order.call(
        body,
        operands,
        outs,
        smem=smem,
        grid=(steps,),
        ins=row_blocks(operands, steps),
        outspecs=row_blocks(outs, steps),
        us=us,
    )


def plus(a_ref, b_ref):
    return a_ref[...].astype(F32) + b_ref[...].astype(F32)


def add(order, a, b):
    def body(a_ref, b_ref, out):
        out[...] = plus(a_ref, b_ref).astype(out.dtype)

    return pointwise(order, body, (a, b), [spec(a.shape, a.dtype)])[0]


class Rows:
    def __init__(self, size, own_rows, square):
        self.size = size
        self.square = square
        me = lax.axis_index("tensor")
        if self.square:
            half = own_rows // 2
            where = [(0, 0), (0, 1), (1, 0), (2, 1), (1, 1), (2, 0), (3, 0), (3, 1)]
            self.bases = jnp.stack([(me ^ r) * own_rows + h * half for r, h in where])
            self.piece = half
            self.blocks = [(6, 7), (2, 4), (5, 3), (0, 1)]
        else:
            self.bases = jnp.arange(size, dtype=jnp.int32) * own_rows
            self.piece = own_rows
            self.blocks = [(i, i + 1) for i in range(0, size, 2)]
        self.count = self.bases.shape[0]
        self.groups = [(i, i + 1) for i in range(0, self.count, 2)]
        self.own = [0, 1] if self.square else None

    def swap(self, value, bit):
        return swap(value, "tensor", self.size, bit)

    def gather_first(self, pieces):
        top, low = pieces
        return [top, low, self.swap(top, 1), self.swap(low, 2)]

    def gather_second(self, pieces):
        top, low = pieces
        return [self.swap(low, 1), self.swap(top, 2)]

    def gather_third(self, x_top, y_low):
        return [self.swap(x_top, 2), self.swap(y_low, 1)]

    def gather_all(self, block):
        return lax.all_gather(block, "tensor", axis=0, tiled=True)

    def gather_whole(self, block):
        return jnp.split(self.gather_all(block), self.size, axis=0)

    def scatter_all(self, whole):
        return lax.psum_scatter(whole, "tensor", scatter_dimension=0, tiled=True)

    def scatter_whole(self, pieces):
        return [[self.scatter_all(jnp.concatenate(pieces, axis=0))]]


class Scatter:
    def __init__(self, order, rows):
        self.order, self.rows, self.parts = order, rows, {}

    def far(self, pieces):
        self.parts.update(pieces)
        if self.rows.square:
            self.y_top = self.rows.swap(pieces[6], 1)
            self.x_low = self.rows.swap(pieces[7], 2)

    def near(self, pieces):
        self.parts.update(pieces)
        if self.rows.square:
            self.x_got_top = self.rows.swap(pieces[2], 1)
            self.y_got_low = self.rows.swap(pieces[3], 2)

    def rest(self, pieces):
        self.parts.update(pieces)
        if self.rows.square:
            self.x_got_low = self.rows.swap(add(self.order, pieces[4], self.x_low), 1)
            self.y_got_top = self.rows.swap(add(self.order, pieces[5], self.y_top), 2)

    def own(self, pieces):
        self.parts.update(pieces)

    def result(self):
        if not self.rows.square:
            return self.rows.scatter_whole([self.parts[i] for i in range(self.rows.count)])
        return [
            [self.parts[0], self.parts[1]],
            [self.x_got_top, self.x_got_low],
            [self.y_got_top, self.y_got_low],
        ]


class Pieced:
    def __init__(self, pieces, rows, width, steps=1):
        self.pieces, self.steps, self.width = pieces, steps, width
        self.grid = (pieces, steps)
        self.block = rows // (pieces * steps)
        self.whole = pl.BlockSpec((self.block, width), lambda p, i: (p * steps + i, 0))
        self.row = pl.BlockSpec((1, width), lambda p, i: (0, 0))

    def piece(self, q):
        last = self.steps - 1
        return pl.BlockSpec(
            (self.block, self.width),
            lambda p, i: (jnp.where(p == q, i, jnp.where(p < q, 0, last)), 0),
        )

    def lists(self, count):
        return [self.piece(q) for _ in range(count) for q in range(self.pieces)]

    def each(self, step):
        for q in range(self.pieces):
            pl.when(pl.program_id(0) == q)(lambda q=q: step(q))

    def total(self, refs, q):
        return sum(ref[...].astype(F32) for ref in refs[q :: self.pieces])


def prepare(order, x, ct, gain, scal, pieces):
    rows, width = x.shape
    plan = Pieced(pieces, rows, width)

    def body(s, x_ref, ct_ref, gain_ref, grad, *outs):
        def step(q):
            value = x_ref[...].astype(F32)
            inv = lax.rsqrt(jnp.mean(value * value, axis=1, keepdims=True) + EPS)
            outs[q][...] = (value * inv * gain_ref[...]).astype(BF16)
            grad[...] = (s[0] * (ct_ref[...].astype(F32) * s[1])).astype(BF16)

        plan.each(step)

    grad, *outs = order.call(
        body,
        (x, ct, gain),
        [spec((rows, width))] + [spec((rows // pieces, width))] * pieces,
        smem=(scal,),
        grid=plan.grid,
        ins=[plan.whole, plan.whole, plan.row],
        outspecs=[plan.whole, *plan.lists(1)], us=2.5)
    return outs, grad


def project(order, pieces, weights, tables, bases, which, earlier=None):
    rows = pieces[0].shape[0]
    width, kv = weights[0].shape[1], weights[1].shape[1]
    many = 0 if earlier is None else len(earlier)
    total = tables[0].shape[0]

    def body(base, a_ref, b_ref, wq, wk, wv, cos_ref, sin_ref, *refs):
        olds, outs = refs[: 2 * many], refs[2 * many :]
        block = stack([a_ref, b_ref])
        ats = [pl.ds(pl.multiple_of(base[i], rows), rows) for i in which]
        cos = jnp.concatenate([cos_ref[at, :] for at in ats])
        sin = jnp.concatenate([sin_ref[at, :] for at in ats])

        def turn(value, refs_out):
            for h in range(value.shape[1] // HD):
                cols = slice(h * HD, (h + 1) * HD)
                u = value[:, cols]
                put_rows(refs_out, u * cos + pltpu.roll(u, HD // 2, 1) * sin, cols)

        turn(nn(block, wq[...]), outs[0:2])
        turn(nn(block, wk[...]), outs[2:4])
        put_rows(outs[4:6], nn(block, wv[...]))
        if many:
            k_all, v_all = outs[6:8]
            done = [i for i in range(many + 2) if i not in which]
            for n, i in enumerate(done):
                at = pl.ds(pl.multiple_of(base[i], rows), rows)
                k_all[at, :] = olds[n][...]
                v_all[at, :] = olds[many + n][...]
            for n in range(2):
                k_all[ats[n], :] = outs[2 + n][...]
                v_all[ats[n], :] = outs[4 + n][...]

    outs = [spec((rows, width))] * 2 + [spec((rows, kv))] * 4
    operands = [*pieces, *weights, *tables]
    if many:
        outs += [spec((total, kv))] * 2
        operands += [k for k, _ in earlier] + [v for _, v in earlier]
    return order.call(body, operands, outs, smem=(bases,), us=2.5)


def attend(order, queries, k_all, v_all, w_out, bases, first):
    piece, width = queries[0].shape
    rows = 2 * piece
    heads = width // HD
    share = heads // (k_all.shape[1] // HD)
    factor = 1.0 / math.sqrt(HD)
    wide = w_out.shape[1]
    blocks = k_all.shape[0] // rows

    def body(base, qa, qb, k_ref, v_ref, wo, *outs):
        attn, lses, parts = outs[0:2], outs[2:4], outs[4:6]
        query_all = stack([qa, qb])
        low = lax.broadcasted_iota(jnp.int32, (rows, rows), 1) <= lax.broadcasted_iota(
            jnp.int32, (rows, rows), 0
        )
        place = base[first] // rows

        def upto(n):
            for h in range(heads):
                g = h // share
                cols = slice(h * HD, (h + 1) * HD)
                kv = slice(g * HD, (g + 1) * HD)
                query = query_all[:, cols]
                raw = [nt(query, k_ref[j * rows : (j + 1) * rows, kv]) for j in range(n)]
                raw[-1] = jnp.where(low, raw[-1], -1e30)
                top = functools.reduce(
                    jnp.maximum, [jnp.max(s, axis=1, keepdims=True) for s in raw]
                )
                powers = [jnp.exp((s - top) * factor) for s in raw]
                total = sum(jnp.sum(p, axis=1, keepdims=True) for p in powers)
                mixed = sum(
                    nn(powers[j].astype(BF16), v_ref[j * rows : (j + 1) * rows, kv])
                    for j in range(n)
                )
                put_rows(attn, mixed / total, cols)
                put_rows(lses, top * factor + jnp.log(total), slice(h, h + 1))

        for n in range(1, blocks + 1):
            pl.when(place == n - 1)(functools.partial(upto, n))
        value = stack(attn)
        for at, size in tiles(wide, 512):
            put_rows(parts, nn(value, wo[:, at : at + size]), slice(at, at + size))

    return order.call(
        body,
        (*queries, k_all, v_all, w_out),
        [spec((piece, width))] * 2 + [spec((piece, heads), F32)] * 2 + [spec((piece, wide))] * 2,
        smem=(bases,), us=3.0)


def second_norm(order, x, sums, gain, scal, pieces):
    rows, width = x.shape
    plan = Pieced(pieces, rows, width)
    count = len(sums)

    def body(s, x_ref, gain_ref, *refs):
        h_one, *outs = refs[count * pieces :]

        def step(q):
            value = x_ref[...].astype(F32) + s[0] * plan.total(refs[: count * pieces], q)
            h_one[...] = value
            inv = lax.rsqrt(jnp.mean(value * value, axis=1, keepdims=True) + EPS)
            outs[q][...] = (value * inv * gain_ref[...]).astype(BF16)

        plan.each(step)

    got = order.call(
        body,
        (x, gain, *[p for s in sums for p in s]),
        [spec((rows, width), F32)] + [spec((rows // pieces, width))] * pieces,
        smem=(scal,),
        grid=plan.grid,
        ins=[plan.whole, plan.row, *plan.lists(count)],
        outspecs=[plan.whole, *plan.lists(1)], us=2.4)
    return got[0], list(got[1:])


def put_pieces(out, value, base, piece, cols=slice(None)):
    for p in range(value.shape[0] // piece):
        at = pl.ds(pl.multiple_of(base[p], piece), piece)
        out[at, cols] = value[p * piece : (p + 1) * piece].astype(out.dtype)


def back_hidden(order, grad_m, w_down, step=512):
    rows, depth = grad_m.shape
    width = w_down.shape[0]

    def body(grad_ref, wd, out):
        out[...] = nt(grad_ref[...], wd[...]).astype(BF16)

    return order.call(
        body,
        (grad_m, w_down),
        [spec((rows, width))],
        grid=(pl.cdiv(width, step),),
        ins=[VMEM, pl.BlockSpec((step, depth), lambda i: (i, 0))],
        outspecs=[pl.BlockSpec((rows, step), lambda i: (0, i))], us=7.3)[0]


def feed_forward(order, n_pieces, dhid, w_gate, w_up, bases, which, step=512):
    piece, depth = n_pieces[0].shape
    width = w_gate.shape[1]
    rows = 2 * piece

    def body(base, na, nb, da, db, wg, wu, hid, dg, du):
        n_two = stack([na, nb])
        gate = nn(n_two, wg[...])
        up = nn(n_two, wu[...])
        grad = stack([da, db]).astype(F32)
        sig = 1.0 / (1.0 + jnp.exp(-gate))
        silu = gate * sig
        hid[...] = (silu * up).astype(BF16)
        dg[...] = (grad * up * (sig + silu * (1.0 - sig))).astype(BF16)
        du[...] = (grad * silu).astype(BF16)

    def rows_of(p):
        return pl.BlockSpec((piece, step), lambda i, base: (base[p] // piece, i))

    across = pl.BlockSpec((depth, step), lambda i, base: (0, i))
    out = pl.BlockSpec((rows, step), lambda i, base: (0, i))
    return order.call(
        body,
        (*n_pieces, dhid, dhid, w_gate, w_up),
        [spec((rows, width))] * 3,
        prefetch=(bases,),
        grid=(pl.cdiv(width, step),),
        ins=[VMEM, VMEM, rows_of(which[0]), rows_of(which[1]), across, across],
        outspecs=[out] * 3, us=7.3)


def back_two(order, dgates, dups, w_gate, w_up, bases, piece, step=256):
    many = len(dgates)
    depth, width = w_gate.shape
    rows = many * dgates[0].shape[0]

    def body(base, *refs):
        wg, wu, out = refs[2 * many :]
        value = nt(stack(refs[:many]), wg[...]) + nt(stack(refs[many : 2 * many]), wu[...])
        put_pieces(out, value, base, piece)

    weight = pl.BlockSpec((step, width), lambda i: (i, 0))
    return order.call(
        body,
        (*dgates, *dups, w_gate, w_up),
        [spec((rows, depth))],
        smem=(bases,),
        grid=(depth // step,),
        ins=[VMEM] * (2 * many) + [weight, weight],
        outspecs=[pl.BlockSpec((rows, step), lambda i: (0, i))], us=16.0)[0]


def down_rows(order, hiddens, w_down, bases, piece, step=512):
    many = len(hiddens)
    width, depth = w_down.shape
    rows = many * hiddens[0].shape[0]

    def body(base, *refs):
        wd, out = refs[many:]
        put_pieces(out, nn(stack(refs[:many]), wd[...]), base, piece)

    return order.call(
        body,
        (*hiddens, w_down),
        [spec((rows, depth))],
        smem=(bases,),
        grid=(depth // step,),
        ins=[VMEM] * many + [pl.BlockSpec((width, step), lambda i: (0, i))],
        outspecs=[pl.BlockSpec((rows, step), lambda i: (0, i))], us=8.5)[0]


def norm_back(h, gain, grad):
    inv = lax.rsqrt(jnp.mean(h * h, axis=1, keepdims=True) + EPS)
    scaled = grad * gain
    mean = jnp.mean(h * scaled, axis=1, keepdims=True)
    return inv * (scaled - h * (inv * inv * mean)), jnp.sum(grad * h * inv, axis=0, keepdims=True)


def second_back(order, h_one, ct, total, gain, scal, steps=2):
    rows, width = h_one.shape

    def body(s, h_ref, ct_ref, total_ref, gain_ref, dh, gsum, out):
        @pl.when(pl.program_id(0) == 0)
        def _():
            gsum[...] = jnp.zeros_like(gsum)

        grad, gain_grad = norm_back(h_ref[...], gain_ref[...], total_ref[...].astype(F32))
        value = ct_ref[...].astype(F32) * s[1] + grad
        dh[...] = value
        gsum[...] += gain_grad
        out[...] = (s[0] * value).astype(BF16)

    block = pl.BlockSpec((rows // steps, width), lambda i: (i, 0))
    row = pl.BlockSpec((1, width), lambda i: (0, 0))
    return order.call(
        body,
        (h_one, ct, total, gain),
        [spec((rows, width), F32), spec((1, width), F32), spec((rows, width))],
        smem=(scal,),
        grid=(steps,),
        ins=[block, block, block, row],
        outspecs=[block, row, block], us=2.6)


def first_back(order, x, dh, total, gain, steps=2):
    rows, width = x.shape

    def body(x_ref, dh_ref, total_ref, gain_ref, out, gsum):
        @pl.when(pl.program_id(0) == 0)
        def _():
            gsum[...] = jnp.zeros_like(gsum)

        grad, gain_grad = norm_back(
            x_ref[...].astype(F32), gain_ref[...], total_ref[...].astype(F32)
        )
        out[...] = dh_ref[...] + grad
        gsum[...] += gain_grad

    block = pl.BlockSpec((rows // steps, width), lambda i: (i, 0))
    row = pl.BlockSpec((1, width), lambda i: (0, 0))
    return order.call(
        body,
        (x, dh, total, gain),
        [spec((rows, width), F32), spec((1, width), F32)],
        grid=(steps,),
        ins=[block, block, block, row],
        outspecs=[block, row], us=2.8)


def mix(order, h_one, total, scal):
    def body(s, h_ref, total_ref, out):
        out[...] = (h_ref[...] + s[0] * total_ref[...].astype(F32)).astype(BF16)

    return pointwise(order, body, (h_one, total), [spec(h_one.shape)], smem=(scal,), steps=2)[0]


def back_out(order, grad_a, w_out, steps=2):
    rows, depth = grad_a.shape
    width = w_out.shape[0]

    def body(a_ref, wo, out):
        out[...] = nt(a_ref[...], wo[...]).astype(BF16)

    return order.call(
        body,
        (grad_a, w_out),
        [spec((rows, width))],
        grid=(steps,),
        ins=[pl.BlockSpec((rows // steps, depth), lambda i: (i, 0)), VMEM],
        outspecs=[pl.BlockSpec((rows // steps, width), lambda i: (i, 0))], us=3.0)[0]


def attend_back(order, qs, k_all, v_all, grads, lses, tables, bases):
    count = len(qs)
    piece, width = qs[0].shape
    rows = 2 * piece
    heads = width // HD
    total, kv_width = k_all.shape
    groups = kv_width // HD
    share = heads // groups
    factor = 1.0 / math.sqrt(HD)

    def body(base, *refs):
        q_in, lse_in = refs[:count], refs[count : 2 * count]
        do_ref, k_ref, v_ref, cos_ref, sin_ref, out, q_ref, lse_ref, dq, dk, dv = refs[2 * count :]
        for p in range(count):
            at = pl.ds(pl.multiple_of(base[p], piece), piece)
            q_ref[at, :] = q_in[p][...]
            lse_ref[at, :] = lse_in[p][...]
        low = lax.broadcasted_iota(jnp.int32, (rows, rows), 1) <= lax.broadcasted_iota(
            jnp.int32, (rows, rows), 0
        )
        dk[...] = jnp.zeros_like(dk)
        dv[...] = jnp.zeros_like(dv)
        for i in range(total // rows):
            here = slice(i * rows, (i + 1) * rows)
            for h in range(heads):
                g = h // share
                cols = slice(h * HD, (h + 1) * HD)
                kv = slice(g * HD, (g + 1) * HD)
                query, grad = q_ref[here, cols], do_ref[here, cols]
                lse = lse_ref[here, h : h + 1]
                probs, dps = [], []
                for j in range(i + 1):
                    there = slice(j * rows, (j + 1) * rows)
                    prob = jnp.exp(nt(query, k_ref[there, kv]) * factor - lse)
                    probs.append(jnp.where(low, prob, 0.0) if j == i else prob)
                    dps.append(nt(grad, v_ref[there, kv]))
                delta = sum(
                    jnp.sum(p * d, axis=1, keepdims=True) for p, d in zip(probs, dps)
                )
                sum_q = jnp.zeros((rows, HD), F32)
                for j in range(i + 1):
                    there = slice(j * rows, (j + 1) * rows)
                    ds = (probs[j] * (dps[j] - delta)).astype(BF16)
                    sum_q += nn(ds, k_ref[there, kv])
                    dk[there, kv] += tn(ds, query)
                    dv[there, kv] += tn(probs[j].astype(BF16), grad)
                dq[here, cols] = sum_q
        for p in range(count):
            at = pl.ds(pl.multiple_of(base[p], piece), piece)
            to = slice(p * piece, (p + 1) * piece)
            cos, sin = cos_ref[at, :], sin_ref[at, :]
            for src, wide, start in ((dq, width, 0), (dk, kv_width, width)):
                for h in range(wide // HD):
                    w = src[at, h * HD : (h + 1) * HD] * factor
                    turned = w * cos - pltpu.roll(w, HD // 2, 1) * sin
                    out[to, start + h * HD : start + (h + 1) * HD] = turned.astype(BF16)
            out[to, width + kv_width :] = dv[at, :].astype(BF16)

    return order.call(
        body,
        (*qs, *lses, grads, k_all, v_all, *tables),
        [spec((total, width + 2 * kv_width))],
        smem=(bases,),
        scratch=[
            pltpu.VMEM((total, width), BF16),
            pltpu.VMEM((total, heads), F32),
            pltpu.VMEM((total, width), F32),
            pltpu.VMEM((total, kv_width), F32),
            pltpu.VMEM((total, kv_width), F32),
        ], us=13.8)[0]


def back_one(order, grads, weights, bases, piece, step=512):
    rows, total = grads.shape
    depth = weights[0].shape[0]
    edges = [0]
    for w in weights:
        edges.append(edges[-1] + w.shape[1])

    def body(base, g_ref, *refs):
        value = sum(
            nt(g_ref[:, edges[i] : edges[i + 1]], refs[i][...]) for i in range(len(weights))
        )
        put_pieces(refs[-1], value, base, piece)

    return order.call(
        body,
        (grads, *weights),
        [spec((rows, depth))],
        smem=(bases,),
        grid=(depth // step,),
        ins=[VMEM] + [pl.BlockSpec((step, w.shape[1]), lambda i: (i, 0)) for w in weights],
        outspecs=[pl.BlockSpec((rows, step), lambda i: (0, i))], us=6.0)[0]


class Job:
    def __init__(self, groups, outs, half=256):
        self.groups, self.outs, self.half = groups, outs, half
        self.pairs = [pair for group in groups for pair in group]
        self.rows = self.pairs[0][0][0].shape[1]
        self.chunks = self.rows // (2 * half)
        self.widths = [sum(right[0].shape[1] for _, right, _ in group) for group in groups]
        self.results = [() for _ in groups]
        self.got = {}


def product(order, job, pick, chunks, bases, piece, add_to=None):
    first, count, half, many = chunks[0], len(chunks), job.half, len(job.groups)
    width = job.widths[0]
    lefts, places = [], []
    for left, _, _ in job.pairs:
        if not any(left is known for known, _ in places):
            places.append((left, len(lefts)))
            lefts += left
    rights = [block for _, right, _ in job.pairs for block in right]
    total = sum(p.shape[0] for p in job.pairs[0][0])
    extra = 0 if add_to is None else 1

    def body(pick_ref, base, *refs):
        left_refs, refs = refs[: len(lefts)], refs[len(lefts) :]
        right_refs, refs = refs[: len(rights)], refs[len(rights) :]
        got, outs, whole = refs[:extra], refs[extra:-1], refs[-1]

        @pl.when(pl.program_id(0) == 0)
        def _():
            at, n = 0, 0
            for _, right, placed in job.pairs:
                wide = right[0].shape[1]
                value = stack(right_refs[n : n + len(right)])
                here = slice(at, at + wide)
                if placed:
                    put_pieces(whole, value, base, piece, here)
                else:
                    whole[:, here] = value
                at += wide
                n += len(right)

        stacks = {
            start: stack(left_refs[start : start + len(left)]) for left, start in places
        }
        at = 0
        for g, group in enumerate(job.groups):
            put = 0
            for left, right, _ in group:
                wide = right[0].shape[1]
                start = next(s for known, s in places if known is left)
                value = tn(stacks[start], whole[:, at : at + wide])
                here = slice(put, put + wide)
                if extra:
                    mine = slice(g * half, (g + 1) * half)
                    value = (value + got[0][mine, here].astype(F32)).astype(BF16)
                    for i in range(count):

                        @pl.when(pl.program_id(0) == i)
                        def _():
                            outs[i * many + g][:, here] = value
                else:
                    outs[0][g * half : (g + 1) * half, here] = value.astype(BF16)
                at += wide
                put += wide

    block = pl.BlockSpec((many * half, width), lambda i, pick_ref, base: (i, 0))
    if extra:
        outs, outspecs = [spec((half, width))] * (count * many), None
    else:
        outs, outspecs = [spec((count * many * half, width))], [block]
    return order.call(
        body,
        (*lefts, *rights, *([add_to] if extra else [])),
        outs,
        prefetch=(pick, bases),
        grid=(count,),
        ins=[
            pl.BlockSpec((p.shape[0], half), lambda i, pick_ref, base: (0, 2 * (first + i) + pick_ref[0]))
            for p in lefts
        ]
        + [VMEM] * len(rights)
        + [block] * extra,
        outspecs=outspecs,
        scratch=[pltpu.VMEM((total, sum(job.widths)), BF16)], us=0.5 + count * many * half * width / 2.4e5)


def lay(order, job, group, core, chunk, mine, other):
    block = job.half

    def body(core_ref, mine_ref, other_ref, *outs):
        for n, ref in ((0, mine_ref), (1, other_ref)):

            @pl.when(pl.program_id(0) == n)
            def _():
                for (at, width, turned), out in zip(job.outs[group], outs):
                    value = ref[:, at : at + width].astype(F32)
                    out[...] = value.T if turned else value

    def place(n, core_ref):
        return 2 * chunk + (core_ref[0] ^ n)

    def across(n, core_ref):
        return (place(n, core_ref), 0)

    def down(n, core_ref):
        return (0, place(n, core_ref))

    shapes, specs = [], []
    for _, width, turned in job.outs[group]:
        shapes.append(pltpu.HBM((width, job.rows) if turned else (job.rows, width), F32))
        specs.append(
            pl.BlockSpec((width, block), down) if turned else pl.BlockSpec((block, width), across)
        )
    job.results[group] = order.call(
        body,
        (mine, other),
        shapes,
        prefetch=(core,),
        grid=(2,),
        outspecs=specs,
        reuse=job.results[group], us=2.5)


class Line:
    LAG = 2

    def __init__(self, order, size, bases, piece):
        self.order, self.size, self.bases, self.piece = order, size, bases, piece
        where = lax.axis_index("dp")
        core, z = where % 2, where // 2
        self.mine = core.reshape(1).astype(jnp.int32)
        self.other = (1 - core).reshape(1).astype(jnp.int32)
        self.middle = ((z == 1) | (z == 2)).astype(jnp.int32).reshape(1)
        self.count = 0
        self.chunks = []
        self.part, self.fold, self.half, self.mids = [], {}, {}, {}
        self.whole, self.ends, self.final, self.done = {}, {}, {}, {}

    def hop(self, value, steps):
        pairs = [(2 * a + c, 2 * b + c) for a, b in steps for c in range(2)]
        return lax.ppermute(value, "dp", pairs)

    def send(self, job, chunks):
        part = product(self.order, job, self.other, chunks, self.bases, self.piece)[0]
        job.got[tuple(chunks)] = swap(part, "dp", self.size, 1)

    def enter(self, job, chunks):
        got = job.got[tuple(chunks)]
        parts = iter(product(self.order, job, self.mine, chunks, self.bases, self.piece, got))
        for k in chunks:
            for group in range(len(job.groups)):
                part = next(parts)
                n = len(self.part)
                if n < 2 * self.LAG:
                    self.fold[n] = self.hop(part, [(0, 1), (3, 2)])
                self.chunks.append((job, group, k))
                self.part.append(part)

    def tick(self, k):
        b, c, ahead = k - self.LAG, k - 2 * self.LAG, k + self.LAG
        here, back, out = k < self.count, 0 <= b < self.count, 0 <= c < self.count
        on = 2 * self.LAG <= ahead < self.count
        merged = back and on and self.half[b].shape == self.part[ahead].shape
        operands, outs = [], []
        if here:
            operands += [self.part[k], self.fold[k]]
            outs.append(spec(self.part[k].shape))
        if back:
            operands += [self.half[b], self.mids[b]]
            outs.append(spec(self.half[b].shape))
        if merged:
            operands.append(self.part[ahead])
        if out:
            operands += [self.whole[c], self.ends[c]]
            outs.append(spec(self.whole[c].shape))

        def body(flag, *refs):
            middle = flag[0] != 0
            refs, results = list(refs[: len(operands)]), list(refs[len(operands) :])
            if here:
                results.pop(0)[...] = plus(refs.pop(0), refs.pop(0)).astype(BF16)
            if back:
                both = plus(refs.pop(0), refs.pop(0)).astype(BF16)
                results.pop(0)[...] = jnp.where(middle, both, refs.pop(0)[...]) if merged else both
            if out:
                results.pop(0)[...] = jnp.where(middle, refs.pop(0)[...], refs.pop(0)[...])

        got = list(pointwise(self.order, body, operands, outs, smem=(self.middle,), us=2.5))
        if here:
            self.half[k] = got.pop(0)
        if back:
            self.whole[b] = got.pop(0)
        if out:
            self.final[c] = got.pop(0)
        if here:
            self.mids[k] = self.hop(self.half[k], [(1, 2), (2, 1), (0, 0), (3, 3)])
        if merged:
            both = self.hop(self.whole[b], [(0, 1), (1, 0), (2, 3), (3, 2)])
            self.ends[b] = self.fold[ahead] = both
        else:
            if back:
                self.ends[b] = self.hop(self.whole[b], [(1, 0), (2, 3)])
            if on:
                self.fold[ahead] = self.hop(self.part[ahead], [(0, 1), (3, 2)])
        if out:
            self.done[c] = swap(self.final[c], "dp", self.size, 1)

    def lay(self, i):
        if 0 <= i < self.count:
            job, group, k = self.chunks[i]
            lay(self.order, job, group, self.mine, k, self.final[i], self.done[i])


class SmallSum:
    def __init__(self, order, value, mesh_shape):
        self.order, self.value = order, value
        self.steps = []
        for axis in ("dp", "tensor"):
            size, bit = mesh_shape[axis], 1
            if size & (size - 1):
                self.steps.append((axis, size, None))
                continue
            while bit < size:
                self.steps.append((axis, size, bit))
                bit *= 2

    def step(self):
        if self.steps:
            axis, size, bit = self.steps.pop(0)
            if bit is None:
                self.value = lax.psum(self.value, axis)
            else:
                self.value = add(self.order, self.value, swap(self.value, axis, size, bit))


def local(
    mesh_shape,
    tokens,
    cotangent,
    w_query,
    w_key,
    w_value,
    w_output,
    w_gate,
    w_up,
    w_down,
    gain_attn,
    gain_mlp,
    dropped,
    exit_scale,
    positions,
):
    x, ct = tokens[0], cotangent[0]
    order = Order()
    square = mesh_shape["tensor"] == 4 and mesh_shape["dp"] == 8
    rows = Rows(mesh_shape["tensor"], x.shape[0], square)
    bases = rows.bases
    line = Line(order, mesh_shape["dp"], bases, rows.piece)
    pieces = 2 if square else 1
    scal = jnp.stack([1.0 - dropped[0].astype(F32), exit_scale[0]])
    gain_one, gain_two = gain_attn[None], gain_mlp[None]
    attn_weights = (w_query, w_key, w_value)

    freqs = jnp.exp(jnp.arange(HD // 2, dtype=F32) * (-2.0 * math.log(10000.0) / HD))
    turned = positions[0].astype(F32)[:, None] * freqs[None, :]
    cos, sin = jnp.cos(turned), jnp.sin(turned)
    tables = (jnp.concatenate([cos, cos], axis=1), jnp.concatenate([-sin, sin], axis=1))

    n_own, grad_m_own = prepare(order, x, ct, gain_one, scal, pieces)
    qs, ks, vs = {}, {}, {}

    def project_group(group, n_one):
        last = group is rows.groups[-1]
        done = [(ks[i], vs[i]) for i in sorted(ks)] if last else None
        got = project(
            order, [n_one[i] for i in group], attn_weights, tables, bases, group, done
        )
        for n, i in enumerate(group):
            qs[i], ks[i], vs[i] = got[n], got[2 + n], got[4 + n]
        return got[6:]

    if square:
        n_one = rows.gather_first(n_own)
        n_one += rows.gather_second(n_own)
        project_group(rows.groups[0], n_one)
        n_one += rows.gather_third(*order.tie(n_one[2], n_one[3]))
        project_group(rows.groups[1], n_one)
        project_group(rows.groups[2], n_one)
        grad_m = rows.gather_all(order.tie(grad_m_own))
        k_all, v_all = project_group(rows.groups[3], n_one)
    else:
        n_one = rows.gather_whole(n_own[0])
        grad_m = rows.gather_all(grad_m_own)
        for group in rows.groups:
            k_all, v_all = project_group(group, n_one) or (None, None)

    attn, lses, parts = {}, {}, {}

    def attend_block(block):
        got = attend(order, [qs[i] for i in block], k_all, v_all, w_output, bases, block[0])
        for n, i in enumerate(block):
            attn[i], lses[i], parts[i] = got[n], got[2 + n], got[4 + n]

    out_sum = Scatter(order, rows)
    if square:
        attend_block(rows.blocks[0])
        out_sum.far({i: parts[i] for i in (6, 7)})
        attend_block(rows.blocks[1])
        attend_block(rows.blocks[2])
        out_sum.near({i: parts[i] for i in (2, 3)})
        out_sum.rest({i: parts[i] for i in (4, 5)})
        attend_block(rows.blocks[3])
        out_sum.own({i: parts[i] for i in (0, 1)})
    else:
        for block in rows.blocks:
            attend_block(block)
        out_sum.own(parts)
    h_one, n_two_own = second_norm(order, x, out_sum.result(), gain_two, scal, pieces)

    hidden, dgate, dup = [], [], []
    dhid = back_hidden(order, grad_m, w_down)

    def feed(g):
        group = rows.groups[g]
        got = feed_forward(
            order, [n_two[i] for i in group], dhid, w_gate, w_up, bases, group
        )
        for made, values in zip(got, (hidden, dgate, dup)):
            values.append(made)

    every = range(rows.count)
    if square:
        n_two = rows.gather_first(n_two_own)
        n_two += rows.gather_second(n_two_own)
        feed(0)
        n_two += rows.gather_third(*order.tie(n_two[2], n_two[3]))
        feed(1)
        feed(2)
        feed(3)
    else:
        n_two = rows.gather_whole(n_two_own[0])
        for g in range(len(rows.groups)):
            feed(g)

    def back_two_all():
        return rows.scatter_all(
            back_two(order, dgate, dup, w_gate, w_up, bases, rows.piece)
        )

    def second_back_all(total):
        return second_back(order, h_one, ct, total, gain_two, scal)

    def attend_back_all(grad_a):
        return attend_back(
            order,
            [qs[i] for i in every],
            k_all,
            v_all,
            back_out(order, grad_a, w_output),
            [lses[i] for i in every],
            tables,
            bases,
        )

    def back_one_all(gqkv):
        return rows.scatter_all(back_one(order, gqkv, attn_weights, bases, rows.piece))

    def down_all():
        return rows.scatter_all(down_rows(order, hidden, w_down, bases, rows.piece))

    ff, width, kv = w_gate.shape[1], w_query.shape[1], w_key.shape[1]
    late_outs = [
        (0, width, True),
        (width, width, False),
        (2 * width, kv, False),
        (2 * width + kv, kv, False),
    ]
    down = Job([[([grad_m], hidden, True)]], [[(0, ff, True)]])
    wide = Job(
        [[(n_two, dgate, False)], [(n_two, dup, False)]], [[(0, ff, False)], [(0, ff, False)]]
    )

    def late_job(grad_a, gqkv):
        every_attn = [attn[i] for i in every]
        return Job([[([grad_a], every_attn, True), (n_one, [gqkv], False)]], [late_outs])

    if square:
        line.count = 16
        line.send(down, [0, 1])
        line.send(down, [2, 3])
        line.enter(down, [0, 1])
        two_total = back_two_all()
        line.tick(0)
        line.enter(down, [2, 3])
        line.send(wide, [0, 1])
        line.tick(1)
        line.enter(wide, [0, 1])
        line.tick(2)
        line.send(wide, [2, 3])
        line.tick(3)
        dh, gain_two_sum, grad_a_own = second_back_all(two_total)
        grad_a = rows.gather_all(grad_a_own)
        line.tick(4)
        line.enter(wide, [2, 3])
        line.tick(5)
        line.lay(0)
        mix_total = down_all()
        line.tick(6)
        line.lay(1)
        line.tick(7)
        line.lay(2)
        gqkv = attend_back_all(grad_a)
        late = late_job(grad_a, gqkv)
        line.tick(8)
        line.lay(3)
        line.send(late, [0, 1, 2, 3])
        one_total = back_one_all(gqkv)
        line.tick(9)
        line.lay(4)
        line.enter(late, [0, 1, 2, 3])
        line.tick(10)
        line.lay(5)
        line.tick(11)
        line.lay(6)
        mixed = mix(order, h_one, mix_total, scal)
        line.tick(12)
        line.lay(7)
        line.tick(13)
        line.lay(8)
        input_grad, gain_one_sum = first_back(order, x, dh, one_total, gain_one)
        gains = SmallSum(order, jnp.concatenate([gain_one_sum, gain_two_sum]), mesh_shape)
        for k in range(14, line.count + 2 * line.LAG):
            line.tick(k)
            line.lay(k - 5)
            gains.step()
        line.lay(line.count - 1)
    else:
        dh, gain_two_sum, grad_a_own = second_back_all(back_two_all())
        grad_a = rows.gather_all(grad_a_own)
        gqkv = attend_back_all(grad_a)
        late = late_job(grad_a, gqkv)
        mixed = mix(order, h_one, down_all(), scal)
        input_grad, gain_one_sum = first_back(order, x, dh, back_one_all(gqkv), gain_one)
        gains = SmallSum(order, jnp.concatenate([gain_one_sum, gain_two_sum]), mesh_shape)
        for job in (down, wide, late):
            for n, group in enumerate(job.groups):
                parts = [tn(jnp.concatenate(a), jnp.concatenate(b)) for a, b, _ in group]
                whole = jnp.concatenate(parts, axis=1).astype(BF16)
                whole = lax.psum(whole, "dp").astype(F32)
                job.results[n] = [
                    whole[:, at : at + size].T if turned else whole[:, at : at + size]
                    for at, size, turned in job.outs[n]
                ]
    while gains.steps:
        gains.step()
    grad_output, grad_query, grad_key, grad_value = late.results[0]
    return (
        mixed[None],
        input_grad[None],
        grad_query,
        grad_key,
        grad_value,
        grad_output,
        wide.results[0][0],
        wide.results[1][0],
        down.results[0][0],
        gains.value[0],
        gains.value[1],
    )


def solution(mesh):
    shape = dict(mesh.shape)
    placed = (
        P("dp", "tensor", None),
        P("dp", "tensor", None),
        P(None, "tensor"),
        P(None, "tensor"),
        P(None, "tensor"),
        P("tensor", None),
        P(None, "tensor"),
        P(None, "tensor"),
        P("tensor", None),
        P(),
        P(),
        P("dp"),
        P("dp"),
        P("dp", None),
    )

    def step(*args):
        return local(shape, *args)

    return jax.shard_map(
        step,
        mesh=mesh,
        in_specs=placed,
        out_specs=(
            P("dp", "tensor", None),
            P("dp", "tensor", None),
            P(None, "tensor"),
            P(None, "tensor"),
            P(None, "tensor"),
            P("tensor", None),
            P(None, "tensor"),
            P(None, "tensor"),
            P("tensor", None),
            P(),
            P(),
        ),
        check_vma=False,
    )
```

time: 1630 us -> 647 us (0.40)
  waiting for transfers between devices: 1310 us -> 152 us
  Pallas kernels: 0 us -> 242 us
  matrix products: 168 us -> 0 us
  starting transfers between devices: 0.37 us -> 132 us
  blocking collectives: 39.7 us -> 0 us
  local copies, waits for them, and re-layouts: 55.6 us -> 87.8 us
  other arithmetic: 32.9 us -> 2.35 us
    psum x1 -> x0, waiting for transfers between devices: 909 us -> none  [local(): lax.psum((grad_wq, grad_wk, grad_wv, grad_wo, mlp_sums[0], mlp_sums[1], m...]
    pallas_call x0 -> x76, Pallas kernels: none -> 242 us  [call(): pl.pallas_call(kernel, out_shape=(*outs, pltpu.HBM((8, 128), F32)), grid_...]
    reduce_scatter x4 -> x3, waiting for transfers between devices: 214 us -> 0.43 us  [scatter_all(): return lax.psum_scatter(whole, 'tensor', scatter_dimension=0, tiled=True)]
    all_gather x4 -> x2, waiting for transfers between devices: 183 us -> 0.01 us  [gather_all(): return lax.all_gather(block, 'tensor', axis=0, tiled=True)]
    dot_general x33 -> x0, matrix products: 168 us -> none  [the longest x1 15.6 us: local(): jnp.einsum('sd,fd->sf', grad_m, w_down, preferred_element_type=fp32)]
    ppermute x0 -> x84, waiting for transfers between devices: none -> 152 us  [the longest x44 79.2 us: swap(): return lax.ppermute(value, axis, [(i, i ^ bit) for i in range(size)])]
    ppermute x0 -> x84, starting transfers between devices: none -> 132 us  [the longest x40 84.9 us: hop(): return lax.ppermute(value, 'dp', pairs)]
    psum x1 -> x0, blocking collectives: 39.7 us -> none  [local(): gain_sums = lax.psum((gain_one_part, gain_two_part), ('dp', 'tensor'))]
  transfers between devices with their start and end apart: 9 -> 89, of which waited for: 9 -> 19; matrix products, arithmetic and copies ran while one was open for 6% -> 0% of each run, Pallas kernels for 0% -> 34%
where the time goes in v2:
time: 647 us; the launch traced here: 635 us
  Pallas kernels  242 us (37%)
  waiting for transfers between devices  152 us (23%)
  starting transfers between devices  132 us (20%)
  local copies, waits for them, and re-layouts  87.8 us (14%)
  between operations  18.3 us (3%)
    pallas_call x76, Pallas kernels, call(): pl.pallas_call(kernel, out_shape=(*outs, pltpu.HBM((8, 128), F32)), grid_...  242 us
    unnamed x492, local copies, waits for them, and re-layouts  87.1 us
    ppermute x40, starting transfers between devices, hop(): return lax.ppermute(value, 'dp', pairs)  84.9 us
    ppermute x44, waiting for transfers between devices, swap(): return lax.ppermute(value, axis, [(i, i ^ bit) for i in range(size)])  79.2 us
    ppermute x40, waiting for transfers between devices, hop(): return lax.ppermute(value, 'dp', pairs)  72.6 us
    ppermute x44, starting transfers between devices, swap(): return lax.ppermute(value, axis, [(i, i ^ bit) for i in range(size)])  47.1 us
  transfers between devices with their start and end apart: 89, of which 19 were waited for; matrix products, arithmetic and copies ran while one was open for 0% of the time, Pallas kernels for 34%

profile of v2, /device:TPU:1, one launch (start us, length us, event | category | flops | bytes accessed | tf_op | source)
XLA Modules:
  0.0 634.6 jit_solution(10513907530739940298)
XLA Ops:
  29.3 10.4 %collective-permute-done.1.refs_2_.refs_6_ = bf16[128,2048]{1,0:T(8,128)(2,1)} collective-permute-done((bf16[128,2048]{1,0:T(8,128)(2,1)}, bf16[128,2048]{1,0:T(8,128)(2,1)}, u32[]{:S(2)}, u32[]{:S(2)}) %collective-permute-start.1) | collective-permute-done | bytes 524320 | tf_op jit(solution)/shard_map/ppermute | solution.py:115
  68.7 3.4 shard_map.225
  72.1 3.7 shard_map.226
  84.6 3.5 shard_map.228
  96.4 18.2 %collective-permute-done.8.refs_5_ = bf16[128,2048]{1,0:T(8,128)(2,1)S(1)} collective-permute-done((bf16[128,2048]{1,0:T(8,128)(2,1)S(1)}, bf16[128,2048]{1,0:T(8,128)(2,1)S(1)}, u32[]{:S(2)}, u32[]{:S(2)}) %collective-permute-start.8) | collective-permute-done | bytes 524320 | tf_op jit(solution)/shard_map/ppermute | solution.py:115
  114.6 19.9 %collective-permute-done.10.refs_7_ = bf16[128,2048]{1,0:T(8,128)(2,1)S(1)} collective-permute-done((bf16[128,2048]{1,0:T(8,128)(2,1)S(1)}, bf16[128,2048]{1,0:T(8,128)(2,1)S(1)}, u32[]{:S(2)}, u32[]{:S(2)}) %collective-permute-start.10) | collective-permute-done | bytes 524320 | tf_op jit(solution)/shard_map/ppermute | solution.py:115
  145.4 7.4 %shard_map.233 = (bf16[1024,1408]{1,0:T(8,128)(2,1)S(1)}, f32[8,128]{1,0:T(8,128)}) custom-call(bf16[1024,2048]{1,0:T(8,128)(2,1)S(1)} %copy-done.9, bf16[1408,2048]{1,0:T(8,128)(2,1)S(1)} %copy-done.5, f32[8,128]{1,0:T(8,128)} %get-tuple-element.323.refs_2_), custom_call_target="tpu_custom_call" | custom-call | flops 20000000000 | bytes 120000000 | tf_op jit(solution)/shard_map/pallas_call | solution.py:92
  158.1 6.6 %shard_map.234 = (bf16[256,1408]{1,0:T(8,128)(2,1)S(1)}, bf16[256,1408]{1,0:T(8,128)(2,1)S(1)}, bf16[256,1408]{1,0:T(8,128)(2,1)S(1)}, f32[8,128]{1,0:T(8,128)}) custom-call(s32[8]{0:T(128)S(1)} %stack.40.refs_0_.refs_1_, bf16[128,2048]{1,0:T(8,128)(2,1)S(1)} %get-tuple-element.319.refs_1_.refs_2_, bf16[128,2048]{1,0:T(8,128)(2,1)S(1)} %get-tuple-element.320.refs_2_.refs_3_, ...), custom_call_target="tpu_custom_call" | custom-call | flops 20000000000 | bytes 120000000 | tf_op jit(solution)/shard_map/pallas_call | solution.py:92
  167.1 7.2 %shard_map.235 = (bf16[256,1408]{1,0:T(8,128)(2,1)S(1)}, bf16[256,1408]{1,0:T(8,128)(2,1)S(1)}, bf16[256,1408]{1,0:T(8,128)(2,1)S(1)}, f32[8,128]{1,0:T(8,128)}) custom-call(s32[8]{0:T(128)S(1)} %stack.40.refs_0_.refs_1_, bf16[128,2048]{1,0:T(8,128)(2,1)S(1)} %collective-permute-done.12.refs_1_.refs_4_, ...), custom_call_target="tpu_custom_call" | custom-call | flops 20000000000 | bytes 120000000 | tf_op jit(solution)/shard_map/pallas_call | solution.py:92
  174.4 7.1 %shard_map.236 = (bf16[256,1408]{1,0:T(8,128)(2,1)S(1)}, bf16[256,1408]{1,0:T(8,128)(2,1)S(1)}, bf16[256,1408]{1,0:T(8,128)(2,1)S(1)}, f32[8,128]{1,0:T(8,128)}) custom-call(s32[8]{0:T(128)S(1)} %stack.40.refs_0_.refs_1_, bf16[128,2048]{1,0:T(8,128)(2,1)} %collective-permute-done.14.refs_1_.refs_6_, ...), custom_call_target="tpu_custom_call" | custom-call | flops 20000000000 | bytes 120000000 | tf_op jit(solution)/shard_map/pallas_call | solution.py:92
  181.7 6.7 %shard_map.237 = (bf16[256,1408]{1,0:T(8,128)(2,1)S(1)}, bf16[256,1408]{1,0:T(8,128)(2,1)S(1)}, bf16[256,1408]{1,0:T(8,128)(2,1)S(1)}, f32[8,128]{1,0:T(8,128)}) custom-call(s32[8]{0:T(128)S(1)} %stack.40.refs_0_.refs_1_, bf16[128,2048]{1,0:T(8,128)(2,1)S(1)} %collective-permute-done.16.refs_1_.refs_8_, ...), custom_call_target="tpu_custom_call" | custom-call | flops 20000000000 | bytes 120000000 | tf_op jit(solution)/shard_map/pallas_call | solution.py:92
  191.5 4.8 collective-permute-start.19
  202.8 4.0 shard_map.240
  206.8 3.2 collective-permute-start.20
  210.1 15.9 %shard_map.241 = (bf16[1024,2048]{1,0:T(8,128)(2,1)S(1)}, f32[8,128]{1,0:T(8,128)}) custom-call(s32[8]{0:T(128)S(1)} %stack.40.refs_0_.refs_1_, bf16[256,1408]{1,0:T(8,128)(2,1)S(1)} %copy-done.99, bf16[256,1408]{1,0:T(8,128)(2,1)S(1)} %copy-done.109, bf16[256,1408]{1,0:T(8,128)(2,1)S(1)} %copy-done.119, ...), custom_call_target="tpu_custom_call" | custom-call | flops 20000000000 | bytes 120000000 | tf_op jit(solution)/shard_map/pallas_call | solution.py:92
  230.3 3.1 shard_map.243
  233.6 6.7 %shard_map.244 = (bf16[1024,1408]{1,0:T(8,128)(2,1)}, f32[8,128]{1,0:T(8,128)}) custom-call(s32[1]{0:T(128)} %bitcast.15.refs_0_, s32[8]{0:T(128)S(1)} %stack.40.refs_0_.refs_1_, bf16[128,2048]{1,0:T(8,128)(2,1)S(1)} %copy-done.50, bf16[128,2048]{1,0:T(8,128)(2,1)S(1)} %copy-done.54, bf16[128,2048]{1,0:T(8,128)(2,1)S(1)} %copy-done.62, ...), custom_call_target="tpu_custom_call" | custom-call | flops 20000000000 | bytes 120000000 | tf_op jit(solution)/shard_map/pallas_call | solution.py:92
  247.5 11.5 %collective-permute-done.22.refs_2_ = bf16[256,1408]{1,0:T(8,128)(2,1)} collective-permute-done((bf16[256,1408]{1,0:T(8,128)(2,1)}, bf16[256,1408]{1,0:T(8,128)(2,1)}, u32[]{:S(2)}, u32[]{:S(2)}) %collective-permute-start.22) | collective-permute-done | bytes 720928 | tf_op jit(solution)/shard_map/ppermute | solution.py:805
  263.2 7.1 %shard_map.246 = (bf16[256,1408]{1,0:T(8,128)(2,1)S(1)}, bf16[256,1408]{1,0:T(8,128)(2,1)S(1)}, bf16[256,1408]{1,0:T(8,128)(2,1)S(1)}, bf16[256,1408]{1,0:T(8,128)(2,1)S(1)}, f32[8,128]{1,0:T(8,128)}) custom-call(s32[1]{0:T(128)} %bitcast.13.refs_0_, s32[8]{0:T(128)S(1)} %stack.40.refs_0_.refs_1_, bf16[128,2048]{1,0:T(8,128)(2,1)S(1)} %copy-done.51, ...), custom_call_target="tpu_custom_call" | custom-call | flops 20000000000 | bytes 120000000 | tf_op jit(solution)/shard_map/pallas_call | solution.py:92
  270.3 4.0 collective-permute-done.23.refs_2_
  278.0 6.9 %collective-permute-start.26 = (bf16[256,1408]{1,0:T(8,128)(2,1)}, bf16[256,1408]{1,0:T(8,128)(2,1)}, u32[]{:S(2)}, u32[]{:S(2)}) collective-permute-start(bf16[256,1408]{1,0:T(8,128)(2,1)} %get-tuple-element.362.refs_3_), channel_id=1, source_target_pairs={{8,16},{12,20},{16,8},{20,12},{0,0},{4,4},{24,24},{28,28},{9,17},{... | collective-permute-start | bytes 2162696 | tf_op jit(solution)/shard_map/ppermute | solution.py:805
  284.8 6.7 %shard_map.248 = (bf16[1024,1408]{1,0:T(8,128)(2,1)}, f32[8,128]{1,0:T(8,128)}) custom-call(s32[1]{0:T(128)} %bitcast.15.refs_0_, s32[8]{0:T(128)S(1)} %stack.40.refs_0_.refs_1_, bf16[128,2048]{1,0:T(8,128)(2,1)S(1)} %copy-done.51, bf16[128,2048]{1,0:T(8,128)(2,1)S(1)} %copy-done.55, bf16[128,2048]{1,0:T(8,128)(2,1)S(1)} %copy-done.63, ...), custom_call_target="tpu_custom_call" | custom-call | flops 20000000000 | bytes 120000000 | tf_op jit(solution)/shard_map/pallas_call | solution.py:92
  299.4 3.4 shard_map.250
  314.7 6.9 %shard_map.252 = (bf16[256,1408]{1,0:T(8,128)(2,1)S(1)}, bf16[256,1408]{1,0:T(8,128)(2,1)S(1)}, bf16[256,1408]{1,0:T(8,128)(2,1)S(1)}, bf16[256,1408]{1,0:T(8,128)(2,1)S(1)}, f32[8,128]{1,0:T(8,128)}) custom-call(s32[1]{0:T(128)} %bitcast.13.refs_0_, s32[8]{0:T(128)S(1)} %stack.40.refs_0_.refs_1_, bf16[128,2048]{1,0:T(8,128)(2,1)S(1)} %copy-done.52, ...), custom_call_target="tpu_custom_call" | custom-call | flops 20000000000 | bytes 120000000 | tf_op jit(solution)/shard_map/pallas_call | solution.py:92
  321.7 3.1 shard_map.253
  332.2 8.4 %shard_map.255 = (bf16[1024,2048]{1,0:T(8,128)(2,1)S(1)}, f32[8,128]{1,0:T(8,128)}) custom-call(s32[8]{0:T(128)S(1)} %stack.40.refs_0_.refs_1_, bf16[256,1408]{1,0:T(8,128)(2,1)S(1)} %copy-done.88, bf16[256,1408]{1,0:T(8,128)(2,1)S(1)} %copy-done.91, bf16[256,1408]{1,0:T(8,128)(2,1)S(1)} %copy-done.94, bf16[256,1408]{1,0:T(8,128)(2,1)S(1)} %copy-done.97, ...), custom_call_target="tpu_custom_call" | custom-call | flops 20000000000 | bytes 120000000 | tf_op jit(solution)/shard_map/pallas_call | solution.py:92
  345.9 5.6 collective-permute-done.38.refs_2_.refs_7_
  356.3 6.8 %collective-permute-start.47 = (bf16[256,1408]{1,0:T(8,128)(2,1)}, bf16[256,1408]{1,0:T(8,128)(2,1)}, u32[]{:S(2)}, u32[]{:S(2)}) collective-permute-start(bf16[256,1408]{1,0:T(8,128)(2,1)} %get-tuple-element.430.refs_3_), channel_id=1, source_target_pairs={{8,16},{12,20},{16,8},{20,12},{0,0},{4,4},{24,24},{28,28},{9,17},{... | collective-permute-start | bytes 2162696 | tf_op jit(solution)/shard_map/ppermute | solution.py:805
  364.1 6.9 %collective-permute-start.36 = (bf16[256,1408]{1,0:T(8,128)(2,1)}, bf16[256,1408]{1,0:T(8,128)(2,1)}, u32[]{:S(2)}, u32[]{:S(2)}) collective-permute-start(bf16[256,1408]{1,0:T(8,128)(2,1)} %get-tuple-element.388.refs_3_), channel_id=1, source_target_pairs={{8,16},{12,20},{16,8},{20,12},{0,0},{4,4},{24,24},{28,28},{9,17},{... | collective-permute-start | bytes 2162696 | tf_op jit(solution)/shard_map/ppermute | solution.py:805
  380.8 13.7 %shard_map.261 = (bf16[1024,1024]{1,0:T(8,128)(2,1)S(1)}, f32[8,128]{1,0:T(8,128)}) custom-call(s32[8]{0:T(128)S(1)} %stack.40.refs_0_.refs_1_, bf16[128,512]{1,0:T(8,128)(2,1)S(1)} %copy-done.185, bf16[128,512]{1,0:T(8,128)(2,1)S(1)} %copy-done.187, bf16[128,512]{1,0:T(8,128)(2,1)S(1)} %copy-done.189, bf16[128,512]{1,0:T(8,128)(2,1)S(1)} %copy-done.192, ...), custom_call_target="tpu_custom_call" | custom-call | flops 20000000000 | bytes 120000000 | tf_op jit(solution)/shard_map/pallas_call | solution.py:92
  394.6 3.8 shard_map.262
  400.4 3.8 shard_map.263
  404.8 7.8 %shard_map.264 = (bf16[1024,1536]{1,0:T(8,128)(2,1)}, f32[8,128]{1,0:T(8,128)}) custom-call(s32[1]{0:T(128)} %bitcast.15.refs_0_, s32[8]{0:T(128)S(1)} %stack.40.refs_0_.refs_1_, bf16[1024,2048]{1,0:T(8,128)(2,1)S(1)} %copy-done.7, bf16[128,2048]{1,0:T(8,128)(2,1)} %get-tuple-element.271.refs_1_.refs_3_, ...), custom_call_target="tpu_custom_call" | custom-call | flops 20000000000 | bytes 120000000 | tf_op jit(solution)/shard_map/pallas_call | solution.py:92
  412.7 6.1 shard_map.265
  420.9 3.6 shard_map.266
  433.5 9.1 %shard_map.268 = (bf16[256,1536]{1,0:T(8,128)(2,1)S(1)}, bf16[256,1536]{1,0:T(8,128)(2,1)S(1)}, bf16[256,1536]{1,0:T(8,128)(2,1)S(1)}, bf16[256,1536]{1,0:T(8,128)(2,1)}, f32[8,128]{1,0:T(8,128)}) custom-call(s32[1]{0:T(128)} %bitcast.13.refs_0_, s32[8]{0:T(128)S(1)} %stack.40.refs_0_.refs_1_, bf16[1024,2048]{1,0:T(8,128)(2,1)S(1)} %copy-done.8, ...), custom_call_target="tpu_custom_call" | custom-call | flops 20000000000 | bytes 120000000 | tf_op jit(solution)/shard_map/pallas_call | solution.py:92
  442.6 3.1 shard_map.269
  452.8 5.8 collective-permute-start.52
  478.7 3.2 shard_map.274
  485.0 16.5 %collective-permute-done.58.refs_6_ = bf16[256,1408]{1,0:T(8,128)(2,1)S(1)} collective-permute-done((bf16[256,1408]{1,0:T(8,128)(2,1)S(1)}, bf16[256,1408]{1,0:T(8,128)(2,1)S(1)}, u32[]{:S(2)}, u32[]{:S(2)}) %collective-permute-start.58) | collective-permute-done | bytes 720928 | tf_op jit(solution)/shard_map/ppermute | solution.py:805
  507.1 7.4 %collective-permute-start.66 = (bf16[256,1536]{1,0:T(8,128)(2,1)}, bf16[256,1536]{1,0:T(8,128)(2,1)}, u32[]{:S(2)}, u32[]{:S(2)}) collective-permute-start(bf16[256,1536]{1,0:T(8,128)(2,1)} %get-tuple-element.472.refs_3_), channel_id=1, source_target_pairs={{8,16},{12,20},{16,8},{20,12},{0,0},{4,4},{24,24},{28,28},{9,17},{... | collective-permute-start | bytes 2359304 | tf_op jit(solution)/shard_map/ppermute | solution.py:805
  521.6 3.1 collective-permute-done.65.refs_2_
  535.9 4.6 collective-permute-start.70
  546.3 11.6 %collective-permute-done.70.refs_1_ = f32[2,2048]{1,0:T(2,128)S(1)} collective-permute-done((f32[2,2048]{1,0:T(2,128)S(1)}, f32[2,2048]{1,0:T(2,128)S(1)}, u32[]{:S(2)}, u32[]{:S(2)}) %collective-permute-start.70) | collective-permute-done | bytes 16416 | tf_op jit(solution)/shard_map/ppermute | solution.py:115
  559.2 6.9 %collective-permute-start.72 = (f32[2,2048]{1,0:T(2,128)S(1)}, f32[2,2048]{1,0:T(2,128)S(1)}, u32[]{:S(2)}, u32[]{:S(2)}) collective-permute-start(f32[2,2048]{1,0:T(2,128)S(1)} %get-tuple-element.486.refs_0_), channel_id=1, source_target_pairs={{0,16},{4,20},{8,24},{12,28},{16,0},{20,4},{24,8},{28,12},{1,17},{... | collective-permute-start | bytes 49160 | tf_op jit(solution)/shard_map/ppermute | solution.py:115
  568.1 15.2 %collective-permute-done.72.refs_1_ = f32[2,2048]{1,0:T(2,128)S(1)} collective-permute-done((f32[2,2048]{1,0:T(2,128)S(1)}, f32[2,2048]{1,0:T(2,128)S(1)}, u32[]{:S(2)}, u32[]{:S(2)}) %collective-permute-start.72) | collective-permute-done | bytes 16416 | tf_op jit(solution)/shard_map/ppermute | solution.py:115
  590.8 14.6 %collective-permute-done.81.refs_2_ = bf16[256,1536]{1,0:T(8,128)(2,1)S(1)} collective-permute-done((bf16[256,1536]{1,0:T(8,128)(2,1)S(1)}, bf16[256,1536]{1,0:T(8,128)(2,1)S(1)}, u32[]{:S(2)}, u32[]{:S(2)}) %collective-permute-start.81) | collective-permute-done | bytes 786464 | tf_op jit(solution)/shard_map/ppermute | solution.py:805
  608.7 13.7 %collective-permute-done.76.refs_2_ = bf16[256,1536]{1,0:T(8,128)(2,1)S(1)} collective-permute-done((bf16[256,1536]{1,0:T(8,128)(2,1)S(1)}, bf16[256,1536]{1,0:T(8,128)(2,1)S(1)}, u32[]{:S(2)}, u32[]{:S(2)}) %collective-permute-start.76) | collective-permute-done | bytes 786464 | tf_op jit(solution)/shard_map/ppermute | solution.py:805
  (714 shorter events, 253.7 us)
Async XLA Ops:
  7.2 133.4 %all-gather.3.cloned.1.call-start = ((), (), s32[]{:S(2)}) async-start(), calls=%async_computation.3 | async-start | bytes 5242880 | tf_op jit(solution)/shard_map/all_gather | solution.py:180
  14.4 35.2 %collective-permute-start.5 = (bf16[128,2048]{1,0:T(8,128)(2,1)}, bf16[128,2048]{1,0:T(8,128)(2,1)}, u32[]{:S(2)}, u32[]{:S(2)}) collective-permute-start(bf16[128,2048]{1,0:T(8,128)(2,1)} %get-tuple-element.271.refs_1_.refs_3_), channel_id=1, source_target_pairs={{0,2},{1,3},{2,0},{3,1},{4,6},{5,7},{6,4},{7,5},{8,10},{9,11},{10,... | collective-permute-start | bytes 1572872 | tf_op jit(solution)/shard_map/ppermute | solution.py:115
  17.7 31.9 %collective-permute-start.4 = (bf16[128,2048]{1,0:T(8,128)(2,1)}, bf16[128,2048]{1,0:T(8,128)(2,1)}, u32[]{:S(2)}, u32[]{:S(2)}) collective-permute-start(bf16[128,2048]{1,0:T(8,128)(2,1)} %get-tuple-element.272.refs_2_.refs_4_), channel_id=1, source_target_pairs={{0,1},{1,0},{2,3},{3,2},{4,5},{5,4},{6,7},{7,6},{8,9},{9,8},{10,11... | collective-permute-start | bytes 1572872 | tf_op jit(solution)/shard_map/ppermute | solution.py:115
  56.0 239.9 %reduce-scatter.4.cloned.1.call-start = ((), (), s32[]{:S(2)}) async-start(), calls=%async_computation.4 | async-start | bytes 5242880 | tf_op jit(solution)/shard_map/reduce_scatter | solution.py:186
  83.7 30.9 %collective-permute-start.8 = (bf16[128,2048]{1,0:T(8,128)(2,1)S(1)}, bf16[128,2048]{1,0:T(8,128)(2,1)S(1)}, u32[]{:S(2)}, u32[]{:S(2)}) collective-permute-start(bf16[128,2048]{1,0:T(8,128)(2,1)S(1)} %get-tuple-element.313), channel_id=1, source_target_pairs={{0,1},{1,0},{2,3},{3,2},{4,5},{5,4},{6,7},{7,6},{8,9},{9,8},{10,11... | collective-permute-start | bytes 1572872 | tf_op jit(solution)/shard_map/ppermute | solution.py:115
  88.2 26.5 %collective-permute-start.11 = (bf16[128,2048]{1,0:T(8,128)(2,1)S(1)}, bf16[128,2048]{1,0:T(8,128)(2,1)S(1)}, u32[]{:S(2)}, u32[]{:S(2)}) collective-permute-start(bf16[128,2048]{1,0:T(8,128)(2,1)S(1)} %get-tuple-element.316), channel_id=1, source_target_pairs={{0,2},{1,3},{2,0},{3,1},{4,6},{5,7},{6,4},{7,5},{8,10},{9,11},{10,... | collective-permute-start | bytes 1572872 | tf_op jit(solution)/shard_map/ppermute | solution.py:115
  92.3 42.2 %collective-permute-start.10 = (bf16[128,2048]{1,0:T(8,128)(2,1)S(1)}, bf16[128,2048]{1,0:T(8,128)(2,1)S(1)}, u32[]{:S(2)}, u32[]{:S(2)}) collective-permute-start(bf16[128,2048]{1,0:T(8,128)(2,1)S(1)} %get-tuple-element.315), channel_id=1, source_target_pairs={{0,2},{1,3},{2,0},{3,1},{4,6},{5,7},{6,4},{7,5},{8,10},{9,11},{10,... | collective-permute-start | bytes 1572872 | tf_op jit(solution)/shard_map/ppermute | solution.py:115
  92.8 41.8 %collective-permute-start.9 = (bf16[128,2048]{1,0:T(8,128)(2,1)S(1)}, bf16[128,2048]{1,0:T(8,128)(2,1)S(1)}, u32[]{:S(2)}, u32[]{:S(2)}) collective-permute-start(bf16[128,2048]{1,0:T(8,128)(2,1)S(1)} %get-tuple-element.314), channel_id=1, source_target_pairs={{0,1},{1,0},{2,3},{3,2},{4,5},{5,4},{6,7},{7,6},{8,9},{9,8},{10,11... | collective-permute-start | bytes 1572872 | tf_op jit(solution)/shard_map/ppermute | solution.py:115
  137.7 36.7 %collective-permute-start.15 = (bf16[128,2048]{1,0:T(8,128)(2,1)S(1)}, bf16[128,2048]{1,0:T(8,128)(2,1)S(1)}, u32[]{:S(2)}, u32[]{:S(2)}) collective-permute-start(bf16[128,2048]{1,0:T(8,128)(2,1)S(1)} %get-tuple-element.319.refs_1_.refs_2_), channel_id=1, source_target_pairs={{0,2},{1,3},{2,0},{3,1},{4,6},{5,7},{6,4},{7,5},{8,10},{9,11},{10,... | collective-permute-start | bytes 1572872 | tf_op jit(solution)/shard_map/ppermute | solution.py:115
  137.8 27.7 %collective-permute-start.12 = (bf16[128,2048]{1,0:T(8,128)(2,1)S(1)}, bf16[128,2048]{1,0:T(8,128)(2,1)S(1)}, u32[]{:S(2)}, u32[]{:S(2)}) collective-permute-start(bf16[128,2048]{1,0:T(8,128)(2,1)S(1)} %get-tuple-element.319.refs_1_.refs_2_), channel_id=1, source_target_pairs={{0,1},{1,0},{2,3},{3,2},{4,5},{5,4},{6,7},{7,6},{8,9},{9,8},{10,11... | collective-permute-start | bytes 1572872 | tf_op jit(solution)/shard_map/ppermute | solution.py:115
  139.1 35.2 %collective-permute-start.14 = (bf16[128,2048]{1,0:T(8,128)(2,1)S(1)}, bf16[128,2048]{1,0:T(8,128)(2,1)}, u32[]{:S(2)}, u32[]{:S(2)}) collective-permute-start(bf16[128,2048]{1,0:T(8,128)(2,1)S(1)} %get-tuple-element.320.refs_2_.refs_3_), channel_id=1, source_target_pairs={{0,1},{1,0},{2,3},{3,2},{4,5},{5,4},{6,7},{7,6},{8,9},{9,8},{10,11... | collective-permute-start | bytes 1572872 | tf_op jit(solution)/shard_map/ppermute | solution.py:115
  139.3 26.3 %collective-permute-start.13 = (bf16[128,2048]{1,0:T(8,128)(2,1)S(1)}, bf16[128,2048]{1,0:T(8,128)(2,1)}, u32[]{:S(2)}, u32[]{:S(2)}) collective-permute-start(bf16[128,2048]{1,0:T(8,128)(2,1)S(1)} %get-tuple-element.320.refs_2_.refs_3_), channel_id=1, source_target_pairs={{0,2},{1,3},{2,0},{3,1},{4,6},{5,7},{6,4},{7,5},{8,10},{9,11},{10,... | collective-permute-start | bytes 1572872 | tf_op jit(solution)/shard_map/ppermute | solution.py:115
  199.3 28.9 %collective-permute-start.18 = (bf16[512,1408]{1,0:T(8,128)(2,1)S(1)}, bf16[512,1408]{1,0:T(8,128)(2,1)S(1)}, u32[]{:S(2)}, u32[]{:S(2)}) collective-permute-start(bf16[512,1408]{1,0:T(8,128)(2,1)S(1)} %get-tuple-element.345), channel_id=1, source_target_pairs={{0,4},{4,0},{8,12},{12,8},{16,20},{20,16},{24,28},{28,24},{1,5},{5... | collective-permute-start | bytes 4325384 | tf_op jit(solution)/shard_map/ppermute | solution.py:115
  244.0 131.0 %all-gather.5.cloned.1.call-start = ((), (), s32[]{:S(2)}) async-start(), calls=%async_computation.6 | async-start | bytes 5242880 | tf_op jit(solution)/shard_map/all_gather | solution.py:180
  244.1 30.3 %collective-permute-start.23 = (bf16[256,1408]{1,0:T(8,128)(2,1)S(1)}, bf16[256,1408]{1,0:T(8,128)(2,1)S(1)}, u32[]{:S(2)}, u32[]{:S(2)}) collective-permute-start(bf16[256,1408]{1,0:T(8,128)(2,1)S(1)} %get-tuple-element.358.refs_1_), channel_id=1, source_target_pairs={{0,8},{4,12},{24,16},{28,20},{1,9},{5,13},{25,17},{29,21},{2,10},{... | collective-permute-start | bytes 2162696 | tf_op jit(solution)/shard_map/ppermute | solution.py:805
  245.4 46.2 %collective-permute-start.27 = (bf16[256,1408]{1,0:T(8,128)(2,1)S(1)}, bf16[256,1408]{1,0:T(8,128)(2,1)S(1)}, u32[]{:S(2)}, u32[]{:S(2)}) collective-permute-start(bf16[256,1408]{1,0:T(8,128)(2,1)S(1)} %get-tuple-element.365.refs_1_), channel_id=1, source_target_pairs={{0,8},{4,12},{24,16},{28,20},{1,9},{5,13},{25,17},{29,21},{2,10},{... | collective-permute-start | bytes 2162696 | tf_op jit(solution)/shard_map/ppermute | solution.py:805
  246.7 27.6 %collective-permute-start.24 = (bf16[256,1408]{1,0:T(8,128)(2,1)S(1)}, bf16[256,1408]{1,0:T(8,128)(2,1)S(1)}, u32[]{:S(2)}, u32[]{:S(2)}) collective-permute-start(bf16[256,1408]{1,0:T(8,128)(2,1)S(1)} %get-tuple-element.359.refs_3_), channel_id=1, source_target_pairs={{8,16},{12,20},{16,8},{20,12},{0,0},{4,4},{24,24},{28,28},{9,17},{... | collective-permute-start | bytes 2162696 | tf_op jit(solution)/shard_map/ppermute | solution.py:805
  260.7 30.9 %collective-permute-start.28 = (bf16[256,1408]{1,0:T(8,128)(2,1)S(1)}, bf16[256,1408]{1,0:T(8,128)(2,1)S(1)}, u32[]{:S(2)}, u32[]{:S(2)}) collective-permute-start(bf16[256,1408]{1,0:T(8,128)(2,1)S(1)} %get-tuple-element.366.refs_3_), channel_id=1, source_target_pairs={{8,16},{12,20},{16,8},{20,12},{0,0},{4,4},{24,24},{28,28},{9,17},{... | collective-permute-start | bytes 2162696 | tf_op jit(solution)/shard_map/ppermute | solution.py:805
  275.7 29.6 %collective-permute-start.25 = (bf16[256,1408]{1,0:T(8,128)(2,1)}, bf16[256,1408]{1,0:T(8,128)(2,1)}, u32[]{:S(2)}, u32[]{:S(2)}) collective-permute-start(bf16[256,1408]{1,0:T(8,128)(2,1)} %get-tuple-element.361.refs_6_), channel_id=1, source_target_pairs={{0,8},{4,12},{8,0},{12,4},{16,24},{20,28},{24,16},{28,20},{1,9},{5... | collective-permute-start | bytes 2162696 | tf_op jit(solution)/shard_map/ppermute | solution.py:805
  278.0 27.3 %collective-permute-start.26 = (bf16[256,1408]{1,0:T(8,128)(2,1)}, bf16[256,1408]{1,0:T(8,128)(2,1)}, u32[]{:S(2)}, u32[]{:S(2)}) collective-permute-start(bf16[256,1408]{1,0:T(8,128)(2,1)} %get-tuple-element.362.refs_3_), channel_id=1, source_target_pairs={{8,16},{12,20},{16,8},{20,12},{0,0},{4,4},{24,24},{28,28},{9,17},{... | collective-permute-start | bytes 2162696 | tf_op jit(solution)/shard_map/ppermute | solution.py:805
  292.1 29.6 %collective-permute-start.30 = (bf16[256,1408]{1,0:T(8,128)(2,1)S(1)}, bf16[256,1408]{1,0:T(8,128)(2,1)}, u32[]{:S(2)}, u32[]{:S(2)}) collective-permute-start(bf16[256,1408]{1,0:T(8,128)(2,1)S(1)} %get-tuple-element.373.refs_6_), channel_id=1, source_target_pairs={{0,8},{4,12},{8,0},{12,4},{16,24},{20,28},{24,16},{28,20},{1,9},{5... | collective-permute-start | bytes 2162696 | tf_op jit(solution)/shard_map/ppermute | solution.py:805
  292.6 29.0 %collective-permute-start.31 = (bf16[256,1408]{1,0:T(8,128)(2,1)S(1)}, bf16[256,1408]{1,0:T(8,128)(2,1)}, u32[]{:S(2)}, u32[]{:S(2)}) collective-permute-start(bf16[256,1408]{1,0:T(8,128)(2,1)S(1)} %get-tuple-element.374.refs_3_), channel_id=1, source_target_pairs={{8,16},{12,20},{16,8},{20,12},{0,0},{4,4},{24,24},{28,28},{9,17},{... | collective-permute-start | bytes 2162696 | tf_op jit(solution)/shard_map/ppermute | solution.py:805
  304.1 165.3 %reduce-scatter.6.cloned.1.call-start = ((), (), s32[]{:S(2)}) async-start(), calls=%async_computation.5 | async-start | bytes 5242880 | tf_op jit(solution)/shard_map/reduce_scatter | solution.py:186
  311.5 31.2 %collective-permute-start.33 = (bf16[256,1408]{1,0:T(8,128)(2,1)S(1)}, bf16[256,1408]{1,0:T(8,128)(2,1)S(1)}, u32[]{:S(2)}, u32[]{:S(2)}) collective-permute-start(bf16[256,1408]{1,0:T(8,128)(2,1)S(1)} %get-tuple-element.384.refs_6_), channel_id=1, source_target_pairs={{0,8},{4,12},{8,0},{12,4},{16,24},{20,28},{24,16},{28,20},{1,9},{5... | collective-permute-start | bytes 2162696 | tf_op jit(solution)/shard_map/ppermute | solution.py:805
  313.8 28.9 %collective-permute-start.34 = (bf16[256,1408]{1,0:T(8,128)(2,1)S(1)}, bf16[256,1408]{1,0:T(8,128)(2,1)S(1)}, u32[]{:S(2)}, u32[]{:S(2)}) collective-permute-start(bf16[256,1408]{1,0:T(8,128)(2,1)S(1)} %get-tuple-element.385.refs_3_), channel_id=1, source_target_pairs={{8,16},{12,20},{16,8},{20,12},{0,0},{4,4},{24,24},{28,28},{9,17},{... | collective-permute-start | bytes 2162696 | tf_op jit(solution)/shard_map/ppermute | solution.py:805
  324.8 26.8 %collective-permute-start.38 = (bf16[256,1408]{1,0:T(8,128)(2,1)S(1)}, bf16[256,1408]{1,0:T(8,128)(2,1)S(1)}, u32[]{:S(2)}, u32[]{:S(2)}) collective-permute-start(bf16[256,1408]{1,0:T(8,128)(2,1)S(1)} %get-tuple-element.399.refs_6_), channel_id=1, source_target_pairs={{0,8},{4,12},{8,0},{12,4},{16,24},{20,28},{24,16},{28,20},{1,9},{5... | collective-permute-start | bytes 2162696 | tf_op jit(solution)/shard_map/ppermute | solution.py:805
  353.3 46.6 %collective-permute-start.43 = (bf16[256,1408]{1,0:T(8,128)(2,1)}, bf16[256,1408]{1,0:T(8,128)(2,1)}, u32[]{:S(2)}, u32[]{:S(2)}) collective-permute-start(bf16[256,1408]{1,0:T(8,128)(2,1)} %get-tuple-element.423.refs_1_), channel_id=1, source_target_pairs={{0,4},{4,0},{8,12},{12,8},{16,20},{20,16},{24,28},{28,24},{1,5},{5... | collective-permute-start | bytes 2162696 | tf_op jit(solution)/shard_map/ppermute | solution.py:115
  354.1 66.7 %collective-permute-start.46 = (bf16[256,1408]{1,0:T(8,128)(2,1)}, bf16[256,1408]{1,0:T(8,128)(2,1)}, u32[]{:S(2)}, u32[]{:S(2)}) collective-permute-start(bf16[256,1408]{1,0:T(8,128)(2,1)} %get-tuple-element.429.refs_6_), channel_id=1, source_target_pairs={{0,8},{4,12},{8,0},{12,4},{16,24},{20,28},{24,16},{28,20},{1,9},{5... | collective-permute-start | bytes 2162696 | tf_op jit(solution)/shard_map/ppermute | solution.py:805
  356.3 64.6 %collective-permute-start.47 = (bf16[256,1408]{1,0:T(8,128)(2,1)}, bf16[256,1408]{1,0:T(8,128)(2,1)}, u32[]{:S(2)}, u32[]{:S(2)}) collective-permute-start(bf16[256,1408]{1,0:T(8,128)(2,1)} %get-tuple-element.430.refs_3_), channel_id=1, source_target_pairs={{8,16},{12,20},{16,8},{20,12},{0,0},{4,4},{24,24},{28,28},{9,17},{... | collective-permute-start | bytes 2162696 | tf_op jit(solution)/shard_map/ppermute | solution.py:805
  363.1 31.4 %collective-permute-start.35 = (bf16[256,1408]{1,0:T(8,128)(2,1)}, bf16[256,1408]{1,0:T(8,128)(2,1)}, u32[]{:S(2)}, u32[]{:S(2)}) collective-permute-start(bf16[256,1408]{1,0:T(8,128)(2,1)} %get-tuple-element.387.refs_6_), channel_id=1, source_target_pairs={{0,8},{4,12},{8,0},{12,4},{16,24},{20,28},{24,16},{28,20},{1,9},{5... | collective-permute-start | bytes 2162696 | tf_op jit(solution)/shard_map/ppermute | solution.py:805
  363.2 153.1 %reduce-scatter.8.cloned.1.call-start = ((), (), s32[]{:S(2)}) async-start(), calls=%async_computation.7 | async-start | bytes 5242880 | tf_op jit(solution)/shard_map/reduce_scatter | solution.py:186
  364.1 30.5 %collective-permute-start.36 = (bf16[256,1408]{1,0:T(8,128)(2,1)}, bf16[256,1408]{1,0:T(8,128)(2,1)}, u32[]{:S(2)}, u32[]{:S(2)}) collective-permute-start(bf16[256,1408]{1,0:T(8,128)(2,1)} %get-tuple-element.388.refs_3_), channel_id=1, source_target_pairs={{8,16},{12,20},{16,8},{20,12},{0,0},{4,4},{24,24},{28,28},{9,17},{... | collective-permute-start | bytes 2162696 | tf_op jit(solution)/shard_map/ppermute | solution.py:805
  398.3 44.3 %collective-permute-start.41 = (bf16[256,1408]{1,0:T(8,128)(2,1)}, bf16[256,1408]{1,0:T(8,128)(2,1)}, u32[]{:S(2)}, u32[]{:S(2)}) collective-permute-start(bf16[256,1408]{1,0:T(8,128)(2,1)} %get-tuple-element.412.refs_5_), channel_id=1, source_target_pairs={{0,8},{4,12},{8,0},{12,4},{16,24},{20,28},{24,16},{28,20},{1,9},{5... | collective-permute-start | bytes 2162696 | tf_op jit(solution)/shard_map/ppermute | solution.py:805
  398.4 44.3 %collective-permute-start.42 = (bf16[256,1408]{1,0:T(8,128)(2,1)S(1)}, bf16[256,1408]{1,0:T(8,128)(2,1)}, u32[]{:S(2)}, u32[]{:S(2)}) collective-permute-start(bf16[256,1408]{1,0:T(8,128)(2,1)S(1)} %get-tuple-element.413.refs_3_), channel_id=1, source_target_pairs={{8,16},{12,20},{16,8},{20,12},{0,0},{4,4},{24,24},{28,28},{9,17},{... | collective-permute-start | bytes 2162696 | tf_op jit(solution)/shard_map/ppermute | solution.py:805
  399.9 27.7 %collective-permute-start.45 = (bf16[256,1408]{1,0:T(8,128)(2,1)S(1)}, bf16[256,1408]{1,0:T(8,128)(2,1)S(1)}, u32[]{:S(2)}, u32[]{:S(2)}) collective-permute-start(bf16[256,1408]{1,0:T(8,128)(2,1)S(1)} %get-tuple-element.428.refs_1_), channel_id=1, source_target_pairs={{0,4},{4,0},{8,12},{12,8},{16,20},{20,16},{24,28},{28,24},{1,5},{5... | collective-permute-start | bytes 2162696 | tf_op jit(solution)/shard_map/ppermute | solution.py:115
  424.5 28.3 %collective-permute-start.49 = (bf16[256,1408]{1,0:T(8,128)(2,1)}, bf16[256,1408]{1,0:T(8,128)(2,1)}, u32[]{:S(2)}, u32[]{:S(2)}) collective-permute-start(bf16[256,1408]{1,0:T(8,128)(2,1)} %get-tuple-element.438.refs_5_), channel_id=1, source_target_pairs={{0,8},{4,12},{8,0},{12,4},{16,24},{20,28},{24,16},{28,20},{1,9},{5... | collective-permute-start | bytes 2162696 | tf_op jit(solution)/shard_map/ppermute | solution.py:805
  427.5 31.0 %collective-permute-start.50 = (bf16[256,1408]{1,0:T(8,128)(2,1)}, bf16[256,1408]{1,0:T(8,128)(2,1)S(1)}, u32[]{:S(2)}, u32[]{:S(2)}) collective-permute-start(bf16[256,1408]{1,0:T(8,128)(2,1)} %get-tuple-element.439.refs_3_), channel_id=1, source_target_pairs={{8,16},{12,20},{16,8},{20,12},{0,0},{4,4},{24,24},{28,28},{9,17},{... | collective-permute-start | bytes 2162696 | tf_op jit(solution)/shard_map/ppermute | solution.py:805
  446.9 27.1 %collective-permute-start.53 = (bf16[256,1408]{1,0:T(8,128)(2,1)}, bf16[256,1408]{1,0:T(8,128)(2,1)S(1)}, u32[]{:S(2)}, u32[]{:S(2)}) collective-permute-start(bf16[256,1408]{1,0:T(8,128)(2,1)} %get-tuple-element.450.refs_3_), channel_id=1, source_target_pairs={{8,16},{12,20},{16,8},{20,12},{0,0},{4,4},{24,24},{28,28},{9,17},{... | collective-permute-start | bytes 2162696 | tf_op jit(solution)/shard_map/ppermute | solution.py:805
  448.6 27.5 %collective-permute-start.54 = (bf16[256,1408]{1,0:T(8,128)(2,1)}, bf16[256,1408]{1,0:T(8,128)(2,1)}, u32[]{:S(2)}, u32[]{:S(2)}) collective-permute-start(bf16[256,1408]{1,0:T(8,128)(2,1)} %get-tuple-element.451.refs_5_), channel_id=1, source_target_pairs={{8,0},{12,4},{16,24},{20,28},{9,1},{13,5},{17,25},{21,29},{10,2},{... | collective-permute-start | bytes 2162696 | tf_op jit(solution)/shard_map/ppermute | solution.py:805
  458.6 44.2 %collective-permute-start.56 = (bf16[256,1536]{1,0:T(8,128)(2,1)S(1)}, bf16[256,1536]{1,0:T(8,128)(2,1)}, u32[]{:S(2)}, u32[]{:S(2)}) collective-permute-start(bf16[256,1536]{1,0:T(8,128)(2,1)S(1)} %get-tuple-element.454.refs_1_), channel_id=1, source_target_pairs={{0,8},{4,12},{24,16},{28,20},{1,9},{5,13},{25,17},{29,21},{2,10},{... | collective-permute-start | bytes 2359304 | tf_op jit(solution)/shard_map/ppermute | solution.py:805
  465.6 66.6 %collective-permute-start.60 = (bf16[256,1536]{1,0:T(8,128)(2,1)}, bf16[256,1536]{1,0:T(8,128)(2,1)}, u32[]{:S(2)}, u32[]{:S(2)}) collective-permute-start(bf16[256,1536]{1,0:T(8,128)(2,1)} %get-tuple-element.465.refs_1_), channel_id=1, source_target_pairs={{0,8},{4,12},{24,16},{28,20},{1,9},{5,13},{25,17},{29,21},{2,10},{... | collective-permute-start | bytes 2359304 | tf_op jit(solution)/shard_map/ppermute | solution.py:805
  474.8 49.9 %collective-permute-start.65 = (bf16[256,1536]{1,0:T(8,128)(2,1)S(1)}, bf16[256,1536]{1,0:T(8,128)(2,1)S(1)}, u32[]{:S(2)}, u32[]{:S(2)}) collective-permute-start(bf16[256,1536]{1,0:T(8,128)(2,1)S(1)} %get-tuple-element.471.refs_1_), channel_id=1, source_target_pairs={{0,8},{4,12},{24,16},{28,20},{1,9},{5,13},{25,17},{29,21},{2,10},{... | collective-permute-start | bytes 2359304 | tf_op jit(solution)/shard_map/ppermute | solution.py:805
  505.9 30.1 %collective-permute-start.62 = (bf16[256,1408]{1,0:T(8,128)(2,1)}, bf16[256,1408]{1,0:T(8,128)(2,1)}, u32[]{:S(2)}, u32[]{:S(2)}) collective-permute-start(bf16[256,1408]{1,0:T(8,128)(2,1)} %get-tuple-element.467.refs_5_), channel_id=1, source_target_pairs={{8,0},{12,4},{16,24},{20,28},{9,1},{13,5},{17,25},{21,29},{10,2},{... | collective-permute-start | bytes 2162696 | tf_op jit(solution)/shard_map/ppermute | solution.py:805
  531.5 27.7 %collective-permute-start.74 = (bf16[256,1536]{1,0:T(8,128)(2,1)S(1)}, bf16[256,1536]{1,0:T(8,128)(2,1)S(1)}, u32[]{:S(2)}, u32[]{:S(2)}) collective-permute-start(bf16[256,1536]{1,0:T(8,128)(2,1)S(1)} %get-tuple-element.488.refs_1_), channel_id=1, source_target_pairs={{8,16},{12,20},{16,8},{20,12},{0,0},{4,4},{24,24},{28,28},{9,17},{... | collective-permute-start | bytes 2359304 | tf_op jit(solution)/shard_map/ppermute | solution.py:805
  532.2 33.9 %collective-permute-start.75 = (bf16[256,1536]{1,0:T(8,128)(2,1)S(1)}, bf16[256,1536]{1,0:T(8,128)(2,1)S(1)}, u32[]{:S(2)}, u32[]{:S(2)}) collective-permute-start(bf16[256,1536]{1,0:T(8,128)(2,1)S(1)} %get-tuple-element.489.refs_3_), channel_id=1, source_target_pairs={{8,0},{12,4},{16,24},{20,28},{9,1},{13,5},{17,25},{21,29},{10,2},{... | collective-permute-start | bytes 2359304 | tf_op jit(solution)/shard_map/ppermute | solution.py:805
  543.8 41.9 %collective-permute-start.68 = (bf16[256,1536]{1,0:T(8,128)(2,1)S(1)}, bf16[256,1536]{1,0:T(8,128)(2,1)S(1)}, u32[]{:S(2)}, u32[]{:S(2)}) collective-permute-start(bf16[256,1536]{1,0:T(8,128)(2,1)S(1)} %get-tuple-element.479.refs_1_), channel_id=1, source_target_pairs={{8,16},{12,20},{16,8},{20,12},{0,0},{4,4},{24,24},{28,28},{9,17},{... | collective-permute-start | bytes 2359304 | tf_op jit(solution)/shard_map/ppermute | solution.py:805
  557.9 27.8 %collective-permute-start.69 = (bf16[256,1536]{1,0:T(8,128)(2,1)S(1)}, bf16[256,1536]{1,0:T(8,128)(2,1)S(1)}, u32[]{:S(2)}, u32[]{:S(2)}) collective-permute-start(bf16[256,1536]{1,0:T(8,128)(2,1)S(1)} %get-tuple-element.480.refs_3_), channel_id=1, source_target_pairs={{8,0},{12,4},{16,24},{20,28},{9,1},{13,5},{17,25},{21,29},{10,2},{... | collective-permute-start | bytes 2359304 | tf_op jit(solution)/shard_map/ppermute | solution.py:805
  586.0 36.3 %collective-permute-start.76 = (bf16[256,1536]{1,0:T(8,128)(2,1)S(1)}, bf16[256,1536]{1,0:T(8,128)(2,1)S(1)}, u32[]{:S(2)}, u32[]{:S(2)}) collective-permute-start(bf16[256,1536]{1,0:T(8,128)(2,1)S(1)} %get-tuple-element.495.refs_1_), channel_id=1, source_target_pairs={{8,0},{12,4},{16,24},{20,28},{9,1},{13,5},{17,25},{21,29},{10,2},{... | collective-permute-start | bytes 2359304 | tf_op jit(solution)/shard_map/ppermute | solution.py:805
  (287 other events, 2296.6 us)
Sparse Core Ops, SparseCore 0:
  56.2 76.3 all-gather.2
  244.1 51.7 reduce-scatter.3
  304.3 52.6 all-gather.4
  363.3 52.3 reduce-scatter.5
  427.7 51.0 reduce-scatter.7

commit v3 on v2

--- a/solution.py
+++ b/solution.py
@@ -15,7 +15,7 @@
 VMEM = pl.BlockSpec(memory_space=pltpu.VMEM)
 SMEM = pl.BlockSpec(memory_space=pltpu.SMEM)
 HBM = pl.BlockSpec(memory_space=pltpu.HBM)
-PER_US = 1150000000.0
+STEP_FLOPS, STEP_BYTES = 20_000_000_000, 120_000_000
 MIB = 1024 * 1024
 LIMIT = 28
 
@@ -80,10 +80,12 @@
         ins=None,
         outspecs=None,
         reuse=(),
-        us=1.5,
+        wait=(),
+        weight=1,
     ):
         ahead, total = len(prefetch) + len(smem), len(prefetch) + len(smem) + len(operands)
-        skip = len(self.last) + len(reuse)
+        last = (*self.last, *wait)
+        skip = len(last) + len(reuse)
 
         def kernel(*refs):
             results = refs[total + skip :]
@@ -101,12 +103,12 @@
                 out_specs=(*(outspecs or [VMEM] * len(outs)), HBM),
                 scratch_shapes=scratch,
             ),
-            input_output_aliases={total + len(self.last) + n: n for n in range(len(reuse))},
+            input_output_aliases={total + len(last) + n: n for n in range(len(reuse))},
             cost_estimate=pl.CostEstimate(
-                flops=int(2e10), bytes_accessed=int(1.2e8), transcendentals=0
+                flops=weight * STEP_FLOPS, bytes_accessed=weight * STEP_BYTES, transcendentals=0
             ),
             compiler_params=pltpu.CompilerParams(vmem_limit_bytes=LIMIT * MIB),
-        )(*prefetch, *smem, *operands, *map(in_hbm, (*self.last, *reuse)))
+        )(*prefetch, *smem, *operands, *map(in_hbm, (*last, *reuse)))
         self.last = (got[-1],)
         return got[:-1]
 
@@ -119,7 +121,7 @@
     return [pl.BlockSpec((a.shape[0] // steps, a.shape[1]), lambda i: (i, 0)) for a in arrays]
 
 
-def pointwise(order, body, operands, outs, smem=(), steps=1, us=1.5):
+def pointwise(order, body, operands, outs, smem=(), steps=1, wait=()):
     return order.call(
         body,
         operands,
@@ -128,7 +130,7 @@
         grid=(steps,),
         ins=row_blocks(operands, steps),
         outspecs=row_blocks(outs, steps),
-        us=us,
+        wait=wait,
     )
 
 
@@ -270,7 +272,8 @@
         smem=(scal,),
         grid=plan.grid,
         ins=[plan.whole, plan.whole, plan.row],
-        outspecs=[plan.whole, *plan.lists(1)], us=2.5)
+        outspecs=[plan.whole, *plan.lists(1)],
+    )
     return outs, grad
 
 
@@ -312,7 +315,7 @@
     if many:
         outs += [spec((total, kv))] * 2
         operands += [k for k, _ in earlier] + [v for _, v in earlier]
-    return order.call(body, operands, outs, smem=(bases,), us=2.5)
+    return order.call(body, operands, outs, smem=(bases,))
 
 
 def attend(order, queries, k_all, v_all, w_out, bases, first):
@@ -362,7 +365,8 @@
         body,
         (*queries, k_all, v_all, w_out),
         [spec((piece, width))] * 2 + [spec((piece, heads), F32)] * 2 + [spec((piece, wide))] * 2,
-        smem=(bases,), us=3.0)
+        smem=(bases,),
+    )
 
 
 def second_norm(order, x, sums, gain, scal, pieces):
@@ -388,7 +392,8 @@
         smem=(scal,),
         grid=plan.grid,
         ins=[plan.whole, plan.row, *plan.lists(count)],
-        outspecs=[plan.whole, *plan.lists(1)], us=2.4)
+        outspecs=[plan.whole, *plan.lists(1)],
+    )
     return got[0], list(got[1:])
 
 
@@ -411,7 +416,8 @@
         [spec((rows, width))],
         grid=(pl.cdiv(width, step),),
         ins=[VMEM, pl.BlockSpec((step, depth), lambda i: (i, 0))],
-        outspecs=[pl.BlockSpec((rows, step), lambda i: (0, i))], us=7.3)[0]
+        outspecs=[pl.BlockSpec((rows, step), lambda i: (0, i))],
+    )[0]
 
 
 def feed_forward(order, n_pieces, dhid, w_gate, w_up, bases, which, step=512):
@@ -442,7 +448,8 @@
         prefetch=(bases,),
         grid=(pl.cdiv(width, step),),
         ins=[VMEM, VMEM, rows_of(which[0]), rows_of(which[1]), across, across],
-        outspecs=[out] * 3, us=7.3)
+        outspecs=[out] * 3,
+    )
 
 
 def back_two(order, dgates, dups, w_gate, w_up, bases, piece, step=256):
@@ -463,7 +470,9 @@
         smem=(bases,),
         grid=(depth // step,),
         ins=[VMEM] * (2 * many) + [weight, weight],
-        outspecs=[pl.BlockSpec((rows, step), lambda i: (0, i))], us=16.0)[0]
+        outspecs=[pl.BlockSpec((rows, step), lambda i: (0, i))],
+        weight=1,
+    )[0]
 
 
 def down_rows(order, hiddens, w_down, bases, piece, step=512):
@@ -482,7 +491,8 @@
         smem=(bases,),
         grid=(depth // step,),
         ins=[VMEM] * many + [pl.BlockSpec((width, step), lambda i: (0, i))],
-        outspecs=[pl.BlockSpec((rows, step), lambda i: (0, i))], us=8.5)[0]
+        outspecs=[pl.BlockSpec((rows, step), lambda i: (0, i))],
+    )[0]
 
 
 def norm_back(h, gain, grad):
@@ -515,7 +525,8 @@
         smem=(scal,),
         grid=(steps,),
         ins=[block, block, block, row],
-        outspecs=[block, row, block], us=2.6)
+        outspecs=[block, row, block],
+    )
 
 
 def first_back(order, x, dh, total, gain, steps=2):
@@ -540,7 +551,8 @@
         [spec((rows, width), F32), spec((1, width), F32)],
         grid=(steps,),
         ins=[block, block, block, row],
-        outspecs=[block, row], us=2.8)
+        outspecs=[block, row],
+    )
 
 
 def mix(order, h_one, total, scal):
@@ -563,7 +575,8 @@
         [spec((rows, width))],
         grid=(steps,),
         ins=[pl.BlockSpec((rows // steps, depth), lambda i: (i, 0)), VMEM],
-        outspecs=[pl.BlockSpec((rows // steps, width), lambda i: (i, 0))], us=3.0)[0]
+        outspecs=[pl.BlockSpec((rows // steps, width), lambda i: (i, 0))],
+    )[0]
 
 
 def attend_back(order, qs, k_all, v_all, grads, lses, tables, bases):
@@ -635,7 +648,8 @@
             pltpu.VMEM((total, width), F32),
             pltpu.VMEM((total, kv_width), F32),
             pltpu.VMEM((total, kv_width), F32),
-        ], us=13.8)[0]
+        ],
+    )[0]
 
 
 def back_one(order, grads, weights, bases, piece, step=512):
@@ -658,31 +672,37 @@
         smem=(bases,),
         grid=(depth // step,),
         ins=[VMEM] + [pl.BlockSpec((step, w.shape[1]), lambda i: (i, 0)) for w in weights],
-        outspecs=[pl.BlockSpec((rows, step), lambda i: (0, i))], us=6.0)[0]
+        outspecs=[pl.BlockSpec((rows, step), lambda i: (0, i))],
+    )[0]
 
 
 class Job:
-    def __init__(self, groups, outs, half=256):
-        self.groups, self.outs, self.half = groups, outs, half
+    def __init__(self, groups, outs, halves):
+        self.groups, self.outs = groups, outs
         self.pairs = [pair for group in groups for pair in group]
         self.rows = self.pairs[0][0][0].shape[1]
-        self.chunks = self.rows // (2 * half)
-        self.widths = [sum(right[0].shape[1] for _, right, _ in group) for group in groups]
+        self.chunks, at = [], 0
+        for half in halves:
+            self.chunks.append((at, half))
+            at += 2 * half
+        self.widths = [sum(n for _, right, _ in group for _, _, n in right[:1]) for group in groups]
         self.results = [() for _ in groups]
         self.got = {}
 
 
 def product(order, job, pick, chunks, bases, piece, add_to=None):
-    first, count, half, many = chunks[0], len(chunks), job.half, len(job.groups)
+    start, half = job.chunks[chunks[0]]
+    first, count, many = start // half, len(chunks), len(job.groups)
     width = job.widths[0]
     lefts, places = [], []
     for left, _, _ in job.pairs:
         if not any(left is known for known, _ in places):
             places.append((left, len(lefts)))
             lefts += left
-    rights = [block for _, right, _ in job.pairs for block in right]
+    rights = [window for _, right, _ in job.pairs for window in right]
     total = sum(p.shape[0] for p in job.pairs[0][0])
     extra = 0 if add_to is None else 1
+    got_array, got_at = add_to if extra else (None, 0)
 
     def body(pick_ref, base, *refs):
         left_refs, refs = refs[: len(lefts)], refs[len(lefts) :]
@@ -693,7 +713,7 @@
         def _():
             at, n = 0, 0
             for _, right, placed in job.pairs:
-                wide = right[0].shape[1]
+                wide = right[0][2]
                 value = stack(right_refs[n : n + len(right)])
                 here = slice(at, at + wide)
                 if placed:
@@ -710,7 +730,7 @@
         for g, group in enumerate(job.groups):
             put = 0
             for left, right, _ in group:
-                wide = right[0].shape[1]
+                wide = right[0][2]
                 start = next(s for known, s in places if known is left)
                 value = tn(stacks[start], whole[:, at : at + wide])
                 here = slice(put, put + wide)
@@ -734,47 +754,57 @@
         outs, outspecs = [spec((count * many * half, width))], [block]
     return order.call(
         body,
-        (*lefts, *rights, *([add_to] if extra else [])),
+        (*lefts, *[array for array, _, _ in rights], *([got_array] if extra else [])),
         outs,
         prefetch=(pick, bases),
         grid=(count,),
         ins=[
-            pl.BlockSpec((p.shape[0], half), lambda i, pick_ref, base: (0, 2 * (first + i) + pick_ref[0]))
+            pl.BlockSpec((p.shape[0], half), lambda i, pick_ref, base: (0, first + 2 * i + pick_ref[0]))
             for p in lefts
         ]
-        + [VMEM] * len(rights)
-        + [block] * extra,
+        + [
+            pl.BlockSpec((array.shape[0], n), lambda i, pick_ref, base, at=at // n: (0, at))
+            for array, at, n in rights
+        ]
+        + [
+            pl.BlockSpec((many * half, width), lambda i, pick_ref, base: (i + got_at, 0))
+        ]
+        * extra,
         outspecs=outspecs,
-        scratch=[pltpu.VMEM((total, sum(job.widths)), BF16)], us=0.5 + count * many * half * width / 2.4e5)
+        scratch=[pltpu.VMEM((total, sum(job.widths)), BF16)],
+    )
 
 
 def lay(order, job, group, core, chunk, mine, other):
-    block = job.half
+    start, half = job.chunks[chunk]
 
     def body(core_ref, mine_ref, other_ref, *outs):
         for n, ref in ((0, mine_ref), (1, other_ref)):
 
             @pl.when(pl.program_id(0) == n)
             def _():
-                for (at, width, turned), out in zip(job.outs[group], outs):
+                for (at, width, turned, _, _), out in zip(job.outs[group], outs):
                     value = ref[:, at : at + width].astype(F32)
                     out[...] = value.T if turned else value
 
-    def place(n, core_ref):
-        return 2 * chunk + (core_ref[0] ^ n)
-
-    def across(n, core_ref):
-        return (place(n, core_ref), 0)
-
-    def down(n, core_ref):
-        return (0, place(n, core_ref))
-
     shapes, specs = [], []
-    for _, width, turned in job.outs[group]:
-        shapes.append(pltpu.HBM((width, job.rows) if turned else (job.rows, width), F32))
-        specs.append(
-            pl.BlockSpec((width, block), down) if turned else pl.BlockSpec((block, width), across)
-        )
+    for _, width, turned, whole, place in job.outs[group]:
+        if turned:
+            shapes.append(pltpu.HBM((whole, job.rows), F32))
+            specs.append(
+                pl.BlockSpec(
+                    (width, half),
+                    lambda n, core_ref, p=place: (p, start // half + (core_ref[0] ^ n)),
+                )
+            )
+        else:
+            shapes.append(pltpu.HBM((job.rows, whole), F32))
+            specs.append(
+                pl.BlockSpec(
+                    (half, width),
+                    lambda n, core_ref, p=place: (start // half + (core_ref[0] ^ n), p),
+                )
+            )
     job.results[group] = order.call(
         body,
         (mine, other),
@@ -782,7 +812,8 @@
         prefetch=(core,),
         grid=(2,),
         outspecs=specs,
-        reuse=job.results[group], us=2.5)
+        reuse=job.results[group],
+    )
 
 
 class Line:
@@ -806,10 +837,12 @@
 
     def send(self, job, chunks):
         part = product(self.order, job, self.other, chunks, self.bases, self.piece)[0]
-        job.got[tuple(chunks)] = swap(part, "dp", self.size, 1)
+        got = swap(part, "dp", self.size, 1)
+        for n, k in enumerate(chunks):
+            job.got[k] = (got, n)
 
     def enter(self, job, chunks):
-        got = job.got[tuple(chunks)]
+        got = job.got[chunks[0]]
         parts = iter(product(self.order, job, self.mine, chunks, self.bases, self.piece, got))
         for k in chunks:
             for group in range(len(job.groups)):
@@ -849,7 +882,8 @@
             if out:
                 results.pop(0)[...] = jnp.where(middle, refs.pop(0)[...], refs.pop(0)[...])
 
-        got = list(pointwise(self.order, body, operands, outs, smem=(self.middle,), us=2.5))
+        wait = [self.done[c - 1]] if c - 1 in self.done else []
+        got = list(pointwise(self.order, body, operands, outs, smem=(self.middle,), wait=wait))
         if here:
             self.half[k] = got.pop(0)
         if back:
@@ -857,7 +891,7 @@
         if out:
             self.final[c] = got.pop(0)
         if here:
-            self.mids[k] = self.hop(self.half[k], [(1, 2), (2, 1), (0, 0), (3, 3)])
+            self.mids[k] = self.hop(self.half[k], [(1, 2), (2, 1)])
         if merged:
             both = self.hop(self.whole[b], [(0, 1), (1, 0), (2, 3), (3, 2)])
             self.ends[b] = self.fold[ahead] = both
@@ -879,7 +913,7 @@
     def __init__(self, order, value, mesh_shape):
         self.order, self.value = order, value
         self.steps = []
-        for axis in ("dp", "tensor"):
+        for axis in ("tensor", "dp"):
             size, bit = mesh_shape[axis], 1
             if size & (size - 1):
                 self.steps.append((axis, size, None))
@@ -945,8 +979,8 @@
 
     if square:
         n_one = rows.gather_first(n_own)
-        n_one += rows.gather_second(n_own)
         project_group(rows.groups[0], n_one)
+        n_one += rows.gather_second(order.tie(*n_own))
         n_one += rows.gather_third(*order.tie(n_one[2], n_one[3]))
         project_group(rows.groups[1], n_one)
         project_group(rows.groups[2], n_one)
@@ -1033,30 +1067,44 @@
         return rows.scatter_all(down_rows(order, hidden, w_down, bases, rows.piece))
 
     ff, width, kv = w_gate.shape[1], w_query.shape[1], w_key.shape[1]
-    late_outs = [
-        (0, width, True),
-        (width, width, False),
-        (2 * width, kv, False),
-        (2 * width + kv, kv, False),
-    ]
-    down = Job([[([grad_m], hidden, True)]], [[(0, ff, True)]])
+    def whole_of(arrays):
+        return [(array, 0, array.shape[1]) for array in arrays]
+
+    ff_out = [[(0, ff, False, ff, 0)]]
+    down = Job([[([grad_m], whole_of(hidden), True)]], [[(0, ff, True, ff, 0)]], [256] * 4)
     wide = Job(
-        [[(n_two, dgate, False)], [(n_two, dup, False)]], [[(0, ff, False)], [(0, ff, False)]]
+        [[(n_two, whole_of(dgate), False)], [(n_two, whole_of(dup), False)]],
+        ff_out * 2,
+        [256] * 4,
     )
 
-    def late_job(grad_a, gqkv):
-        every_attn = [attn[i] for i in every]
-        return Job([[([grad_a], every_attn, True), (n_one, [gqkv], False)]], [late_outs])
+    def late_jobs(grad_a, gqkv):
+        total = gqkv.shape[1]
+        rest = HD if square else 0
+        right = [(gqkv, 0, total - rest)]
+        outs = [
+            (0, width, True, width, 0),
+            (width, width, False, width, 0),
+            (2 * width, kv, False, kv, 0),
+            (2 * width + kv, kv - rest, False, kv, 0),
+        ]
+        pairs = [([grad_a], whole_of([attn[i] for i in every]), True), (n_one, right, False)]
+        jobs = [Job([pairs], [outs], [256, 256, 256, 128, 128])]
+        if rest:
+            pairs = [(n_one, [(gqkv, total - rest, rest)], False)]
+            jobs.append(Job([pairs], [[(0, rest, False, kv, kv // rest - 1)]], [1024]))
+        return jobs
 
     if square:
-        line.count = 16
+        line.count = 18
         line.send(down, [0, 1])
         line.send(down, [2, 3])
-        line.enter(down, [0, 1])
+        line.enter(down, [0])
         two_total = back_two_all()
+        line.enter(down, [1])
+        line.send(wide, [0, 1])
         line.tick(0)
         line.enter(down, [2, 3])
-        line.send(wide, [0, 1])
         line.tick(1)
         line.enter(wide, [0, 1])
         line.tick(2)
@@ -1067,57 +1115,76 @@
         line.tick(4)
         line.enter(wide, [2, 3])
         line.tick(5)
-        line.lay(0)
         mix_total = down_all()
         line.tick(6)
-        line.lay(1)
+        line.lay(0)
         line.tick(7)
-        line.lay(2)
         gqkv = attend_back_all(grad_a)
-        late = late_job(grad_a, gqkv)
+        late, late_rest = late_jobs(grad_a, gqkv)
         line.tick(8)
-        line.lay(3)
-        line.send(late, [0, 1, 2, 3])
+        line.send(late, [0, 1, 2])
         one_total = back_one_all(gqkv)
         line.tick(9)
+        line.enter(late, [0, 1, 2])
+        line.tick(10)
+        line.send(late, [3, 4])
+        line.send(late_rest, [0])
+        line.tick(11)
+        line.lay(1)
+        line.enter(late, [3, 4])
+        line.enter(late_rest, [0])
+        line.tick(12)
+        line.lay(2)
+        line.lay(3)
+        line.tick(13)
         line.lay(4)
-        line.enter(late, [0, 1, 2, 3])
-        line.tick(10)
         line.lay(5)
-        line.tick(11)
-        line.lay(6)
-        mixed = mix(order, h_one, mix_total, scal)
-        line.tick(12)
-        line.lay(7)
-        line.tick(13)
-        line.lay(8)
-        input_grad, gain_one_sum = first_back(order, x, dh, one_total, gain_one)
-        gains = SmallSum(order, jnp.concatenate([gain_one_sum, gain_two_sum]), mesh_shape)
+        laid = 6
         for k in range(14, line.count + 2 * line.LAG):
             line.tick(k)
-            line.lay(k - 5)
-            gains.step()
+            if k == 14:
+                mixed = mix(order, h_one, mix_total, scal)
+                input_grad, gain_one_sum = first_back(order, x, dh, one_total, gain_one)
+                gains = SmallSum(
+                    order, jnp.concatenate([gain_one_sum, gain_two_sum]), mesh_shape
+                )
+            while laid <= min(k - 5, laid + 2) and laid < 6 + 2 * (k - 13):
+                line.lay(laid)
+                laid += 1
+            if k in (15, 16, 17, 18, 20):
+                gains.step()
+        while laid < line.count - 1:
+            line.lay(laid)
+            laid += 1
+        late_rest.results[0] = (late.results[0][3],)
         line.lay(line.count - 1)
+        gain_sums = gains.value
     else:
         dh, gain_two_sum, grad_a_own = second_back_all(back_two_all())
         grad_a = rows.gather_all(grad_a_own)
         gqkv = attend_back_all(grad_a)
-        late = late_job(grad_a, gqkv)
+        (late,) = late_jobs(grad_a, gqkv)
         mixed = mix(order, h_one, down_all(), scal)
         input_grad, gain_one_sum = first_back(order, x, dh, back_one_all(gqkv), gain_one)
         gains = SmallSum(order, jnp.concatenate([gain_one_sum, gain_two_sum]), mesh_shape)
+        while gains.steps:
+            gains.step()
+        gain_sums = gains.value
         for job in (down, wide, late):
             for n, group in enumerate(job.groups):
-                parts = [tn(jnp.concatenate(a), jnp.concatenate(b)) for a, b, _ in group]
+                parts = [
+                    tn(jnp.concatenate(a), jnp.concatenate([array for array, _, _ in b]))
+                    for a, b, _ in group
+                ]
                 whole = jnp.concatenate(parts, axis=1).astype(BF16)
                 whole = lax.psum(whole, "dp").astype(F32)
                 job.results[n] = [
                     whole[:, at : at + size].T if turned else whole[:, at : at + size]
-                    for at, size, turned in job.outs[n]
+                    for at, size, turned, _, _ in job.outs[n]
                 ]
-    while gains.steps:
-        gains.step()
     grad_output, grad_query, grad_key, grad_value = late.results[0]
+    if square:
+        grad_value = late_rest.results[0][0]
     return (
         mixed[None],
         input_grad[None],
@@ -1128,8 +1195,8 @@
         wide.results[0][0],
         wide.results[1][0],
         down.results[0][0],
-        gains.value[0],
-        gains.value[1],
+        gain_sums[0],
+        gain_sums[1],
     )
 
 

time: 647 us -> 613 us (0.947)
  waiting for transfers between devices: 152 us -> 110 us
  Pallas kernels: 242 us -> 256 us
  starting transfers between devices: 132 us -> 125 us
    ppermute x44 -> x48, waiting for transfers between devices: 79.2 us -> 54.2 us  [swap(): return lax.ppermute(value, axis, [(i, i ^ bit) for i in range(size)])]
    ppermute x40 -> x43, waiting for transfers between devices: 72.6 us -> 49 us  [hop(): return lax.ppermute(value, 'dp', pairs)]
    pallas_call x76 -> x85, Pallas kernels: 242 us -> 256 us  [call(): pl.pallas_call(kernel, out_shape=(*outs, pltpu.HBM((8, 128), F32)), grid_...]
    ppermute x40 -> x43, starting transfers between devices: 84.9 us -> 76.5 us  [hop(): return lax.ppermute(value, 'dp', pairs)]
    unnamed x492 -> x510, local copies, waits for them, and re-layouts: 87.1 us -> 89 us
    ppermute x44 -> x48, starting transfers between devices: 47.1 us -> 48.5 us  [swap(): return lax.ppermute(value, axis, [(i, i ^ bit) for i in range(size)])]
  transfers between devices with their start and end apart: 89 -> 96, of which waited for: 19 -> 20; matrix products, arithmetic and copies ran while one was open for 0% -> 0% of each run, Pallas kernels for 34% -> 40%
where the time goes in v3:
time: 613 us; the launch traced here: 602 us
  Pallas kernels  256 us (42%)
  starting transfers between devices  125 us (20%)
  waiting for transfers between devices  110 us (18%)
  local copies, waits for them, and re-layouts  89.7 us (15%)
  between operations  18.1 us (3%)
    pallas_call x85, Pallas kernels, call(): pl.pallas_call(kernel, out_shape=(*outs, pltpu.HBM((8, 128), F32)), grid_...  256 us
    unnamed x510, local copies, waits for them, and re-layouts  89 us
    ppermute x43, starting transfers between devices, hop(): return lax.ppermute(value, 'dp', pairs)  76.5 us
    ppermute x48, waiting for transfers between devices, swap(): return lax.ppermute(value, axis, [(i, i ^ bit) for i in range(size)])  54.2 us
    ppermute x43, waiting for transfers between devices, hop(): return lax.ppermute(value, 'dp', pairs)  49 us
    ppermute x48, starting transfers between devices, swap(): return lax.ppermute(value, axis, [(i, i ^ bit) for i in range(size)])  48.5 us
  transfers between devices with their start and end apart: 96, of which 20 were waited for; matrix products, arithmetic and copies ran while one was open for 0% of the time, Pallas kernels for 40%

profile of v3, /device:TPU:1, one launch (start us, length us, event | category | flops | bytes accessed | tf_op | source)
XLA Modules:
  0.0 601.7 jit_solution(10089151024843609041)
XLA Ops:
  47.4 4.8 collective-permute-done.2.refs_1_.refs_9_.refs_8_
  59.7 3.4 shard_map.225
  63.2 3.7 shard_map.226
  73.0 3.3 shard_map.228
  79.2 4.0 collective-permute-done.7.refs_1_
  87.7 17.8 %collective-permute-done.11.refs_8_ = bf16[128,2048]{1,0:T(8,128)(2,1)S(1)} collective-permute-done((bf16[128,2048]{1,0:T(8,128)(2,1)S(1)}, bf16[128,2048]{1,0:T(8,128)(2,1)S(1)}, u32[]{:S(2)}, u32[]{:S(2)}) %collective-permute-start.11) | collective-permute-done | bytes 524320 | tf_op jit(solution)/shard_map/ppermute | solution.py:117
  105.5 22.5 %collective-permute-done.10.refs_7_ = bf16[128,2048]{1,0:T(8,128)(2,1)S(1)} collective-permute-done((bf16[128,2048]{1,0:T(8,128)(2,1)S(1)}, bf16[128,2048]{1,0:T(8,128)(2,1)S(1)}, u32[]{:S(2)}, u32[]{:S(2)}) %collective-permute-start.10) | collective-permute-done | bytes 524320 | tf_op jit(solution)/shard_map/ppermute | solution.py:117
  138.7 7.4 %shard_map.233 = (bf16[1024,1408]{1,0:T(8,128)(2,1)S(1)}, f32[8,128]{1,0:T(8,128)}) custom-call(bf16[1024,2048]{1,0:T(8,128)(2,1)S(1)} %copy-done.9, bf16[1408,2048]{1,0:T(8,128)(2,1)S(1)} %copy-done.5, f32[8,128]{1,0:T(8,128)} %get-tuple-element.351.refs_2_), custom_call_target="tpu_custom_call" | custom-call | flops 20000000000 | bytes 120000000 | tf_op jit(solution)/shard_map/pallas_call | solution.py:94
  151.4 6.6 %shard_map.234 = (bf16[256,1408]{1,0:T(8,128)(2,1)S(1)}, bf16[256,1408]{1,0:T(8,128)(2,1)S(1)}, bf16[256,1408]{1,0:T(8,128)(2,1)S(1)}, f32[8,128]{1,0:T(8,128)}) custom-call(s32[8]{0:T(128)S(1)} %stack.40.refs_0_.refs_1_, bf16[128,2048]{1,0:T(8,128)(2,1)S(1)} %get-tuple-element.347.refs_1_.refs_2_, bf16[128,2048]{1,0:T(8,128)(2,1)S(1)} %get-tuple-element.348.refs_2_.refs_3_, ...), custom_call_target="tpu_custom_call" | custom-call | flops 20000000000 | bytes 120000000 | tf_op jit(solution)/shard_map/pallas_call | solution.py:94
  159.6 7.1 %shard_map.235 = (bf16[256,1408]{1,0:T(8,128)(2,1)S(1)}, bf16[256,1408]{1,0:T(8,128)(2,1)S(1)}, bf16[256,1408]{1,0:T(8,128)(2,1)S(1)}, f32[8,128]{1,0:T(8,128)}) custom-call(s32[8]{0:T(128)S(1)} %stack.40.refs_0_.refs_1_, bf16[128,2048]{1,0:T(8,128)(2,1)} %collective-permute-done.12.refs_1_.refs_4_, ...), custom_call_target="tpu_custom_call" | custom-call | flops 20000000000 | bytes 120000000 | tf_op jit(solution)/shard_map/pallas_call | solution.py:94
  166.8 7.2 %shard_map.236 = (bf16[256,1408]{1,0:T(8,128)(2,1)S(1)}, bf16[256,1408]{1,0:T(8,128)(2,1)S(1)}, bf16[256,1408]{1,0:T(8,128)(2,1)S(1)}, f32[8,128]{1,0:T(8,128)}) custom-call(s32[8]{0:T(128)S(1)} %stack.40.refs_0_.refs_1_, bf16[128,2048]{1,0:T(8,128)(2,1)S(1)} %collective-permute-done.14.refs_1_.refs_6_, ...), custom_call_target="tpu_custom_call" | custom-call | flops 20000000000 | bytes 120000000 | tf_op jit(solution)/shard_map/pallas_call | solution.py:94
  174.1 6.7 %shard_map.237 = (bf16[256,1408]{1,0:T(8,128)(2,1)S(1)}, bf16[256,1408]{1,0:T(8,128)(2,1)S(1)}, bf16[256,1408]{1,0:T(8,128)(2,1)S(1)}, f32[8,128]{1,0:T(8,128)}) custom-call(s32[8]{0:T(128)S(1)} %stack.40.refs_0_.refs_1_, bf16[128,2048]{1,0:T(8,128)(2,1)S(1)} %collective-permute-done.16.refs_1_.refs_8_, ...), custom_call_target="tpu_custom_call" | custom-call | flops 20000000000 | bytes 120000000 | tf_op jit(solution)/shard_map/pallas_call | solution.py:94
  180.9 3.0 shard_map.238
  186.8 3.8 shard_map.239
  193.5 4.0 collective-permute-start.22
  197.5 15.9 %shard_map.241 = (bf16[1024,2048]{1,0:T(8,128)(2,1)S(1)}, f32[8,128]{1,0:T(8,128)}) custom-call(s32[8]{0:T(128)S(1)} %stack.40.refs_0_.refs_1_, bf16[256,1408]{1,0:T(8,128)(2,1)S(1)} %get-tuple-element.363.refs_1_.refs_10_, bf16[256,1408]{1,0:T(8,128)(2,1)S(1)} %get-tuple-element.364.refs_2_.refs_11_, ...), custom_call_target="tpu_custom_call" | custom-call | flops 20000000000 | bytes 120000000 | tf_op jit(solution)/shard_map/pallas_call | solution.py:94
  218.0 6.7 %shard_map.243 = (bf16[1024,1408]{1,0:T(8,128)(2,1)}, f32[8,128]{1,0:T(8,128)}) custom-call(s32[1]{0:T(128)} %bitcast.15.refs_0_, s32[8]{0:T(128)S(1)} %stack.40.refs_0_.refs_1_, bf16[128,2048]{1,0:T(8,128)(2,1)S(1)} %copy-done.81, bf16[128,2048]{1,0:T(8,128)(2,1)S(1)} %copy-done.85, bf16[128,2048]{1,0:T(8,128)(2,1)} %collective-permute-done.12.refs_1_.refs_4_, ...), custom_call_target="tpu_custom_call" | custom-call | flops 20000000000 | bytes 120000000 | tf_op jit(solution)/shard_map/pallas_call | solution.py:94
  229.0 3.3 shard_map.245
  236.9 4.4 collective-permute-start.23
  241.4 7.0 %shard_map.247 = (bf16[256,1408]{1,0:T(8,128)(2,1)S(1)}, bf16[256,1408]{1,0:T(8,128)(2,1)S(1)}, bf16[256,1408]{1,0:T(8,128)(2,1)S(1)}, bf16[256,1408]{1,0:T(8,128)(2,1)S(1)}, f32[8,128]{1,0:T(8,128)}) custom-call(s32[1]{0:T(128)} %bitcast.14.refs_0_, s32[8]{0:T(128)S(1)} %stack.40.refs_0_.refs_1_, bf16[128,2048]{1,0:T(8,128)(2,1)S(1)} %copy-done.82, ...), custom_call_target="tpu_custom_call" | custom-call | flops 20000000000 | bytes 120000000 | tf_op jit(solution)/shard_map/pallas_call | solution.py:94
  254.6 6.7 %shard_map.249 = (bf16[1024,1408]{1,0:T(8,128)(2,1)}, f32[8,128]{1,0:T(8,128)}) custom-call(s32[1]{0:T(128)} %bitcast.15.refs_0_, s32[8]{0:T(128)S(1)} %stack.40.refs_0_.refs_1_, bf16[128,2048]{1,0:T(8,128)(2,1)S(1)} %copy-done.82, bf16[128,2048]{1,0:T(8,128)(2,1)S(1)} %copy-done.86, bf16[128,2048]{1,0:T(8,128)(2,1)} %collective-permute-done.12.refs_1_.refs_4_, ...), custom_call_target="tpu_custom_call" | custom-call | flops 20000000000 | bytes 120000000 | tf_op jit(solution)/shard_map/pallas_call | solution.py:94
  270.1 6.8 %reduce-scatter.4.cloned.1.call-done.refs_3_ = bf16[256,2048]{1,0:T(8,128)(2,1)} async-done(((bf16[1024,2048]{1,0:T(8,128)(2,1)}), bf16[256,2048]{1,0:T(8,128)(2,1)}) %reduce-scatter.4.cloned.1.call-update) | async-done | bytes 1048592 | tf_op jit(solution)/shard_map/reduce_scatter | solution.py:188
  279.7 3.5 shard_map.251
  286.9 3.5 shard_map.252
  294.0 7.3 %shard_map.253 = (bf16[256,1408]{1,0:T(8,128)(2,1)S(1)}, bf16[256,1408]{1,0:T(8,128)(2,1)S(1)}, bf16[256,1408]{1,0:T(8,128)(2,1)S(1)}, bf16[256,1408]{1,0:T(8,128)(2,1)S(1)}, f32[8,128]{1,0:T(8,128)}) custom-call(s32[1]{0:T(128)} %bitcast.14.refs_0_, s32[8]{0:T(128)S(1)} %stack.40.refs_0_.refs_1_, bf16[128,2048]{1,0:T(8,128)(2,1)S(1)} %copy-done.83, ...), custom_call_target="tpu_custom_call" | custom-call | flops 20000000000 | bytes 120000000 | tf_op jit(solution)/shard_map/pallas_call | solution.py:94
  307.6 3.0 shard_map.254
  312.0 8.4 %shard_map.255 = (bf16[1024,2048]{1,0:T(8,128)(2,1)S(1)}, f32[8,128]{1,0:T(8,128)}) custom-call(s32[8]{0:T(128)S(1)} %stack.40.refs_0_.refs_1_, bf16[256,1408]{1,0:T(8,128)(2,1)S(1)} %copy-done.123, bf16[256,1408]{1,0:T(8,128)(2,1)S(1)} %copy-done.126, bf16[256,1408]{1,0:T(8,128)(2,1)S(1)} %copy-done.129, bf16[256,1408]{1,0:T(8,128)(2,1)S(1)} %copy-done.138, ...), custom_call_target="tpu_custom_call" | custom-call | flops 20000000000 | bytes 120000000 | tf_op jit(solution)/shard_map/pallas_call | solution.py:94
  330.1 3.4 shard_map.256
  338.3 3.4 collective-permute-done.33.refs_2_.refs_7_
  342.5 3.8 shard_map.258
  348.3 4.2 collective-permute-start.43
  359.3 14.2 %shard_map.260 = (bf16[1024,1024]{1,0:T(8,128)(2,1)S(1)}, f32[8,128]{1,0:T(8,128)}) custom-call(s32[8]{0:T(128)S(1)} %stack.40.refs_0_.refs_1_, bf16[128,512]{1,0:T(8,128)(2,1)S(1)} %copy-done.206, bf16[128,512]{1,0:T(8,128)(2,1)S(1)} %copy-done.209, bf16[128,512]{1,0:T(8,128)(2,1)S(1)} %copy-done.212, bf16[128,512]{1,0:T(8,128)(2,1)S(1)} %copy-done.215, ...), custom_call_target="tpu_custom_call" | custom-call | flops 20000000000 | bytes 120000000 | tf_op jit(solution)/shard_map/pallas_call | solution.py:94
  373.6 3.8 shard_map.261
  378.8 7.1 %shard_map.262 = (bf16[768,1408]{1,0:T(8,128)(2,1)}, f32[8,128]{1,0:T(8,128)}) custom-call(s32[1]{0:T(128)} %bitcast.15.refs_0_, s32[8]{0:T(128)S(1)} %stack.40.refs_0_.refs_1_, bf16[1024,2048]{1,0:T(8,128)(2,1)S(1)} %copy-done.7, bf16[128,2048]{1,0:T(8,128)(2,1)} %get-tuple-element.310.refs_1_.refs_3_.refs_2_, ...), custom_call_target="tpu_custom_call" | custom-call | flops 20000000000 | bytes 120000000 | tf_op jit(solution)/shard_map/pallas_call | solution.py:94
  386.1 6.1 %shard_map.263 = (bf16[1024,2048]{1,0:T(8,128)(2,1)S(1)}, f32[8,128]{1,0:T(8,128)}) custom-call(s32[8]{0:T(128)S(1)} %stack.40.refs_0_.refs_1_, bf16[1024,1024]{1,0:T(8,128)(2,1)S(1)} %get-tuple-element.441.refs_19_.refs_1_.refs_10_, bf16[2048,512]{1,0:T(8,128)(2,1)S(1)} %copy-done.17, bf16[2048,256]{1,0:T(8,128)(2,1)S(1)} %copy-done.25, ...), custom_call_target="tpu_custom_call" | custom-call | flops 20000000000 | bytes 120000000 | tf_op jit(solution)/shard_map/pallas_call | solution.py:94
  404.8 6.3 %shard_map.265 = (bf16[256,1408]{1,0:T(8,128)(2,1)S(1)}, bf16[256,1408]{1,0:T(8,128)(2,1)S(1)}, bf16[256,1408]{1,0:T(8,128)(2,1)S(1)}, f32[8,128]{1,0:T(8,128)}) custom-call(s32[1]{0:T(128)} %bitcast.14.refs_0_, s32[8]{0:T(128)S(1)} %stack.40.refs_0_.refs_1_, bf16[1024,2048]{1,0:T(8,128)(2,1)S(1)} %copy-done.8, ...), custom_call_target="tpu_custom_call" | custom-call | flops 20000000000 | bytes 120000000 | tf_op jit(solution)/shard_map/pallas_call | solution.py:94
  416.9 3.2 shard_map.267
  423.7 3.6 collective-permute-done.53.refs_2_.refs_7_
  433.4 4.5 collective-permute-start.59
  437.9 4.4 shard_map.271
  443.2 3.6 shard_map.272
  446.8 4.7 collective-permute-start.67
  458.9 3.2 shard_map.275
  471.5 17.5 %collective-permute-done.57.refs_2_.refs_6_ = bf16[256,1408]{1,0:T(8,128)(2,1)S(1)} collective-permute-done((bf16[256,1408]{1,0:T(8,128)(2,1)S(1)}, bf16[256,1408]{1,0:T(8,128)(2,1)S(1)}, u32[]{:S(2)}, u32[]{:S(2)}) %collective-permute-start.57) | collective-permute-done | bytes 720928 | tf_op jit(solution)/shard_map/ppermute | solution.py:836
  509.5 7.6 %collective-permute-start.77 = (bf16[1024,128]{1,0:T(8,128)(2,1)}, bf16[1024,128]{1,0:T(8,128)(2,1)}, u32[]{:S(2)}, u32[]{:S(2)}) collective-permute-start(bf16[1024,128]{1,0:T(8,128)(2,1)} %get-tuple-element.530.refs_1_), channel_id=1, source_target_pairs={{0,8},{4,12},{24,16},{28,20},{1,9},{5,13},{25,17},{29,21},{2,10},{... | collective-permute-start | bytes 786440 | tf_op jit(solution)/shard_map/ppermute | solution.py:836
  528.7 8.5 %collective-permute-done.65.refs_6_ = bf16[256,1408]{1,0:T(8,128)(2,1)S(1)} collective-permute-done((bf16[256,1408]{1,0:T(8,128)(2,1)S(1)}, bf16[256,1408]{1,0:T(8,128)(2,1)S(1)}, u32[]{:S(2)}, u32[]{:S(2)}) %collective-permute-start.65) | collective-permute-done | bytes 720928 | tf_op jit(solution)/shard_map/ppermute | solution.py:836
  548.5 4.1 collective-permute-done.79.refs_6_
  561.5 6.5 %collective-permute-done.73.refs_4_ = bf16[256,1408]{1,0:T(8,128)(2,1)S(1)} collective-permute-done((bf16[256,1408]{1,0:T(8,128)(2,1)S(1)}, bf16[256,1408]{1,0:T(8,128)(2,1)S(1)}, u32[]{:S(2)}, u32[]{:S(2)}) %collective-permute-start.73) | collective-permute-done | bytes 720928 | tf_op jit(solution)/shard_map/ppermute | solution.py:836
  (755 shorter events, 278.1 us)
Async XLA Ops:
  7.2 126.7 %all-gather.3.cloned.1.call-start = ((), (), s32[]{:S(2)}) async-start(), calls=%async_computation.3 | async-start | bytes 5242880 | tf_op jit(solution)/shard_map/all_gather | solution.py:182
  29.2 22.9 %collective-permute-start.2 = (bf16[128,2048]{1,0:T(8,128)(2,1)}, bf16[128,2048]{1,0:T(8,128)(2,1)}, u32[]{:S(2)}, u32[]{:S(2)}) collective-permute-start(bf16[128,2048]{1,0:T(8,128)(2,1)} %collective-permute-done.refs_1_.refs_5_.refs_4_), channel_id=1, source_target_pairs={{0,2},{1,3},{2,0},{3,1},{4,6},{5,7},{6,4},{7,5},{8,10},{9,11},{10,... | collective-permute-start | bytes 1572872 | tf_op jit(solution)/shard_map/ppermute | solution.py:117
  30.5 21.7 %collective-permute-start.3 = (bf16[128,2048]{1,0:T(8,128)(2,1)}, bf16[128,2048]{1,0:T(8,128)(2,1)}, u32[]{:S(2)}, u32[]{:S(2)}) collective-permute-start(bf16[128,2048]{1,0:T(8,128)(2,1)} %collective-permute-done.1.refs_2_.refs_6_.refs_5_), channel_id=1, source_target_pairs={{0,1},{1,0},{2,3},{3,2},{4,5},{5,4},{6,7},{7,6},{8,9},{9,8},{10,11... | collective-permute-start | bytes 1572872 | tf_op jit(solution)/shard_map/ppermute | solution.py:117
  47.4 229.5 %reduce-scatter.4.cloned.1.call-start = ((), (), s32[]{:S(2)}) async-start(), calls=%async_computation.4 | async-start | bytes 5242880 | tf_op jit(solution)/shard_map/reduce_scatter | solution.py:188
  76.4 29.1 %collective-permute-start.11 = (bf16[128,2048]{1,0:T(8,128)(2,1)S(1)}, bf16[128,2048]{1,0:T(8,128)(2,1)S(1)}, u32[]{:S(2)}, u32[]{:S(2)}) collective-permute-start(bf16[128,2048]{1,0:T(8,128)(2,1)S(1)} %get-tuple-element.344), channel_id=1, source_target_pairs={{0,2},{1,3},{2,0},{3,1},{4,6},{5,7},{6,4},{7,5},{8,10},{9,11},{10,... | collective-permute-start | bytes 1572872 | tf_op jit(solution)/shard_map/ppermute | solution.py:117
  77.5 27.9 %collective-permute-start.8 = (bf16[128,2048]{1,0:T(8,128)(2,1)S(1)}, bf16[128,2048]{1,0:T(8,128)(2,1)S(1)}, u32[]{:S(2)}, u32[]{:S(2)}) collective-permute-start(bf16[128,2048]{1,0:T(8,128)(2,1)S(1)} %get-tuple-element.341), channel_id=1, source_target_pairs={{0,1},{1,0},{2,3},{3,2},{4,5},{5,4},{6,7},{7,6},{8,9},{9,8},{10,11... | collective-permute-start | bytes 1572872 | tf_op jit(solution)/shard_map/ppermute | solution.py:117
  83.5 44.4 %collective-permute-start.10 = (bf16[128,2048]{1,0:T(8,128)(2,1)S(1)}, bf16[128,2048]{1,0:T(8,128)(2,1)S(1)}, u32[]{:S(2)}, u32[]{:S(2)}) collective-permute-start(bf16[128,2048]{1,0:T(8,128)(2,1)S(1)} %get-tuple-element.343), channel_id=1, source_target_pairs={{0,2},{1,3},{2,0},{3,1},{4,6},{5,7},{6,4},{7,5},{8,10},{9,11},{10,... | collective-permute-start | bytes 1572872 | tf_op jit(solution)/shard_map/ppermute | solution.py:117
  83.9 44.0 %collective-permute-start.9 = (bf16[128,2048]{1,0:T(8,128)(2,1)S(1)}, bf16[128,2048]{1,0:T(8,128)(2,1)S(1)}, u32[]{:S(2)}, u32[]{:S(2)}) collective-permute-start(bf16[128,2048]{1,0:T(8,128)(2,1)S(1)} %get-tuple-element.342), channel_id=1, source_target_pairs={{0,1},{1,0},{2,3},{3,2},{4,5},{5,4},{6,7},{7,6},{8,9},{9,8},{10,11... | collective-permute-start | bytes 1572872 | tf_op jit(solution)/shard_map/ppermute | solution.py:117
  131.0 27.1 %collective-permute-start.13 = (bf16[128,2048]{1,0:T(8,128)(2,1)S(1)}, bf16[128,2048]{1,0:T(8,128)(2,1)S(1)}, u32[]{:S(2)}, u32[]{:S(2)}) collective-permute-start(bf16[128,2048]{1,0:T(8,128)(2,1)S(1)} %get-tuple-element.348.refs_2_.refs_3_), channel_id=1, source_target_pairs={{0,2},{1,3},{2,0},{3,1},{4,6},{5,7},{6,4},{7,5},{8,10},{9,11},{10,... | collective-permute-start | bytes 1572872 | tf_op jit(solution)/shard_map/ppermute | solution.py:117
  131.0 35.8 %collective-permute-start.14 = (bf16[128,2048]{1,0:T(8,128)(2,1)S(1)}, bf16[128,2048]{1,0:T(8,128)(2,1)S(1)}, u32[]{:S(2)}, u32[]{:S(2)}) collective-permute-start(bf16[128,2048]{1,0:T(8,128)(2,1)S(1)} %get-tuple-element.348.refs_2_.refs_3_), channel_id=1, source_target_pairs={{0,1},{1,0},{2,3},{3,2},{4,5},{5,4},{6,7},{7,6},{8,9},{9,8},{10,11... | collective-permute-start | bytes 1572872 | tf_op jit(solution)/shard_map/ppermute | solution.py:117
  132.4 25.6 %collective-permute-start.12 = (bf16[128,2048]{1,0:T(8,128)(2,1)S(1)}, bf16[128,2048]{1,0:T(8,128)(2,1)}, u32[]{:S(2)}, u32[]{:S(2)}) collective-permute-start(bf16[128,2048]{1,0:T(8,128)(2,1)S(1)} %get-tuple-element.347.refs_1_.refs_2_), channel_id=1, source_target_pairs={{0,1},{1,0},{2,3},{3,2},{4,5},{5,4},{6,7},{7,6},{8,9},{9,8},{10,11... | collective-permute-start | bytes 1572872 | tf_op jit(solution)/shard_map/ppermute | solution.py:117
  132.4 34.4 %collective-permute-start.15 = (bf16[128,2048]{1,0:T(8,128)(2,1)S(1)}, bf16[128,2048]{1,0:T(8,128)(2,1)}, u32[]{:S(2)}, u32[]{:S(2)}) collective-permute-start(bf16[128,2048]{1,0:T(8,128)(2,1)S(1)} %get-tuple-element.347.refs_1_.refs_2_), channel_id=1, source_target_pairs={{0,2},{1,3},{2,0},{3,1},{4,6},{5,7},{6,4},{7,5},{8,10},{9,11},{10,... | collective-permute-start | bytes 1572872 | tf_op jit(solution)/shard_map/ppermute | solution.py:117
  190.7 36.6 %collective-permute-start.21 = (bf16[512,1408]{1,0:T(8,128)(2,1)}, bf16[512,1408]{1,0:T(8,128)(2,1)S(1)}, u32[]{:S(2)}, u32[]{:S(2)}) collective-permute-start(bf16[512,1408]{1,0:T(8,128)(2,1)} %get-tuple-element.380), channel_id=1, source_target_pairs={{0,4},{4,0},{8,12},{12,8},{16,20},{20,16},{24,28},{28,24},{1,5},{5... | collective-permute-start | bytes 4325384 | tf_op jit(solution)/shard_map/ppermute | solution.py:117
  193.5 32.1 %collective-permute-start.22 = (bf16[256,1408]{1,0:T(8,128)(2,1)}, bf16[256,1408]{1,0:T(8,128)(2,1)}, u32[]{:S(2)}, u32[]{:S(2)}) collective-permute-start(bf16[256,1408]{1,0:T(8,128)(2,1)} %get-tuple-element.381.refs_1_), channel_id=1, source_target_pairs={{0,8},{4,12},{24,16},{28,20},{1,9},{5,13},{25,17},{29,21},{2,10},{... | collective-permute-start | bytes 2162696 | tf_op jit(solution)/shard_map/ppermute | solution.py:836
  225.5 128.5 %all-gather.5.cloned.1.call-start = ((), (), s32[]{:S(2)}) async-start(), calls=%async_computation.6 | async-start | bytes 5242880 | tf_op jit(solution)/shard_map/all_gather | solution.py:182
  236.0 26.2 %collective-permute-start.24 = (bf16[256,1408]{1,0:T(8,128)(2,1)S(1)}, bf16[256,1408]{1,0:T(8,128)(2,1)S(1)}, u32[]{:S(2)}, u32[]{:S(2)}) collective-permute-start(bf16[256,1408]{1,0:T(8,128)(2,1)S(1)} %get-tuple-element.388.refs_3_), channel_id=1, source_target_pairs={{8,16},{12,20},{16,8},{20,12},{9,17},{13,21},{17,9},{21,13},{10,18... | collective-permute-start | bytes 2162696 | tf_op jit(solution)/shard_map/ppermute | solution.py:836
  236.9 28.0 %collective-permute-start.23 = (bf16[256,1408]{1,0:T(8,128)(2,1)S(1)}, bf16[256,1408]{1,0:T(8,128)(2,1)S(1)}, u32[]{:S(2)}, u32[]{:S(2)}) collective-permute-start(bf16[256,1408]{1,0:T(8,128)(2,1)S(1)} %get-tuple-element.387.refs_1_), channel_id=1, source_target_pairs={{0,8},{4,12},{24,16},{28,20},{1,9},{5,13},{25,17},{29,21},{2,10},{... | collective-permute-start | bytes 2162696 | tf_op jit(solution)/shard_map/ppermute | solution.py:836
  250.7 33.9 %collective-permute-start.30 = (bf16[256,1408]{1,0:T(8,128)(2,1)}, bf16[256,1408]{1,0:T(8,128)(2,1)}, u32[]{:S(2)}, u32[]{:S(2)}) collective-permute-start(bf16[256,1408]{1,0:T(8,128)(2,1)} %get-tuple-element.399.refs_6_), channel_id=1, source_target_pairs={{0,8},{4,12},{8,0},{12,4},{16,24},{20,28},{24,16},{28,20},{1,9},{5... | collective-permute-start | bytes 2162696 | tf_op jit(solution)/shard_map/ppermute | solution.py:836
  253.1 31.5 %collective-permute-start.31 = (bf16[256,1408]{1,0:T(8,128)(2,1)}, bf16[256,1408]{1,0:T(8,128)(2,1)}, u32[]{:S(2)}, u32[]{:S(2)}) collective-permute-start(bf16[256,1408]{1,0:T(8,128)(2,1)} %get-tuple-element.400.refs_3_), channel_id=1, source_target_pairs={{8,16},{12,20},{16,8},{20,12},{9,17},{13,21},{17,9},{21,13},{10,18... | collective-permute-start | bytes 2162696 | tf_op jit(solution)/shard_map/ppermute | solution.py:836
  261.3 31.0 %collective-permute-start.29 = (bf16[1024,1408]{1,0:T(8,128)(2,1)}, bf16[1024,1408]{1,0:T(8,128)(2,1)}, u32[]{:S(2)}, u32[]{:S(2)}) collective-permute-start(bf16[1024,1408]{1,0:T(8,128)(2,1)} %get-tuple-element.398), channel_id=1, source_target_pairs={{0,4},{4,0},{8,12},{12,8},{16,20},{20,16},{24,28},{28,24},{1,5},{5... | collective-permute-start | bytes 8650760 | tf_op jit(solution)/shard_map/ppermute | solution.py:117
  266.2 38.5 %collective-permute-start.27 = (bf16[256,1408]{1,0:T(8,128)(2,1)}, bf16[256,1408]{1,0:T(8,128)(2,1)S(1)}, u32[]{:S(2)}, u32[]{:S(2)}) collective-permute-start(bf16[256,1408]{1,0:T(8,128)(2,1)} %get-tuple-element.395.refs_6_), channel_id=1, source_target_pairs={{0,8},{4,12},{8,0},{12,4},{16,24},{20,28},{24,16},{28,20},{1,9},{5... | collective-permute-start | bytes 2162696 | tf_op jit(solution)/shard_map/ppermute | solution.py:836
  268.5 37.1 %collective-permute-start.28 = (bf16[256,1408]{1,0:T(8,128)(2,1)}, bf16[256,1408]{1,0:T(8,128)(2,1)}, u32[]{:S(2)}, u32[]{:S(2)}) collective-permute-start(bf16[256,1408]{1,0:T(8,128)(2,1)} %get-tuple-element.396.refs_3_), channel_id=1, source_target_pairs={{8,16},{12,20},{16,8},{20,12},{9,17},{13,21},{17,9},{21,13},{10,18... | collective-permute-start | bytes 2162696 | tf_op jit(solution)/shard_map/ppermute | solution.py:836
  284.5 211.4 %reduce-scatter.6.cloned.1.call-start = ((), (), s32[]{:S(2)}) async-start(), calls=%async_computation.5 | async-start | bytes 5242880 | tf_op jit(solution)/shard_map/reduce_scatter | solution.py:188
  291.1 35.9 %collective-permute-start.35 = (bf16[256,1408]{1,0:T(8,128)(2,1)}, bf16[256,1408]{1,0:T(8,128)(2,1)}, u32[]{:S(2)}, u32[]{:S(2)}) collective-permute-start(bf16[256,1408]{1,0:T(8,128)(2,1)} %get-tuple-element.430.refs_6_), channel_id=1, source_target_pairs={{0,8},{4,12},{8,0},{12,4},{16,24},{20,28},{24,16},{28,20},{1,9},{5... | collective-permute-start | bytes 2162696 | tf_op jit(solution)/shard_map/ppermute | solution.py:836
  292.3 34.7 %collective-permute-start.36 = (bf16[256,1408]{1,0:T(8,128)(2,1)}, bf16[256,1408]{1,0:T(8,128)(2,1)}, u32[]{:S(2)}, u32[]{:S(2)}) collective-permute-start(bf16[256,1408]{1,0:T(8,128)(2,1)} %get-tuple-element.431.refs_3_), channel_id=1, source_target_pairs={{8,16},{12,20},{16,8},{20,12},{9,17},{13,21},{17,9},{21,13},{10,18... | collective-permute-start | bytes 2162696 | tf_op jit(solution)/shard_map/ppermute | solution.py:836
  327.0 173.4 %reduce-scatter.8.cloned.1.call-start = ((), (), s32[]{:S(2)}) async-start(), calls=%async_computation.7 | async-start | bytes 5242880 | tf_op jit(solution)/shard_map/reduce_scatter | solution.py:188
  334.4 39.0 %collective-permute-start.39 = (bf16[256,1408]{1,0:T(8,128)(2,1)}, bf16[256,1408]{1,0:T(8,128)(2,1)}, u32[]{:S(2)}, u32[]{:S(2)}) collective-permute-start(bf16[256,1408]{1,0:T(8,128)(2,1)} %get-tuple-element.442.refs_6_), channel_id=1, source_target_pairs={{0,8},{4,12},{8,0},{12,4},{16,24},{20,28},{24,16},{28,20},{1,9},{5... | collective-permute-start | bytes 2162696 | tf_op jit(solution)/shard_map/ppermute | solution.py:836
  334.9 38.6 %collective-permute-start.40 = (bf16[256,1408]{1,0:T(8,128)(2,1)}, bf16[256,1408]{1,0:T(8,128)(2,1)}, u32[]{:S(2)}, u32[]{:S(2)}) collective-permute-start(bf16[256,1408]{1,0:T(8,128)(2,1)} %get-tuple-element.443.refs_3_), channel_id=1, source_target_pairs={{8,16},{12,20},{16,8},{20,12},{9,17},{13,21},{17,9},{21,13},{10,18... | collective-permute-start | bytes 2162696 | tf_op jit(solution)/shard_map/ppermute | solution.py:836
  346.3 27.2 %collective-permute-start.41 = (bf16[256,1408]{1,0:T(8,128)(2,1)}, bf16[256,1408]{1,0:T(8,128)(2,1)}, u32[]{:S(2)}, u32[]{:S(2)}) collective-permute-start(bf16[256,1408]{1,0:T(8,128)(2,1)} %get-tuple-element.446.refs_1_), channel_id=1, source_target_pairs={{0,4},{4,0},{8,12},{12,8},{16,20},{20,16},{24,28},{28,24},{1,5},{5... | collective-permute-start | bytes 2162696 | tf_op jit(solution)/shard_map/ppermute | solution.py:117
  348.3 46.7 %collective-permute-start.43 = (bf16[256,1408]{1,0:T(8,128)(2,1)}, bf16[256,1408]{1,0:T(8,128)(2,1)}, u32[]{:S(2)}, u32[]{:S(2)}) collective-permute-start(bf16[256,1408]{1,0:T(8,128)(2,1)} %get-tuple-element.449.refs_6_), channel_id=1, source_target_pairs={{0,8},{4,12},{8,0},{12,4},{16,24},{20,28},{24,16},{28,20},{1,9},{5... | collective-permute-start | bytes 2162696 | tf_op jit(solution)/shard_map/ppermute | solution.py:836
  352.4 43.2 %collective-permute-start.44 = (bf16[256,1408]{1,0:T(8,128)(2,1)}, bf16[256,1408]{1,0:T(8,128)(2,1)}, u32[]{:S(2)}, u32[]{:S(2)}) collective-permute-start(bf16[256,1408]{1,0:T(8,128)(2,1)} %get-tuple-element.450.refs_3_), channel_id=1, source_target_pairs={{8,16},{12,20},{16,8},{20,12},{9,17},{13,21},{17,9},{21,13},{10,18... | collective-permute-start | bytes 2162696 | tf_op jit(solution)/shard_map/ppermute | solution.py:836
  401.2 26.1 %collective-permute-start.53 = (bf16[256,1408]{1,0:T(8,128)(2,1)S(1)}, bf16[256,1408]{1,0:T(8,128)(2,1)S(1)}, u32[]{:S(2)}, u32[]{:S(2)}) collective-permute-start(bf16[256,1408]{1,0:T(8,128)(2,1)S(1)} %get-tuple-element.468.refs_6_), channel_id=1, source_target_pairs={{0,8},{4,12},{8,0},{12,4},{16,24},{20,28},{24,16},{28,20},{1,9},{5... | collective-permute-start | bytes 2162696 | tf_op jit(solution)/shard_map/ppermute | solution.py:836
  404.0 24.1 %collective-permute-start.54 = (bf16[256,1408]{1,0:T(8,128)(2,1)S(1)}, bf16[256,1408]{1,0:T(8,128)(2,1)S(1)}, u32[]{:S(2)}, u32[]{:S(2)}) collective-permute-start(bf16[256,1408]{1,0:T(8,128)(2,1)S(1)} %get-tuple-element.469.refs_3_), channel_id=1, source_target_pairs={{8,16},{12,20},{16,8},{20,12},{9,17},{13,21},{17,9},{21,13},{10,18... | collective-permute-start | bytes 2162696 | tf_op jit(solution)/shard_map/ppermute | solution.py:836
  428.2 23.4 %collective-permute-start.50 = (bf16[256,1408]{1,0:T(8,128)(2,1)S(1)}, bf16[256,1408]{1,0:T(8,128)(2,1)S(1)}, u32[]{:S(2)}, u32[]{:S(2)}) collective-permute-start(bf16[256,1408]{1,0:T(8,128)(2,1)S(1)} %get-tuple-element.463.refs_3_), channel_id=1, source_target_pairs={{8,16},{12,20},{16,8},{20,12},{9,17},{13,21},{17,9},{21,13},{10,18... | collective-permute-start | bytes 2162696 | tf_op jit(solution)/shard_map/ppermute | solution.py:836
  430.2 23.4 %collective-permute-start.56 = (bf16[256,1408]{1,0:T(8,128)(2,1)S(1)}, bf16[256,1408]{1,0:T(8,128)(2,1)S(1)}, u32[]{:S(2)}, u32[]{:S(2)}) collective-permute-start(bf16[256,1408]{1,0:T(8,128)(2,1)S(1)} %get-tuple-element.478.refs_1_), channel_id=1, source_target_pairs={{0,4},{4,0},{8,12},{12,8},{16,20},{20,16},{24,28},{28,24},{1,5},{5... | collective-permute-start | bytes 2162696 | tf_op jit(solution)/shard_map/ppermute | solution.py:117
  433.4 28.7 %collective-permute-start.59 = (bf16[256,1408]{1,0:T(8,128)(2,1)S(1)}, bf16[256,1408]{1,0:T(8,128)(2,1)S(1)}, u32[]{:S(2)}, u32[]{:S(2)}) collective-permute-start(bf16[256,1408]{1,0:T(8,128)(2,1)S(1)} %get-tuple-element.481.refs_5_), channel_id=1, source_target_pairs={{0,8},{4,12},{8,0},{12,4},{16,24},{20,28},{24,16},{28,20},{1,9},{5... | collective-permute-start | bytes 2162696 | tf_op jit(solution)/shard_map/ppermute | solution.py:836
  446.8 62.7 %collective-permute-start.67 = (bf16[128,1408]{1,0:T(8,128)(2,1)}, bf16[128,1408]{1,0:T(8,128)(2,1)}, u32[]{:S(2)}, u32[]{:S(2)}) collective-permute-start(bf16[128,1408]{1,0:T(8,128)(2,1)} %get-tuple-element.504.refs_1_), channel_id=1, source_target_pairs={{0,8},{4,12},{24,16},{28,20},{1,9},{5,13},{25,17},{29,21},{2,10},{... | collective-permute-start | bytes 1081352 | tf_op jit(solution)/shard_map/ppermute | solution.py:836
  451.5 75.2 %collective-permute-start.63 = (bf16[128,1408]{1,0:T(8,128)(2,1)}, bf16[128,1408]{1,0:T(8,128)(2,1)}, u32[]{:S(2)}, u32[]{:S(2)}) collective-permute-start(bf16[128,1408]{1,0:T(8,128)(2,1)} %get-tuple-element.499.refs_1_), channel_id=1, source_target_pairs={{0,8},{4,12},{24,16},{28,20},{1,9},{5,13},{25,17},{29,21},{2,10},{... | collective-permute-start | bytes 1081352 | tf_op jit(solution)/shard_map/ppermute | solution.py:836
  462.1 26.9 %collective-permute-start.57 = (bf16[256,1408]{1,0:T(8,128)(2,1)S(1)}, bf16[256,1408]{1,0:T(8,128)(2,1)S(1)}, u32[]{:S(2)}, u32[]{:S(2)}) collective-permute-start(bf16[256,1408]{1,0:T(8,128)(2,1)S(1)} %get-tuple-element.479.refs_5_), channel_id=1, source_target_pairs={{0,8},{4,12},{8,0},{12,4},{16,24},{20,28},{24,16},{28,20},{1,9},{5... | collective-permute-start | bytes 2162696 | tf_op jit(solution)/shard_map/ppermute | solution.py:836
  462.1 28.5 %collective-permute-start.58 = (bf16[256,1408]{1,0:T(8,128)(2,1)S(1)}, bf16[256,1408]{1,0:T(8,128)(2,1)S(1)}, u32[]{:S(2)}, u32[]{:S(2)}) collective-permute-start(bf16[256,1408]{1,0:T(8,128)(2,1)S(1)} %get-tuple-element.480.refs_3_), channel_id=1, source_target_pairs={{8,16},{12,20},{16,8},{20,12},{9,17},{13,21},{17,9},{21,13},{10,18... | collective-permute-start | bytes 2162696 | tf_op jit(solution)/shard_map/ppermute | solution.py:836
  465.2 26.7 %collective-permute-start.62 = (bf16[256,1408]{1,0:T(8,128)(2,1)S(1)}, bf16[256,1408]{1,0:T(8,128)(2,1)S(1)}, u32[]{:S(2)}, u32[]{:S(2)}) collective-permute-start(bf16[256,1408]{1,0:T(8,128)(2,1)S(1)} %get-tuple-element.492.refs_1_), channel_id=1, source_target_pairs={{0,4},{4,0},{8,12},{12,8},{16,20},{20,16},{24,28},{28,24},{1,5},{5... | collective-permute-start | bytes 2162696 | tf_op jit(solution)/shard_map/ppermute | solution.py:117
  489.0 28.1 %collective-permute-start.68 = (bf16[256,1408]{1,0:T(8,128)(2,1)}, bf16[256,1408]{1,0:T(8,128)(2,1)}, u32[]{:S(2)}, u32[]{:S(2)}) collective-permute-start(bf16[256,1408]{1,0:T(8,128)(2,1)} %get-tuple-element.505.refs_3_), channel_id=1, source_target_pairs={{8,16},{12,20},{16,8},{20,12},{9,17},{13,21},{17,9},{21,13},{10,18... | collective-permute-start | bytes 2162696 | tf_op jit(solution)/shard_map/ppermute | solution.py:836
  490.6 27.2 %collective-permute-start.69 = (bf16[256,1408]{1,0:T(8,128)(2,1)}, bf16[256,1408]{1,0:T(8,128)(2,1)}, u32[]{:S(2)}, u32[]{:S(2)}) collective-permute-start(bf16[256,1408]{1,0:T(8,128)(2,1)} %get-tuple-element.506.refs_5_), channel_id=1, source_target_pairs={{8,0},{12,4},{16,24},{20,28},{9,1},{13,5},{17,25},{21,29},{10,2},{... | collective-permute-start | bytes 2162696 | tf_op jit(solution)/shard_map/ppermute | solution.py:836
  494.0 25.1 %collective-permute-start.70 = (bf16[256,1408]{1,0:T(8,128)(2,1)S(1)}, bf16[256,1408]{1,0:T(8,128)(2,1)S(1)}, u32[]{:S(2)}, u32[]{:S(2)}) collective-permute-start(bf16[256,1408]{1,0:T(8,128)(2,1)S(1)} %get-tuple-element.512.refs_1_), channel_id=1, source_target_pairs={{0,4},{4,0},{8,12},{12,8},{16,20},{20,16},{24,28},{28,24},{1,5},{5... | collective-permute-start | bytes 2162696 | tf_op jit(solution)/shard_map/ppermute | solution.py:117
  509.5 37.0 %collective-permute-start.77 = (bf16[1024,128]{1,0:T(8,128)(2,1)}, bf16[1024,128]{1,0:T(8,128)(2,1)}, u32[]{:S(2)}, u32[]{:S(2)}) collective-permute-start(bf16[1024,128]{1,0:T(8,128)(2,1)} %get-tuple-element.530.refs_1_), channel_id=1, source_target_pairs={{0,8},{4,12},{24,16},{28,20},{1,9},{5,13},{25,17},{29,21},{2,10},{... | collective-permute-start | bytes 786440 | tf_op jit(solution)/shard_map/ppermute | solution.py:836
  526.7 25.9 %collective-permute-start.79 = (bf16[256,1408]{1,0:T(8,128)(2,1)S(1)}, bf16[256,1408]{1,0:T(8,128)(2,1)S(1)}, u32[]{:S(2)}, u32[]{:S(2)}) collective-permute-start(bf16[256,1408]{1,0:T(8,128)(2,1)S(1)} %get-tuple-element.532.refs_5_), channel_id=1, source_target_pairs={{8,0},{12,4},{16,24},{20,28},{9,1},{13,5},{17,25},{21,29},{10,2},{... | collective-permute-start | bytes 2162696 | tf_op jit(solution)/shard_map/ppermute | solution.py:836
  528.0 19.8 %collective-permute-start.78 = (bf16[128,1408]{1,0:T(8,128)(2,1)S(1)}, bf16[128,1408]{1,0:T(8,128)(2,1)S(1)}, u32[]{:S(2)}, u32[]{:S(2)}) collective-permute-start(bf16[128,1408]{1,0:T(8,128)(2,1)S(1)} %get-tuple-element.531.refs_3_), channel_id=1, source_target_pairs={{8,16},{12,20},{16,8},{20,12},{9,17},{13,21},{17,9},{21,13},{10,18... | collective-permute-start | bytes 1081352 | tf_op jit(solution)/shard_map/ppermute | solution.py:836
  546.5 21.5 %collective-permute-start.73 = (bf16[256,1408]{1,0:T(8,128)(2,1)S(1)}, bf16[256,1408]{1,0:T(8,128)(2,1)S(1)}, u32[]{:S(2)}, u32[]{:S(2)}) collective-permute-start(bf16[256,1408]{1,0:T(8,128)(2,1)S(1)} %get-tuple-element.521.refs_3_), channel_id=1, source_target_pairs={{8,0},{12,4},{16,24},{20,28},{9,1},{13,5},{17,25},{21,29},{10,2},{... | collective-permute-start | bytes 2162696 | tf_op jit(solution)/shard_map/ppermute | solution.py:836
  (303 other events, 2627.5 us)
Sparse Core Ops, SparseCore 0:
  47.5 81.0 all-gather.2
  225.6 51.2 reduce-scatter.3
  284.6 52.6 all-gather.4
  341.0 52.6 reduce-scatter.5
  397.1 52.6 reduce-scatter.7

commit v4 on v3

--- a/solution.py
+++ b/solution.py
@@ -899,7 +899,8 @@
             if back:
                 self.ends[b] = self.hop(self.whole[b], [(1, 0), (2, 3)])
             if on:
-                self.fold[ahead] = self.hop(self.part[ahead], [(0, 1), (3, 2)])
+                part = self.order.tie(self.part[ahead])
+                self.fold[ahead] = self.hop(part, [(0, 1), (3, 2)])
         if out:
             self.done[c] = swap(self.final[c], "dp", self.size, 1)
 

time: 613 us -> 598 us (0.976)
  waiting for transfers between devices: 110 us -> 88.2 us
  starting transfers between devices: 125 us -> 133 us
    ppermute x43, waiting for transfers between devices: 49 us -> 27.1 us  [hop(): return lax.ppermute(value, 'dp', pairs)]
    ppermute x43, starting transfers between devices: 76.5 us -> 85.5 us  [hop(): return lax.ppermute(value, 'dp', pairs)]
    unnamed x510 -> x514, local copies, waits for them, and re-layouts: 89 us -> 90.4 us
  transfers between devices with their start and end apart: 96 -> 96, of which waited for: 20 -> 19; matrix products, arithmetic and copies ran while one was open for 0% -> 1% of each run, Pallas kernels for 40% -> 41%
where the time goes in v4:
time: 598 us; the launch traced here: 587 us
  Pallas kernels  255 us (43%)
  starting transfers between devices  133 us (22%)
  local copies, waits for them, and re-layouts  91.2 us (15%)
  waiting for transfers between devices  88.2 us (15%)
  between operations  18.1 us (3%)
    pallas_call x85, Pallas kernels, call(): pl.pallas_call(kernel, out_shape=(*outs, pltpu.HBM((8, 128), F32)), grid_...  255 us
    unnamed x514, local copies, waits for them, and re-layouts  90.4 us
    ppermute x43, starting transfers between devices, hop(): return lax.ppermute(value, 'dp', pairs)  85.5 us
    ppermute x48, waiting for transfers between devices, swap(): return lax.ppermute(value, axis, [(i, i ^ bit) for i in range(size)])  54.2 us
    ppermute x48, starting transfers between devices, swap(): return lax.ppermute(value, axis, [(i, i ^ bit) for i in range(size)])  47.1 us
    ppermute x43, waiting for transfers between devices, hop(): return lax.ppermute(value, 'dp', pairs)  27.1 us
  transfers between devices with their start and end apart: 96, of which 19 were waited for; matrix products, arithmetic and copies ran while one was open for 1% of the time, Pallas kernels for 41%

profile of v4, /device:TPU:1, one launch (start us, length us, event | category | flops | bytes accessed | tf_op | source)
XLA Modules:
  0.0 587.3 jit_solution(11129341729953219310)
XLA Ops:
  47.4 4.8 collective-permute-done.2.refs_1_.refs_9_.refs_8_
  59.7 3.4 shard_map.225
  63.2 3.7 shard_map.226
  73.0 3.3 shard_map.228
  79.2 4.0 collective-permute-done.7.refs_1_
  87.7 17.8 %collective-permute-done.11.refs_8_ = bf16[128,2048]{1,0:T(8,128)(2,1)S(1)} collective-permute-done((bf16[128,2048]{1,0:T(8,128)(2,1)S(1)}, bf16[128,2048]{1,0:T(8,128)(2,1)S(1)}, u32[]{:S(2)}, u32[]{:S(2)}) %collective-permute-start.11) | collective-permute-done | bytes 524320 | tf_op jit(solution)/shard_map/ppermute | solution.py:117
  105.5 22.5 %collective-permute-done.10.refs_7_ = bf16[128,2048]{1,0:T(8,128)(2,1)S(1)} collective-permute-done((bf16[128,2048]{1,0:T(8,128)(2,1)S(1)}, bf16[128,2048]{1,0:T(8,128)(2,1)S(1)}, u32[]{:S(2)}, u32[]{:S(2)}) %collective-permute-start.10) | collective-permute-done | bytes 524320 | tf_op jit(solution)/shard_map/ppermute | solution.py:117
  138.8 7.4 %shard_map.233 = (bf16[1024,1408]{1,0:T(8,128)(2,1)S(1)}, f32[8,128]{1,0:T(8,128)}) custom-call(bf16[1024,2048]{1,0:T(8,128)(2,1)S(1)} %copy-done.9, bf16[1408,2048]{1,0:T(8,128)(2,1)S(1)} %copy-done.5, f32[8,128]{1,0:T(8,128)} %get-tuple-element.354.refs_2_), custom_call_target="tpu_custom_call" | custom-call | flops 20000000000 | bytes 120000000 | tf_op jit(solution)/shard_map/pallas_call | solution.py:94
  151.5 6.6 %shard_map.234 = (bf16[256,1408]{1,0:T(8,128)(2,1)S(1)}, bf16[256,1408]{1,0:T(8,128)(2,1)S(1)}, bf16[256,1408]{1,0:T(8,128)(2,1)S(1)}, f32[8,128]{1,0:T(8,128)}) custom-call(s32[8]{0:T(128)S(1)} %stack.40.refs_0_.refs_1_, bf16[128,2048]{1,0:T(8,128)(2,1)S(1)} %get-tuple-element.350.refs_1_.refs_2_, bf16[128,2048]{1,0:T(8,128)(2,1)S(1)} %get-tuple-element.351.refs_2_.refs_3_, ...), custom_call_target="tpu_custom_call" | custom-call | flops 20000000000 | bytes 120000000 | tf_op jit(solution)/shard_map/pallas_call | solution.py:94
  159.6 7.1 %shard_map.235 = (bf16[256,1408]{1,0:T(8,128)(2,1)S(1)}, bf16[256,1408]{1,0:T(8,128)(2,1)S(1)}, bf16[256,1408]{1,0:T(8,128)(2,1)S(1)}, f32[8,128]{1,0:T(8,128)}) custom-call(s32[8]{0:T(128)S(1)} %stack.40.refs_0_.refs_1_, bf16[128,2048]{1,0:T(8,128)(2,1)} %collective-permute-done.12.refs_1_.refs_4_, ...), custom_call_target="tpu_custom_call" | custom-call | flops 20000000000 | bytes 120000000 | tf_op jit(solution)/shard_map/pallas_call | solution.py:94
  166.8 7.2 %shard_map.236 = (bf16[256,1408]{1,0:T(8,128)(2,1)S(1)}, bf16[256,1408]{1,0:T(8,128)(2,1)S(1)}, bf16[256,1408]{1,0:T(8,128)(2,1)S(1)}, f32[8,128]{1,0:T(8,128)}) custom-call(s32[8]{0:T(128)S(1)} %stack.40.refs_0_.refs_1_, bf16[128,2048]{1,0:T(8,128)(2,1)S(1)} %collective-permute-done.14.refs_1_.refs_6_, ...), custom_call_target="tpu_custom_call" | custom-call | flops 20000000000 | bytes 120000000 | tf_op jit(solution)/shard_map/pallas_call | solution.py:94
  174.1 6.7 %shard_map.237 = (bf16[256,1408]{1,0:T(8,128)(2,1)S(1)}, bf16[256,1408]{1,0:T(8,128)(2,1)S(1)}, bf16[256,1408]{1,0:T(8,128)(2,1)S(1)}, f32[8,128]{1,0:T(8,128)}) custom-call(s32[8]{0:T(128)S(1)} %stack.40.refs_0_.refs_1_, bf16[128,2048]{1,0:T(8,128)(2,1)S(1)} %collective-permute-done.16.refs_1_.refs_8_, ...), custom_call_target="tpu_custom_call" | custom-call | flops 20000000000 | bytes 120000000 | tf_op jit(solution)/shard_map/pallas_call | solution.py:94
  180.9 3.0 shard_map.238
  186.8 3.8 shard_map.239
  193.5 4.0 collective-permute-start.22
  197.5 15.9 %shard_map.241 = (bf16[1024,2048]{1,0:T(8,128)(2,1)S(1)}, f32[8,128]{1,0:T(8,128)}) custom-call(s32[8]{0:T(128)S(1)} %stack.40.refs_0_.refs_1_, bf16[256,1408]{1,0:T(8,128)(2,1)S(1)} %get-tuple-element.366.refs_1_.refs_10_, bf16[256,1408]{1,0:T(8,128)(2,1)S(1)} %get-tuple-element.367.refs_2_.refs_11_, ...), custom_call_target="tpu_custom_call" | custom-call | flops 20000000000 | bytes 120000000 | tf_op jit(solution)/shard_map/pallas_call | solution.py:94
  218.0 6.7 %shard_map.243 = (bf16[1024,1408]{1,0:T(8,128)(2,1)}, f32[8,128]{1,0:T(8,128)}) custom-call(s32[1]{0:T(128)} %bitcast.15.refs_0_, s32[8]{0:T(128)S(1)} %stack.40.refs_0_.refs_1_, bf16[128,2048]{1,0:T(8,128)(2,1)S(1)} %copy-done.81, bf16[128,2048]{1,0:T(8,128)(2,1)S(1)} %copy-done.85, bf16[128,2048]{1,0:T(8,128)(2,1)} %collective-permute-done.12.refs_1_.refs_4_, ...), custom_call_target="tpu_custom_call" | custom-call | flops 20000000000 | bytes 120000000 | tf_op jit(solution)/shard_map/pallas_call | solution.py:94
  229.0 3.3 shard_map.245
  236.9 4.4 collective-permute-start.23
  241.4 7.1 %shard_map.247 = (bf16[256,1408]{1,0:T(8,128)(2,1)S(1)}, bf16[256,1408]{1,0:T(8,128)(2,1)S(1)}, bf16[256,1408]{1,0:T(8,128)(2,1)S(1)}, bf16[256,1408]{1,0:T(8,128)(2,1)S(1)}, f32[8,128]{1,0:T(8,128)}) custom-call(s32[1]{0:T(128)} %bitcast.14.refs_0_, s32[8]{0:T(128)S(1)} %stack.40.refs_0_.refs_1_, bf16[128,2048]{1,0:T(8,128)(2,1)S(1)} %copy-done.82, ...), custom_call_target="tpu_custom_call" | custom-call | flops 20000000000 | bytes 120000000 | tf_op jit(solution)/shard_map/pallas_call | solution.py:94
  254.6 6.7 %shard_map.249 = (bf16[1024,1408]{1,0:T(8,128)(2,1)}, f32[8,128]{1,0:T(8,128)}) custom-call(s32[1]{0:T(128)} %bitcast.15.refs_0_, s32[8]{0:T(128)S(1)} %stack.40.refs_0_.refs_1_, bf16[128,2048]{1,0:T(8,128)(2,1)S(1)} %copy-done.82, bf16[128,2048]{1,0:T(8,128)(2,1)S(1)} %copy-done.86, bf16[128,2048]{1,0:T(8,128)(2,1)} %collective-permute-done.12.refs_1_.refs_4_, ...), custom_call_target="tpu_custom_call" | custom-call | flops 20000000000 | bytes 120000000 | tf_op jit(solution)/shard_map/pallas_call | solution.py:94
  270.1 6.8 %reduce-scatter.4.cloned.1.call-done.refs_3_ = bf16[256,2048]{1,0:T(8,128)(2,1)} async-done(((bf16[1024,2048]{1,0:T(8,128)(2,1)}), bf16[256,2048]{1,0:T(8,128)(2,1)}) %reduce-scatter.4.cloned.1.call-update) | async-done | bytes 1048592 | tf_op jit(solution)/shard_map/reduce_scatter | solution.py:188
  279.7 3.5 shard_map.251
  286.9 3.5 shard_map.252
  293.9 7.3 %shard_map.253 = (bf16[256,1408]{1,0:T(8,128)(2,1)S(1)}, bf16[256,1408]{1,0:T(8,128)(2,1)S(1)}, bf16[256,1408]{1,0:T(8,128)(2,1)S(1)}, bf16[256,1408]{1,0:T(8,128)(2,1)S(1)}, f32[8,128]{1,0:T(8,128)}) custom-call(s32[1]{0:T(128)} %bitcast.14.refs_0_, s32[8]{0:T(128)S(1)} %stack.40.refs_0_.refs_1_, bf16[128,2048]{1,0:T(8,128)(2,1)S(1)} %copy-done.83, ...), custom_call_target="tpu_custom_call" | custom-call | flops 20000000000 | bytes 120000000 | tf_op jit(solution)/shard_map/pallas_call | solution.py:94
  307.6 3.0 shard_map.254
  312.0 8.4 %shard_map.255 = (bf16[1024,2048]{1,0:T(8,128)(2,1)S(1)}, f32[8,128]{1,0:T(8,128)}) custom-call(s32[8]{0:T(128)S(1)} %stack.40.refs_0_.refs_1_, bf16[256,1408]{1,0:T(8,128)(2,1)S(1)} %copy-done.125, bf16[256,1408]{1,0:T(8,128)(2,1)S(1)} %copy-done.128, bf16[256,1408]{1,0:T(8,128)(2,1)S(1)} %copy-done.131, bf16[256,1408]{1,0:T(8,128)(2,1)S(1)} %copy-done.140, ...), custom_call_target="tpu_custom_call" | custom-call | flops 20000000000 | bytes 120000000 | tf_op jit(solution)/shard_map/pallas_call | solution.py:94
  330.1 3.4 shard_map.256
  338.2 3.4 collective-permute-done.33.refs_2_.refs_7_
  342.5 3.7 shard_map.258
  348.2 4.2 collective-permute-start.43
  359.2 14.2 %shard_map.260 = (bf16[1024,1024]{1,0:T(8,128)(2,1)S(1)}, f32[8,128]{1,0:T(8,128)}) custom-call(s32[8]{0:T(128)S(1)} %stack.40.refs_0_.refs_1_, bf16[128,512]{1,0:T(8,128)(2,1)S(1)} %copy-done.208, bf16[128,512]{1,0:T(8,128)(2,1)S(1)} %copy-done.211, bf16[128,512]{1,0:T(8,128)(2,1)S(1)} %copy-done.214, bf16[128,512]{1,0:T(8,128)(2,1)S(1)} %copy-done.217, ...), custom_call_target="tpu_custom_call" | custom-call | flops 20000000000 | bytes 120000000 | tf_op jit(solution)/shard_map/pallas_call | solution.py:94
  373.5 3.8 shard_map.261
  378.7 7.1 %shard_map.262 = (bf16[768,1408]{1,0:T(8,128)(2,1)}, f32[8,128]{1,0:T(8,128)}) custom-call(s32[1]{0:T(128)} %bitcast.15.refs_0_, s32[8]{0:T(128)S(1)} %stack.40.refs_0_.refs_1_, bf16[1024,2048]{1,0:T(8,128)(2,1)S(1)} %copy-done.7, bf16[128,2048]{1,0:T(8,128)(2,1)} %get-tuple-element.313.refs_1_.refs_3_.refs_2_, ...), custom_call_target="tpu_custom_call" | custom-call | flops 20000000000 | bytes 120000000 | tf_op jit(solution)/shard_map/pallas_call | solution.py:94
  386.0 6.1 %shard_map.263 = (bf16[1024,2048]{1,0:T(8,128)(2,1)S(1)}, f32[8,128]{1,0:T(8,128)}) custom-call(s32[8]{0:T(128)S(1)} %stack.40.refs_0_.refs_1_, bf16[1024,1024]{1,0:T(8,128)(2,1)S(1)} %get-tuple-element.444.refs_19_.refs_1_.refs_10_, bf16[2048,512]{1,0:T(8,128)(2,1)S(1)} %copy-done.17, bf16[2048,256]{1,0:T(8,128)(2,1)S(1)} %copy-done.25, ...), custom_call_target="tpu_custom_call" | custom-call | flops 20000000000 | bytes 120000000 | tf_op jit(solution)/shard_map/pallas_call | solution.py:94
  404.7 6.3 %shard_map.265 = (bf16[256,1408]{1,0:T(8,128)(2,1)S(1)}, bf16[256,1408]{1,0:T(8,128)(2,1)S(1)}, bf16[256,1408]{1,0:T(8,128)(2,1)S(1)}, f32[8,128]{1,0:T(8,128)}) custom-call(s32[1]{0:T(128)} %bitcast.14.refs_0_, s32[8]{0:T(128)S(1)} %stack.40.refs_0_.refs_1_, bf16[1024,2048]{1,0:T(8,128)(2,1)S(1)} %copy-done.8, ...), custom_call_target="tpu_custom_call" | custom-call | flops 20000000000 | bytes 120000000 | tf_op jit(solution)/shard_map/pallas_call | solution.py:94
  416.9 3.2 shard_map.267
  423.6 3.6 collective-permute-done.53.refs_2_.refs_7_
  433.4 4.4 collective-permute-start.59
  437.8 4.4 shard_map.271
  449.1 4.9 collective-permute-start.57
  456.7 3.2 shard_map.275
  462.2 3.0 collective-permute-start.62
  465.2 7.9 %collective-permute-start.67 = (bf16[128,1408]{1,0:T(8,128)(2,1)}, bf16[128,1408]{1,0:T(8,128)(2,1)}, u32[]{:S(2)}, u32[]{:S(2)}) collective-permute-start(bf16[128,1408]{1,0:T(8,128)(2,1)} %get-tuple-element.509.refs_1_), channel_id=1, source_target_pairs={{0,8},{4,12},{24,16},{28,20},{1,9},{5,13},{25,17},{29,21},{2,10},{... | collective-permute-start | bytes 1081352 | tf_op jit(solution)/shard_map/ppermute | solution.py:836
  483.0 6.1 %collective-permute-start.63 = (bf16[128,1408]{1,0:T(8,128)(2,1)}, bf16[128,1408]{1,0:T(8,128)(2,1)}, u32[]{:S(2)}, u32[]{:S(2)}) collective-permute-start(bf16[128,1408]{1,0:T(8,128)(2,1)} %get-tuple-element.503.refs_1_), channel_id=1, source_target_pairs={{0,8},{4,12},{24,16},{28,20},{1,9},{5,13},{25,17},{29,21},{2,10},{... | collective-permute-start | bytes 1081352 | tf_op jit(solution)/shard_map/ppermute | solution.py:836
  508.0 4.0 collective-permute-start.77
  533.7 4.5 collective-permute-done.79.refs_6_
  546.0 7.6 %collective-permute-done.73.refs_4_ = bf16[256,1408]{1,0:T(8,128)(2,1)S(1)} collective-permute-done((bf16[256,1408]{1,0:T(8,128)(2,1)S(1)}, bf16[256,1408]{1,0:T(8,128)(2,1)S(1)}, u32[]{:S(2)}, u32[]{:S(2)}) %collective-permute-start.73) | collective-permute-done | bytes 720928 | tf_op jit(solution)/shard_map/ppermute | solution.py:836
  (759 shorter events, 278.4 us)
Async XLA Ops:
  7.2 126.7 %all-gather.3.cloned.1.call-start = ((), (), s32[]{:S(2)}) async-start(), calls=%async_computation.3 | async-start | bytes 5242880 | tf_op jit(solution)/shard_map/all_gather | solution.py:182
  29.2 23.0 %collective-permute-start.2 = (bf16[128,2048]{1,0:T(8,128)(2,1)}, bf16[128,2048]{1,0:T(8,128)(2,1)}, u32[]{:S(2)}, u32[]{:S(2)}) collective-permute-start(bf16[128,2048]{1,0:T(8,128)(2,1)} %collective-permute-done.refs_1_.refs_5_.refs_4_), channel_id=1, source_target_pairs={{0,2},{1,3},{2,0},{3,1},{4,6},{5,7},{6,4},{7,5},{8,10},{9,11},{10,... | collective-permute-start | bytes 1572872 | tf_op jit(solution)/shard_map/ppermute | solution.py:117
  30.5 21.7 %collective-permute-start.3 = (bf16[128,2048]{1,0:T(8,128)(2,1)}, bf16[128,2048]{1,0:T(8,128)(2,1)}, u32[]{:S(2)}, u32[]{:S(2)}) collective-permute-start(bf16[128,2048]{1,0:T(8,128)(2,1)} %collective-permute-done.1.refs_2_.refs_6_.refs_5_), channel_id=1, source_target_pairs={{0,1},{1,0},{2,3},{3,2},{4,5},{5,4},{6,7},{7,6},{8,9},{9,8},{10,11... | collective-permute-start | bytes 1572872 | tf_op jit(solution)/shard_map/ppermute | solution.py:117
  47.4 229.5 %reduce-scatter.4.cloned.1.call-start = ((), (), s32[]{:S(2)}) async-start(), calls=%async_computation.4 | async-start | bytes 5242880 | tf_op jit(solution)/shard_map/reduce_scatter | solution.py:188
  76.4 29.1 %collective-permute-start.11 = (bf16[128,2048]{1,0:T(8,128)(2,1)S(1)}, bf16[128,2048]{1,0:T(8,128)(2,1)S(1)}, u32[]{:S(2)}, u32[]{:S(2)}) collective-permute-start(bf16[128,2048]{1,0:T(8,128)(2,1)S(1)} %get-tuple-element.347), channel_id=1, source_target_pairs={{0,2},{1,3},{2,0},{3,1},{4,6},{5,7},{6,4},{7,5},{8,10},{9,11},{10,... | collective-permute-start | bytes 1572872 | tf_op jit(solution)/shard_map/ppermute | solution.py:117
  77.5 28.0 %collective-permute-start.8 = (bf16[128,2048]{1,0:T(8,128)(2,1)S(1)}, bf16[128,2048]{1,0:T(8,128)(2,1)S(1)}, u32[]{:S(2)}, u32[]{:S(2)}) collective-permute-start(bf16[128,2048]{1,0:T(8,128)(2,1)S(1)} %get-tuple-element.344), channel_id=1, source_target_pairs={{0,1},{1,0},{2,3},{3,2},{4,5},{5,4},{6,7},{7,6},{8,9},{9,8},{10,11... | collective-permute-start | bytes 1572872 | tf_op jit(solution)/shard_map/ppermute | solution.py:117
  83.5 44.4 %collective-permute-start.10 = (bf16[128,2048]{1,0:T(8,128)(2,1)S(1)}, bf16[128,2048]{1,0:T(8,128)(2,1)S(1)}, u32[]{:S(2)}, u32[]{:S(2)}) collective-permute-start(bf16[128,2048]{1,0:T(8,128)(2,1)S(1)} %get-tuple-element.346), channel_id=1, source_target_pairs={{0,2},{1,3},{2,0},{3,1},{4,6},{5,7},{6,4},{7,5},{8,10},{9,11},{10,... | collective-permute-start | bytes 1572872 | tf_op jit(solution)/shard_map/ppermute | solution.py:117
  84.0 43.9 %collective-permute-start.9 = (bf16[128,2048]{1,0:T(8,128)(2,1)S(1)}, bf16[128,2048]{1,0:T(8,128)(2,1)S(1)}, u32[]{:S(2)}, u32[]{:S(2)}) collective-permute-start(bf16[128,2048]{1,0:T(8,128)(2,1)S(1)} %get-tuple-element.345), channel_id=1, source_target_pairs={{0,1},{1,0},{2,3},{3,2},{4,5},{5,4},{6,7},{7,6},{8,9},{9,8},{10,11... | collective-permute-start | bytes 1572872 | tf_op jit(solution)/shard_map/ppermute | solution.py:117
  131.0 27.1 %collective-permute-start.13 = (bf16[128,2048]{1,0:T(8,128)(2,1)S(1)}, bf16[128,2048]{1,0:T(8,128)(2,1)S(1)}, u32[]{:S(2)}, u32[]{:S(2)}) collective-permute-start(bf16[128,2048]{1,0:T(8,128)(2,1)S(1)} %get-tuple-element.351.refs_2_.refs_3_), channel_id=1, source_target_pairs={{0,2},{1,3},{2,0},{3,1},{4,6},{5,7},{6,4},{7,5},{8,10},{9,11},{10,... | collective-permute-start | bytes 1572872 | tf_op jit(solution)/shard_map/ppermute | solution.py:117
  131.0 35.8 %collective-permute-start.14 = (bf16[128,2048]{1,0:T(8,128)(2,1)S(1)}, bf16[128,2048]{1,0:T(8,128)(2,1)S(1)}, u32[]{:S(2)}, u32[]{:S(2)}) collective-permute-start(bf16[128,2048]{1,0:T(8,128)(2,1)S(1)} %get-tuple-element.351.refs_2_.refs_3_), channel_id=1, source_target_pairs={{0,1},{1,0},{2,3},{3,2},{4,5},{5,4},{6,7},{7,6},{8,9},{9,8},{10,11... | collective-permute-start | bytes 1572872 | tf_op jit(solution)/shard_map/ppermute | solution.py:117
  132.5 25.6 %collective-permute-start.12 = (bf16[128,2048]{1,0:T(8,128)(2,1)S(1)}, bf16[128,2048]{1,0:T(8,128)(2,1)}, u32[]{:S(2)}, u32[]{:S(2)}) collective-permute-start(bf16[128,2048]{1,0:T(8,128)(2,1)S(1)} %get-tuple-element.350.refs_1_.refs_2_), channel_id=1, source_target_pairs={{0,1},{1,0},{2,3},{3,2},{4,5},{5,4},{6,7},{7,6},{8,9},{9,8},{10,11... | collective-permute-start | bytes 1572872 | tf_op jit(solution)/shard_map/ppermute | solution.py:117
  132.5 34.4 %collective-permute-start.15 = (bf16[128,2048]{1,0:T(8,128)(2,1)S(1)}, bf16[128,2048]{1,0:T(8,128)(2,1)}, u32[]{:S(2)}, u32[]{:S(2)}) collective-permute-start(bf16[128,2048]{1,0:T(8,128)(2,1)S(1)} %get-tuple-element.350.refs_1_.refs_2_), channel_id=1, source_target_pairs={{0,2},{1,3},{2,0},{3,1},{4,6},{5,7},{6,4},{7,5},{8,10},{9,11},{10,... | collective-permute-start | bytes 1572872 | tf_op jit(solution)/shard_map/ppermute | solution.py:117
  190.7 36.5 %collective-permute-start.21 = (bf16[512,1408]{1,0:T(8,128)(2,1)}, bf16[512,1408]{1,0:T(8,128)(2,1)S(1)}, u32[]{:S(2)}, u32[]{:S(2)}) collective-permute-start(bf16[512,1408]{1,0:T(8,128)(2,1)} %get-tuple-element.383), channel_id=1, source_target_pairs={{0,4},{4,0},{8,12},{12,8},{16,20},{20,16},{24,28},{28,24},{1,5},{5... | collective-permute-start | bytes 4325384 | tf_op jit(solution)/shard_map/ppermute | solution.py:117
  193.5 32.0 %collective-permute-start.22 = (bf16[256,1408]{1,0:T(8,128)(2,1)}, bf16[256,1408]{1,0:T(8,128)(2,1)}, u32[]{:S(2)}, u32[]{:S(2)}) collective-permute-start(bf16[256,1408]{1,0:T(8,128)(2,1)} %get-tuple-element.384.refs_1_), channel_id=1, source_target_pairs={{0,8},{4,12},{24,16},{28,20},{1,9},{5,13},{25,17},{29,21},{2,10},{... | collective-permute-start | bytes 2162696 | tf_op jit(solution)/shard_map/ppermute | solution.py:836
  225.5 128.4 %all-gather.5.cloned.1.call-start = ((), (), s32[]{:S(2)}) async-start(), calls=%async_computation.6 | async-start | bytes 5242880 | tf_op jit(solution)/shard_map/all_gather | solution.py:182
  236.0 26.2 %collective-permute-start.24 = (bf16[256,1408]{1,0:T(8,128)(2,1)S(1)}, bf16[256,1408]{1,0:T(8,128)(2,1)S(1)}, u32[]{:S(2)}, u32[]{:S(2)}) collective-permute-start(bf16[256,1408]{1,0:T(8,128)(2,1)S(1)} %get-tuple-element.391.refs_3_), channel_id=1, source_target_pairs={{8,16},{12,20},{16,8},{20,12},{9,17},{13,21},{17,9},{21,13},{10,18... | collective-permute-start | bytes 2162696 | tf_op jit(solution)/shard_map/ppermute | solution.py:836
  236.9 28.0 %collective-permute-start.23 = (bf16[256,1408]{1,0:T(8,128)(2,1)S(1)}, bf16[256,1408]{1,0:T(8,128)(2,1)S(1)}, u32[]{:S(2)}, u32[]{:S(2)}) collective-permute-start(bf16[256,1408]{1,0:T(8,128)(2,1)S(1)} %get-tuple-element.390.refs_1_), channel_id=1, source_target_pairs={{0,8},{4,12},{24,16},{28,20},{1,9},{5,13},{25,17},{29,21},{2,10},{... | collective-permute-start | bytes 2162696 | tf_op jit(solution)/shard_map/ppermute | solution.py:836
  250.7 33.9 %collective-permute-start.30 = (bf16[256,1408]{1,0:T(8,128)(2,1)}, bf16[256,1408]{1,0:T(8,128)(2,1)}, u32[]{:S(2)}, u32[]{:S(2)}) collective-permute-start(bf16[256,1408]{1,0:T(8,128)(2,1)} %get-tuple-element.402.refs_6_), channel_id=1, source_target_pairs={{0,8},{4,12},{8,0},{12,4},{16,24},{20,28},{24,16},{28,20},{1,9},{5... | collective-permute-start | bytes 2162696 | tf_op jit(solution)/shard_map/ppermute | solution.py:836
  253.0 31.5 %collective-permute-start.31 = (bf16[256,1408]{1,0:T(8,128)(2,1)}, bf16[256,1408]{1,0:T(8,128)(2,1)}, u32[]{:S(2)}, u32[]{:S(2)}) collective-permute-start(bf16[256,1408]{1,0:T(8,128)(2,1)} %get-tuple-element.403.refs_3_), channel_id=1, source_target_pairs={{8,16},{12,20},{16,8},{20,12},{9,17},{13,21},{17,9},{21,13},{10,18... | collective-permute-start | bytes 2162696 | tf_op jit(solution)/shard_map/ppermute | solution.py:836
  261.3 31.0 %collective-permute-start.29 = (bf16[1024,1408]{1,0:T(8,128)(2,1)}, bf16[1024,1408]{1,0:T(8,128)(2,1)}, u32[]{:S(2)}, u32[]{:S(2)}) collective-permute-start(bf16[1024,1408]{1,0:T(8,128)(2,1)} %get-tuple-element.401), channel_id=1, source_target_pairs={{0,4},{4,0},{8,12},{12,8},{16,20},{20,16},{24,28},{28,24},{1,5},{5... | collective-permute-start | bytes 8650760 | tf_op jit(solution)/shard_map/ppermute | solution.py:117
  266.2 38.5 %collective-permute-start.27 = (bf16[256,1408]{1,0:T(8,128)(2,1)}, bf16[256,1408]{1,0:T(8,128)(2,1)S(1)}, u32[]{:S(2)}, u32[]{:S(2)}) collective-permute-start(bf16[256,1408]{1,0:T(8,128)(2,1)} %get-tuple-element.398.refs_6_), channel_id=1, source_target_pairs={{0,8},{4,12},{8,0},{12,4},{16,24},{20,28},{24,16},{28,20},{1,9},{5... | collective-permute-start | bytes 2162696 | tf_op jit(solution)/shard_map/ppermute | solution.py:836
  268.5 37.1 %collective-permute-start.28 = (bf16[256,1408]{1,0:T(8,128)(2,1)}, bf16[256,1408]{1,0:T(8,128)(2,1)}, u32[]{:S(2)}, u32[]{:S(2)}) collective-permute-start(bf16[256,1408]{1,0:T(8,128)(2,1)} %get-tuple-element.399.refs_3_), channel_id=1, source_target_pairs={{8,16},{12,20},{16,8},{20,12},{9,17},{13,21},{17,9},{21,13},{10,18... | collective-permute-start | bytes 2162696 | tf_op jit(solution)/shard_map/ppermute | solution.py:836
  284.5 204.6 %reduce-scatter.6.cloned.1.call-start = ((), (), s32[]{:S(2)}) async-start(), calls=%async_computation.5 | async-start | bytes 5242880 | tf_op jit(solution)/shard_map/reduce_scatter | solution.py:188
  291.0 36.0 %collective-permute-start.35 = (bf16[256,1408]{1,0:T(8,128)(2,1)}, bf16[256,1408]{1,0:T(8,128)(2,1)}, u32[]{:S(2)}, u32[]{:S(2)}) collective-permute-start(bf16[256,1408]{1,0:T(8,128)(2,1)} %get-tuple-element.433.refs_6_), channel_id=1, source_target_pairs={{0,8},{4,12},{8,0},{12,4},{16,24},{20,28},{24,16},{28,20},{1,9},{5... | collective-permute-start | bytes 2162696 | tf_op jit(solution)/shard_map/ppermute | solution.py:836
  292.2 34.8 %collective-permute-start.36 = (bf16[256,1408]{1,0:T(8,128)(2,1)}, bf16[256,1408]{1,0:T(8,128)(2,1)}, u32[]{:S(2)}, u32[]{:S(2)}) collective-permute-start(bf16[256,1408]{1,0:T(8,128)(2,1)} %get-tuple-element.434.refs_3_), channel_id=1, source_target_pairs={{8,16},{12,20},{16,8},{20,12},{9,17},{13,21},{17,9},{21,13},{10,18... | collective-permute-start | bytes 2162696 | tf_op jit(solution)/shard_map/ppermute | solution.py:836
  322.5 19.1 %collective-permute-start.33 = (bf16[256,1408]{1,0:T(8,128)(2,1)}, bf16[256,1408]{1,0:T(8,128)(2,1)}, u32[]{:S(2)}, u32[]{:S(2)}) collective-permute-start(bf16[256,1408]{1,0:T(8,128)(2,1)} %get-tuple-element.430.refs_6_), channel_id=1, source_target_pairs={{0,8},{4,12},{8,0},{12,4},{16,24},{20,28},{24,16},{28,20},{1,9},{5... | collective-permute-start | bytes 2162696 | tf_op jit(solution)/shard_map/ppermute | solution.py:836
  326.9 166.6 %reduce-scatter.8.cloned.1.call-start = ((), (), s32[]{:S(2)}) async-start(), calls=%async_computation.7 | async-start | bytes 5242880 | tf_op jit(solution)/shard_map/reduce_scatter | solution.py:188
  334.4 38.9 %collective-permute-start.39 = (bf16[256,1408]{1,0:T(8,128)(2,1)}, bf16[256,1408]{1,0:T(8,128)(2,1)}, u32[]{:S(2)}, u32[]{:S(2)}) collective-permute-start(bf16[256,1408]{1,0:T(8,128)(2,1)} %get-tuple-element.445.refs_6_), channel_id=1, source_target_pairs={{0,8},{4,12},{8,0},{12,4},{16,24},{20,28},{24,16},{28,20},{1,9},{5... | collective-permute-start | bytes 2162696 | tf_op jit(solution)/shard_map/ppermute | solution.py:836
  334.8 38.5 %collective-permute-start.40 = (bf16[256,1408]{1,0:T(8,128)(2,1)}, bf16[256,1408]{1,0:T(8,128)(2,1)}, u32[]{:S(2)}, u32[]{:S(2)}) collective-permute-start(bf16[256,1408]{1,0:T(8,128)(2,1)} %get-tuple-element.446.refs_3_), channel_id=1, source_target_pairs={{8,16},{12,20},{16,8},{20,12},{9,17},{13,21},{17,9},{21,13},{10,18... | collective-permute-start | bytes 2162696 | tf_op jit(solution)/shard_map/ppermute | solution.py:836
  346.2 27.2 %collective-permute-start.41 = (bf16[256,1408]{1,0:T(8,128)(2,1)}, bf16[256,1408]{1,0:T(8,128)(2,1)}, u32[]{:S(2)}, u32[]{:S(2)}) collective-permute-start(bf16[256,1408]{1,0:T(8,128)(2,1)} %get-tuple-element.449.refs_1_), channel_id=1, source_target_pairs={{0,4},{4,0},{8,12},{12,8},{16,20},{20,16},{24,28},{28,24},{1,5},{5... | collective-permute-start | bytes 2162696 | tf_op jit(solution)/shard_map/ppermute | solution.py:117
  348.2 46.8 %collective-permute-start.43 = (bf16[256,1408]{1,0:T(8,128)(2,1)}, bf16[256,1408]{1,0:T(8,128)(2,1)}, u32[]{:S(2)}, u32[]{:S(2)}) collective-permute-start(bf16[256,1408]{1,0:T(8,128)(2,1)} %get-tuple-element.452.refs_6_), channel_id=1, source_target_pairs={{0,8},{4,12},{8,0},{12,4},{16,24},{20,28},{24,16},{28,20},{1,9},{5... | collective-permute-start | bytes 2162696 | tf_op jit(solution)/shard_map/ppermute | solution.py:836
  352.3 43.4 %collective-permute-start.44 = (bf16[256,1408]{1,0:T(8,128)(2,1)}, bf16[256,1408]{1,0:T(8,128)(2,1)}, u32[]{:S(2)}, u32[]{:S(2)}) collective-permute-start(bf16[256,1408]{1,0:T(8,128)(2,1)} %get-tuple-element.453.refs_3_), channel_id=1, source_target_pairs={{8,16},{12,20},{16,8},{20,12},{9,17},{13,21},{17,9},{21,13},{10,18... | collective-permute-start | bytes 2162696 | tf_op jit(solution)/shard_map/ppermute | solution.py:836
  401.0 26.1 %collective-permute-start.53 = (bf16[256,1408]{1,0:T(8,128)(2,1)S(1)}, bf16[256,1408]{1,0:T(8,128)(2,1)S(1)}, u32[]{:S(2)}, u32[]{:S(2)}) collective-permute-start(bf16[256,1408]{1,0:T(8,128)(2,1)S(1)} %get-tuple-element.471.refs_6_), channel_id=1, source_target_pairs={{0,8},{4,12},{8,0},{12,4},{16,24},{20,28},{24,16},{28,20},{1,9},{5... | collective-permute-start | bytes 2162696 | tf_op jit(solution)/shard_map/ppermute | solution.py:836
  403.9 24.6 %collective-permute-start.54 = (bf16[256,1408]{1,0:T(8,128)(2,1)S(1)}, bf16[256,1408]{1,0:T(8,128)(2,1)S(1)}, u32[]{:S(2)}, u32[]{:S(2)}) collective-permute-start(bf16[256,1408]{1,0:T(8,128)(2,1)S(1)} %get-tuple-element.472.refs_3_), channel_id=1, source_target_pairs={{8,16},{12,20},{16,8},{20,12},{9,17},{13,21},{17,9},{21,13},{10,18... | collective-permute-start | bytes 2162696 | tf_op jit(solution)/shard_map/ppermute | solution.py:836
  423.0 19.2 %collective-permute-start.51 = (bf16[1024,128]{1,0:T(8,128)(2,1)S(1)}, bf16[1024,128]{1,0:T(8,128)(2,1)S(1)}, u32[]{:S(2)}, u32[]{:S(2)}) collective-permute-start(bf16[1024,128]{1,0:T(8,128)(2,1)S(1)} %get-tuple-element.469), channel_id=1, source_target_pairs={{0,4},{4,0},{8,12},{12,8},{16,20},{20,16},{24,28},{28,24},{1,5},{5... | collective-permute-start | bytes 786440 | tf_op jit(solution)/shard_map/ppermute | solution.py:117
  427.2 19.5 %collective-permute-start.49 = (bf16[256,1408]{1,0:T(8,128)(2,1)S(1)}, bf16[256,1408]{1,0:T(8,128)(2,1)S(1)}, u32[]{:S(2)}, u32[]{:S(2)}) collective-permute-start(bf16[256,1408]{1,0:T(8,128)(2,1)S(1)} %get-tuple-element.465.refs_6_), channel_id=1, source_target_pairs={{0,8},{4,12},{8,0},{12,4},{16,24},{20,28},{24,16},{28,20},{1,9},{5... | collective-permute-start | bytes 2162696 | tf_op jit(solution)/shard_map/ppermute | solution.py:836
  433.4 26.4 %collective-permute-start.59 = (bf16[256,1408]{1,0:T(8,128)(2,1)S(1)}, bf16[256,1408]{1,0:T(8,128)(2,1)S(1)}, u32[]{:S(2)}, u32[]{:S(2)}) collective-permute-start(bf16[256,1408]{1,0:T(8,128)(2,1)S(1)} %get-tuple-element.484.refs_5_), channel_id=1, source_target_pairs={{0,8},{4,12},{8,0},{12,4},{16,24},{20,28},{24,16},{28,20},{1,9},{5... | collective-permute-start | bytes 2162696 | tf_op jit(solution)/shard_map/ppermute | solution.py:836
  449.1 30.1 %collective-permute-start.57 = (bf16[256,1408]{1,0:T(8,128)(2,1)S(1)}, bf16[256,1408]{1,0:T(8,128)(2,1)S(1)}, u32[]{:S(2)}, u32[]{:S(2)}) collective-permute-start(bf16[256,1408]{1,0:T(8,128)(2,1)S(1)} %get-tuple-element.482.refs_5_), channel_id=1, source_target_pairs={{0,8},{4,12},{8,0},{12,4},{16,24},{20,28},{24,16},{28,20},{1,9},{5... | collective-permute-start | bytes 2162696 | tf_op jit(solution)/shard_map/ppermute | solution.py:836
  454.1 26.5 %collective-permute-start.58 = (bf16[256,1408]{1,0:T(8,128)(2,1)S(1)}, bf16[256,1408]{1,0:T(8,128)(2,1)S(1)}, u32[]{:S(2)}, u32[]{:S(2)}) collective-permute-start(bf16[256,1408]{1,0:T(8,128)(2,1)S(1)} %get-tuple-element.483.refs_3_), channel_id=1, source_target_pairs={{8,16},{12,20},{16,8},{20,12},{9,17},{13,21},{17,9},{21,13},{10,18... | collective-permute-start | bytes 2162696 | tf_op jit(solution)/shard_map/ppermute | solution.py:836
  465.2 37.5 %collective-permute-start.67 = (bf16[128,1408]{1,0:T(8,128)(2,1)}, bf16[128,1408]{1,0:T(8,128)(2,1)}, u32[]{:S(2)}, u32[]{:S(2)}) collective-permute-start(bf16[128,1408]{1,0:T(8,128)(2,1)} %get-tuple-element.509.refs_1_), channel_id=1, source_target_pairs={{0,8},{4,12},{24,16},{28,20},{1,9},{5,13},{25,17},{29,21},{2,10},{... | collective-permute-start | bytes 1081352 | tf_op jit(solution)/shard_map/ppermute | solution.py:836
  473.1 30.3 %collective-permute-start.68 = (bf16[256,1408]{1,0:T(8,128)(2,1)}, bf16[256,1408]{1,0:T(8,128)(2,1)}, u32[]{:S(2)}, u32[]{:S(2)}) collective-permute-start(bf16[256,1408]{1,0:T(8,128)(2,1)} %get-tuple-element.510.refs_3_), channel_id=1, source_target_pairs={{8,16},{12,20},{16,8},{20,12},{9,17},{13,21},{17,9},{21,13},{10,18... | collective-permute-start | bytes 2162696 | tf_op jit(solution)/shard_map/ppermute | solution.py:836
  479.3 25.4 %collective-permute-start.69 = (bf16[256,1408]{1,0:T(8,128)(2,1)}, bf16[256,1408]{1,0:T(8,128)(2,1)}, u32[]{:S(2)}, u32[]{:S(2)}) collective-permute-start(bf16[256,1408]{1,0:T(8,128)(2,1)} %get-tuple-element.511.refs_5_), channel_id=1, source_target_pairs={{8,0},{12,4},{16,24},{20,28},{9,1},{13,5},{17,25},{21,29},{10,2},{... | collective-permute-start | bytes 2162696 | tf_op jit(solution)/shard_map/ppermute | solution.py:836
  482.7 22.0 %collective-permute-start.70 = (bf16[256,1408]{1,0:T(8,128)(2,1)S(1)}, bf16[256,1408]{1,0:T(8,128)(2,1)S(1)}, u32[]{:S(2)}, u32[]{:S(2)}) collective-permute-start(bf16[256,1408]{1,0:T(8,128)(2,1)S(1)} %get-tuple-element.517.refs_1_), channel_id=1, source_target_pairs={{0,4},{4,0},{8,12},{12,8},{16,20},{20,16},{24,28},{28,24},{1,5},{5... | collective-permute-start | bytes 2162696 | tf_op jit(solution)/shard_map/ppermute | solution.py:117
  483.0 34.9 %collective-permute-start.63 = (bf16[128,1408]{1,0:T(8,128)(2,1)}, bf16[128,1408]{1,0:T(8,128)(2,1)}, u32[]{:S(2)}, u32[]{:S(2)}) collective-permute-start(bf16[128,1408]{1,0:T(8,128)(2,1)} %get-tuple-element.503.refs_1_), channel_id=1, source_target_pairs={{0,8},{4,12},{24,16},{28,20},{1,9},{5,13},{25,17},{29,21},{2,10},{... | collective-permute-start | bytes 1081352 | tf_op jit(solution)/shard_map/ppermute | solution.py:836
  503.4 19.3 %collective-permute-start.65 = (bf16[256,1408]{1,0:T(8,128)(2,1)S(1)}, bf16[256,1408]{1,0:T(8,128)(2,1)S(1)}, u32[]{:S(2)}, u32[]{:S(2)}) collective-permute-start(bf16[256,1408]{1,0:T(8,128)(2,1)S(1)} %copy-done.61), channel_id=1, source_target_pairs={{8,0},{12,4},{16,24},{20,28},{9,1},{13,5},{17,25},{21,29},{10,2},{... | collective-permute-start | bytes 2162696 | tf_op jit(solution)/shard_map/ppermute | solution.py:836
  508.0 23.7 %collective-permute-start.77 = (bf16[1024,128]{1,0:T(8,128)(2,1)S(1)}, bf16[1024,128]{1,0:T(8,128)(2,1)S(1)}, u32[]{:S(2)}, u32[]{:S(2)}) collective-permute-start(bf16[1024,128]{1,0:T(8,128)(2,1)S(1)} %copy-done.107), channel_id=1, source_target_pairs={{0,8},{4,12},{24,16},{28,20},{1,9},{5,13},{25,17},{29,21},{2,10},{... | collective-permute-start | bytes 786440 | tf_op jit(solution)/shard_map/ppermute | solution.py:836
  518.0 20.2 %collective-permute-start.79 = (bf16[256,1408]{1,0:T(8,128)(2,1)S(1)}, bf16[256,1408]{1,0:T(8,128)(2,1)S(1)}, u32[]{:S(2)}, u32[]{:S(2)}) collective-permute-start(bf16[256,1408]{1,0:T(8,128)(2,1)S(1)} %get-tuple-element.538.refs_5_), channel_id=1, source_target_pairs={{8,0},{12,4},{16,24},{20,28},{9,1},{13,5},{17,25},{21,29},{10,2},{... | collective-permute-start | bytes 2162696 | tf_op jit(solution)/shard_map/ppermute | solution.py:836
  531.7 21.9 %collective-permute-start.73 = (bf16[256,1408]{1,0:T(8,128)(2,1)S(1)}, bf16[256,1408]{1,0:T(8,128)(2,1)S(1)}, u32[]{:S(2)}, u32[]{:S(2)}) collective-permute-start(bf16[256,1408]{1,0:T(8,128)(2,1)S(1)} %get-tuple-element.526.refs_3_), channel_id=1, source_target_pairs={{8,0},{12,4},{16,24},{20,28},{9,1},{13,5},{17,25},{21,29},{10,2},{... | collective-permute-start | bytes 2162696 | tf_op jit(solution)/shard_map/ppermute | solution.py:836
  (305 other events, 2662.0 us)
Sparse Core Ops, SparseCore 0:
  47.5 80.9 all-gather.2
  225.6 51.2 reduce-scatter.3
  284.6 52.6 all-gather.4
  341.0 52.6 reduce-scatter.5
  397.1 52.6 reduce-scatter.7
